TPU v7x, 32 devices: a whole 2x2x4 slice. The times are simulated.
32 devices in a mesh: groups: 2 (over y), adapter: 16 (over z, x, core).
Axes of the slice: x: 2, y: 2, z: 4, core: 2. Of those that a mesh axis runs over, the one named last changes fastest.
Arguments:
- hidden: bfloat16 [4096, 8192], P(('groups', 'adapter')), parts along dimension 0, may hold values from -6 to 6
- queries: bfloat16 [4096, 4096], P(('groups', 'adapter')), parts along dimension 0, may hold values from -6 to 6
- base_key_value: bfloat16 [4096, 1024], P(('groups', 'adapter')), parts along dimension 0, may hold values from -6 to 6
- key_value_cache: bfloat16 [4096, 16, 1024], P(('groups', 'adapter')), parts along dimension 0, may hold values from -6 to 6
- lengths: int32 [4096], P(('groups', 'adapter')), parts along dimension 0, may hold values from 2 to 16, as said below
- request_adapter_index: int32 [4096, 1], P(('groups', 'adapter')), parts along dimension 0, may hold values from 0 to 15; in each aligned block of 128 rows (0 to 127, 128 to 255, ...) at most 16 rows name the same one
- adapter_position_map: int32 [32], P('groups'), parts along dimension 0, may hold values from 0 to 15, each once
- adapter_down_weight: bfloat16 [32, 64, 8192], P(('groups', 'adapter')), parts along dimension 0, may hold values from -0.0625 to 0.0625
- adapter_up_weight: bfloat16 [32, 64, 1024], P(('groups', 'adapter')), parts along dimension 0, may hold values from -0.75 to 0.75
Outputs:
- attention: bfloat16 [4096, 4096], P(('groups', 'adapter')), parts along dimension 0
- written_key_value: bfloat16 [4096, 1024], P(('groups', 'adapter')), parts along dimension 0
There are 2 independent parts, one for each index of `groups`. A program takes and returns all parts, laid end to end along the dimension named above; each array names one. Nothing has to cross between parts.
Inputs may be any that keep to these rules, and one draw needn't show every extreme that they name: `lengths`: some request has all 16 positions in use. `request_adapter_index`: the 128 requests of one device name one adapter at most 16 times; in some device one adapter is named exactly 16 times. `adapter_position_map`: A permutation of the adapters.
All inputs are finite; a program needn't handle non-finite values.
Results may differ from a plain program's by a relative error of at most 0.0073.
Values may be sent and summed in bfloat16 or wider, within the bound.
No kernel may reach another device: no remote copies, remote signals or barrier semaphores. Data moves between devices by JAX's collectives and lax.ppermute only.
A program may use at most 64 MiB of HBM per device.

v0:
```python
import jax
import jax.numpy as jnp
from jax import lax
from jax.sharding import PartitionSpec as P

QUERY_HEADS = 32
KEY_VALUE_HEADS = 4
HEAD_SIZE = 128
CONTEXT_LENGTH = 16


adapter_scale = 2.0
score_floor = -1e30


def slot_lookup(request_adapter, adapter_position_map):
    adapter_index = jnp.arange(adapter_position_map.shape[0], dtype=jnp.int32)
    matches = request_adapter[:, None] == adapter_index[None, :]
    return jnp.sum(jnp.where(matches, adapter_position_map[None, :], 0), axis=1)


def attend(queries, key_value_cache, written_key_value, lengths):
    row_total_count = queries.shape[0]
    query_group_size = QUERY_HEADS // KEY_VALUE_HEADS
    key_value_split = KEY_VALUE_HEADS * HEAD_SIZE
    query_head_rows = queries.reshape(row_total_count, KEY_VALUE_HEADS, query_group_size, HEAD_SIZE)
    cached_key_block = key_value_cache[:, :, :key_value_split].reshape(
        row_total_count, CONTEXT_LENGTH, KEY_VALUE_HEADS, HEAD_SIZE
    )
    cached_value_block = key_value_cache[:, :, key_value_split:].reshape(
        row_total_count, CONTEXT_LENGTH, KEY_VALUE_HEADS, HEAD_SIZE
    )
    newest_key = written_key_value[:, :key_value_split].reshape(
        row_total_count, KEY_VALUE_HEADS, HEAD_SIZE
    )
    newest_value = written_key_value[:, key_value_split:].reshape(
        row_total_count, KEY_VALUE_HEADS, HEAD_SIZE
    )
    score_scale = HEAD_SIZE ** (-0.5)
    cached = (
        jnp.einsum(
            "rhgd,rphd->rhgp", query_head_rows, cached_key_block, preferred_element_type=jnp.float32
        )
        * score_scale
    )
    in_range = jnp.arange(CONTEXT_LENGTH, dtype=jnp.int32)[None, :] < lengths[:, None]
    cached = jnp.where(in_range[:, None, None, :], cached, score_floor)
    self_score = (
        jnp.einsum("rhgd,rhd->rhg", query_head_rows, newest_key, preferred_element_type=jnp.float32)
        * score_scale
    )
    peak_score = jnp.maximum(jnp.max(cached, axis=-1), self_score)
    cached_exp = jnp.exp(cached - peak_score[..., None])
    self_exp = jnp.exp(self_score - peak_score)
    denominator = jnp.sum(cached_exp, axis=-1) + self_exp
    cached_weight = (cached_exp / denominator[..., None]).astype(jnp.bfloat16)
    self_weight = (self_exp / denominator).astype(jnp.bfloat16)
    mixed = jnp.einsum(
        "rhgp,rphd->rhgd", cached_weight, cached_value_block, preferred_element_type=jnp.float32
    )
    mixed = (
        mixed
        + self_weight.astype(jnp.float32)[..., None]
        * newest_value.astype(jnp.float32)[:, :, None, :]
    )
    return mixed.reshape(row_total_count, QUERY_HEADS * HEAD_SIZE).astype(jnp.bfloat16)


def on_device(
    hidden,
    queries,
    base_key_value,
    key_value_cache,
    lengths,
    request_adapter_index,
    adapter_position_map,
    adapter_down_weight,
    adapter_up_weight,
):
    devices = lax.axis_size("adapter")
    row_total_count = hidden.shape[0]
    capacity = max(2, 2 * row_total_count // devices)
    slot_index_list = slot_lookup(request_adapter_index[:, 0], adapter_position_map)
    same_slot = slot_index_list[:, None] == slot_index_list[None, :]
    row_order = jnp.arange(row_total_count, dtype=jnp.int32)
    before = row_order[None, :] < row_order[:, None]
    place_rank = jnp.sum(same_slot & before, axis=1)
    target = slot_index_list * capacity + place_rank
    placing = (target[None, :] == jnp.arange(devices * capacity, dtype=jnp.int32)[:, None]).astype(
        jnp.bfloat16
    )
    outgoing = jnp.dot(placing, hidden, preferred_element_type=jnp.float32).astype(jnp.bfloat16)
    outgoing = outgoing.reshape(devices, capacity, hidden.shape[1])
    incoming = lax.all_to_all(outgoing, "adapter", split_axis=0, concat_axis=0, tiled=True)
    item_count = incoming.shape[1]
    flattened_rows = incoming.reshape(-1, incoming.shape[2])
    reduced_output = lax.dot_general(
        flattened_rows,
        adapter_down_weight[0],
        (((1,), (1,)), ((), ())),
        preferred_element_type=jnp.float32,
    ).astype(jnp.bfloat16)
    expanded_output = (
        adapter_scale
        * jnp.dot(reduced_output, adapter_up_weight[0], preferred_element_type=jnp.float32)
    ).astype(jnp.bfloat16)
    returned = lax.all_to_all(
        expanded_output.reshape(devices, item_count, expanded_output.shape[1]),
        "adapter",
        split_axis=0,
        concat_axis=0,
        tiled=True,
    )
    returned = returned.reshape(devices * capacity, returned.shape[2])
    adapter_correction = lax.dot_general(
        placing, returned, (((0,), (0,)), ((), ())), preferred_element_type=jnp.float32
    )
    written_key_value = (base_key_value.astype(jnp.float32) + adapter_correction).astype(
        jnp.bfloat16
    )
    attention = attend(queries, key_value_cache, written_key_value, lengths)
    return (attention, written_key_value)


def solution(mesh):
    placed = (
        P(("groups", "adapter"), None),
        P(("groups", "adapter"), None),
        P(("groups", "adapter"), None),
        P(("groups", "adapter"), None, None),
        P(("groups", "adapter")),
        P(("groups", "adapter"), None),
        P("groups"),
        P(("groups", "adapter"), None, None),
        P(("groups", "adapter"), None, None),
    )
    return jax.shard_map(
        on_device,
        mesh=mesh,
        in_specs=placed,
        out_specs=(P(("groups", "adapter"), None), P(("groups", "adapter"), None)),
        check_vma=False,
    )
```

profile of v0, /device:TPU:0, one launch (start us, length us, event | category | flops | bytes accessed | tf_op | source)
XLA Modules:
  0.0 157.1 jit_solution(1748676476497454882)
XLA Ops:
  0.6 0.0 copy-start
  0.6 0.9 select_reduce_fusion
  1.6 0.2 convert_reduce_fusion
  1.7 0.5 copy-done
  2.3 1.2 convolution_convert_fusion
  3.5 0.0 copy-start.2
  3.5 0.0 copy-start.5
  3.5 99.7 %all_to_all.10 = bf16[16,16,8192]{2,1,0:T(8,128)(2,1)} all-to-all(bf16[16,16,8192]{2,1,0:T(8,128)(2,1)S(1)} %bitcast.47), channel_id=1, replica_groups=mesh['groups'=2,'adapter'=16] {'adapter'}, dimensions={0} | all-to-all | bytes 8388608 | tf_op jit(solution)/shard_map/all_to_all | solution.py:94
  103.2 0.0 copy-done.2
  103.2 0.0 copy-done.5
  103.2 4.9 %fusion.2 = bf16[256,1024]{1,0:T(8,128)(2,1)} fusion(bf16[256,8192]{1,0:T(8,128)(2,1)} %bitcast.46, bf16[1,64,8192]{2,1,0:T(8,128)(2,1)S(1)} %copy-done.2, bf16[1,64,1024]{2,1,0:T(8,128)(2,1)S(1)} %copy-done.5), kind=kOutput, calls=%fused_computation.8 | convolution fusion | flops 302530560 | bytes 5898240 | tf_op jit(solution)/shard_map/dot_general | solution.py:105
  108.1 5.3 %all-to-all-start.1 = ((bf16[16,16,1024]{2,1,0:T(8,128)(2,1)}), bf16[16,16,1024]{2,1,0:T(8,128)(2,1)}, u32[]{:S(2)}, u32[]{:S(2)}) async-start(bf16[16,16,1024]{2,1,0:T(8,128)(2,1)} %bitcast.6), calls=%async_computation.1 | async-start | bytes 1048576 | tf_op jit(solution)/shard_map/all_to_all | solution.py:107
  113.5 1.4 copy.39
  114.9 4.6 %fusion.20 = (bf16[128,16,512]{2,1,0:T(8,128)(2,1)}, bf16[128,16,512]{2,1,0:T(8,128)(2,1)}) fusion(bf16[128,16,1024]{2,1,0:T(8,128)(2,1)} %param.12), kind=kLoop, calls=%fused_computation.39 | loop fusion | bytes 8388608 | tf_op jit(solution)/shard_map/slice | solution.py:27
  119.5 4.5 %copy.37 = bf16[128,16,512]{0,2,1:T(8,128)(2,1)} copy(bf16[128,16,512]{2,1,0:T(8,128)(2,1)} %get-tuple-element.2) | data formatting | bytes 4194304
  124.0 0.0 copy-start.6
  124.1 4.6 %copy.27 = bf16[128,16,4,128]{3,1,2,0:T(8,128)(2,1)} copy(bf16[128,16,4,128]{0,3,2,1:T(8,128)(2,1)} %bitcast.48) | data formatting | bytes 4194304 | tf_op jit(solution)/shard_map/reshape | solution.py:27
  128.7 0.0 copy-done.6
  128.7 0.1 iota_compare_fusion.4
  128.8 4.2 %fusion = (f32[128,4,8]{2,1,0:T(4,128)S(1)}, f32[128,4,8,16]{3,2,1,0:T(8,128)}) fusion(pred[128,16]{1,0:T(8,128)(4,1)S(1)} %iota_compare_fusion.4, bf16[128,4,8,128]{3,2,1,0:T(8,128)(2,1)S(1)} %bitcast.50, bf16[128,16,4,128]{3,1,2,0:T(8,128)(2,1)} %copy.27), kind=kOutput, calls=%fused_computation.5 | convolution fusion | flops 16969728 | bytes 3426304 | tf_op jit(solution)/shard_map/rhgd,rphd->rhgp/dot_general | solution.py:41
  133.0 0.7 copy.28
  133.7 4.5 %copy.38 = bf16[128,16,512]{0,2,1:T(8,128)(2,1)} copy(bf16[128,16,512]{2,1,0:T(8,128)(2,1)} %get-tuple-element.3) | data formatting | bytes 4194304
  138.2 0.0 copy-start.3
  138.2 4.6 %copy.33 = bf16[128,16,4,128]{3,1,2,0:T(8,128)(2,1)} copy(bf16[128,16,4,128]{0,3,2,1:T(8,128)(2,1)} %bitcast.49) | data formatting | bytes 4194304 | tf_op jit(solution)/shard_map/reshape | solution.py:30
  142.8 0.0 all-to-all-done.1
  142.8 0.0 copy-done.3
  142.8 1.3 fusion.3
  144.1 0.0 copy-start.1
  144.1 0.7 copy-done.1
  144.9 0.8 reshape.79
  145.6 0.0 copy-start.4
  145.6 2.3 %fusion.22 = f32[128,4,1,8]{3,2,1,0:T(1,128)} fusion(bf16[128,4,128,1]{2,3,1,0:T(2,128)(2,1)} %reshape.79, bf16[128,4,8,128]{3,2,1,0:T(8,128)(2,1)S(1)} %bitcast.51), kind=kOutput, calls=%fused_computation.41 | convolution fusion | flops 1048576 | bytes 1196032 | tf_op jit(solution)/shard_map/rhgd,rhd->rhg/dot_general | solution.py:49
  148.0 1.0 copy.36
  149.0 0.0 copy-done.4
  149.0 0.2 copy.29
  149.2 2.6 %fusion.1 = f32[128,4,8]{2,1,0:T(4,128)S(1)} fusion(f32[128,4,8,16]{3,2,1,0:T(8,128)} %get-tuple-element.9, f32[128,4,8]{2,1,0:T(4,128)S(1)} %copy.29, pred[128,16]{1,0:T(8,128)(4,1)S(1)} %iota_compare_fusion.4), kind=kLoop, calls=%fused_computation.6 | loop fusion | flops 258048 | bytes 296960 | tf_op jit(solution)/shard_map/reduce_sum | solution.py:55
  151.8 0.1 copy.30
  151.9 0.1 copy.31
  152.1 0.1 copy.34
  152.2 0.1 reshape.75
  152.3 3.4 %add_convert_fusion = bf16[128,4,8,128]{3,2,1,0:T(8,128)(2,1)S(1)} fusion(bf16[128,16,4,128]{3,1,2,0:T(8,128)(2,1)} %copy.33, f32[128,4,8,16]{3,2,1,0:T(8,128)} %get-tuple-element.9, f32[128,4,128]{2,1,0:T(4,128)S(1)} %reshape.75, f32[128,4,8]{2,1,0:T(4,128)S(1)} %copy.34, f32[128,4,8]{2,1,0:T(4,128)S(1)} %copy.31, f32[128,4,8]{2,1,0:T(4,128)S(1)} %copy.29, ...), kind=kOutput, calls=%fused_computation.1 | convolution fusion | flops 18677760 | bytes 3721216 | tf_op jit(solution)/shard_map/rhgp,rphd->rhgd/dot_general | solution.py:58
  155.7 1.4 copy.42
  (4 shorter events, 0.1 us)
Async XLA Ops:
  0.6 1.6 %copy-start = (bf16[128,8192]{1,0:T(8,128)(2,1)S(1)}, bf16[128,8192]{1,0:T(8,128)(2,1)}, u32[]{:S(2)}) copy-start(bf16[128,8192]{1,0:T(8,128)(2,1)} %param.9) | copy-start | bytes 6291460
  3.5 99.7 %copy-start.2 = (bf16[1,64,8192]{2,1,0:T(8,128)(2,1)S(1)}, bf16[1,64,8192]{2,1,0:T(8,128)(2,1)}, u32[]{:S(2)}) copy-start(bf16[1,64,8192]{2,1,0:T(8,128)(2,1)} %param.16) | copy-start | bytes 3145732
  3.5 99.7 %copy-start.5 = (bf16[1,64,1024]{2,1,0:T(8,128)(2,1)S(1)}, bf16[1,64,1024]{2,1,0:T(8,128)(2,1)}, u32[]{:S(2)}) copy-start(bf16[1,64,1024]{2,1,0:T(8,128)(2,1)} %param.17) | copy-start | bytes 393220
  108.1 34.7 %all-to-all-start.1 = ((bf16[16,16,1024]{2,1,0:T(8,128)(2,1)}), bf16[16,16,1024]{2,1,0:T(8,128)(2,1)}, u32[]{:S(2)}, u32[]{:S(2)}) async-start(bf16[16,16,1024]{2,1,0:T(8,128)(2,1)} %bitcast.6), calls=%async_computation.1 | async-start | bytes 1048576 | tf_op jit(solution)/shard_map/all_to_all | solution.py:107
  124.0 4.6 %copy-start.6 = (s32[128]{0:T(128)S(1)}, s32[128]{0:T(128)}, u32[]{:S(2)}) copy-start(s32[128]{0:T(128)} %param.13) | copy-start | bytes 1540
  138.2 4.6 %copy-start.3 = (bf16[128,1024]{1,0:T(8,128)(2,1)S(1)}, bf16[128,1024]{1,0:T(8,128)(2,1)}, u32[]{:S(2)}) copy-start(bf16[128,1024]{1,0:T(8,128)(2,1)} %param.11) | copy-start | bytes 786436
  144.1 0.7 copy-start.1
  145.6 3.4 %copy-start.4 = (f32[128,4,8]{0,2,1:T(8,128)S(1)}, f32[128,4,8]{0,2,1:T(8,128)}, u32[]{:S(2)}) copy-start(f32[128,4,8]{0,2,1:T(8,128)} %copy.28) | copy-start | bytes 49156
where the time goes:
time: 158 us; the launch traced here: 157 us
  blocking collectives  99.7 us (63%)
  local copies, waits for them, and re-layouts  30.1 us (19%)
  matrix products  17.4 us (11%)
  starting transfers between devices  5.35 us (3%)
  other arithmetic  3.82 us (2%)
    all_to_all x1, blocking collectives, on_device(): lax.all_to_all(outgoing, 'adapter', split_axis=0, concat_axis=0, tiled=True)  99.7 us
    unnamed x18, local copies, waits for them, and re-layouts  13.2 us
    all_to_all x1, starting transfers between devices, on_device(): lax.all_to_all(expanded_output.reshape(devices, item_count, expanded_outp...  5.35 us
    dot_general x1, matrix products, on_device(): jnp.dot(reduced_output, adapter_up_weight[0], preferred_element_type=jnp....  4.93 us
    reshape x1, local copies, waits for them, and re-layouts, attend(): key_value_cache[:, :, :key_value_split]  4.61 us
    reshape x1, local copies, waits for them, and re-layouts, attend(): key_value_cache[:, :, key_value_split:]  4.6 us
    slice x1, local copies, waits for them, and re-layouts, attend(): key_value_cache[:, :, :key_value_split]  4.6 us
    dot_general x1, matrix products, attend(): jnp.einsum('rhgd,rphd->rhgp', query_head_rows, cached_key_block, preferre...  4.21 us
  transfers between devices with their start and end apart: 1, of which 0 were waited for; matrix products, arithmetic and copies ran while one was open for 19% of the time, Pallas kernels for 0%

commit v1 on v0

v1 whole, which is shorter than its diff:
```python
import functools

import jax
import jax.numpy as jnp
from jax import lax
from jax.experimental import pallas as pl
from jax.experimental.pallas import tpu as pltpu
from jax.sharding import PartitionSpec as P

QUERY_HEADS = 32
KEY_VALUE_HEADS = 4
HEAD_SIZE = 128
GROUP = QUERY_HEADS // KEY_VALUE_HEADS
SPLIT = KEY_VALUE_HEADS * HEAD_SIZE
PLANE = 4
COLS = 1024

adapter_scale = 2.0
score_floor = -1e30
score_scale = HEAD_SIZE ** (-0.5)

NT = (((1,), (1,)), ((), ()))


def slot_lookup(request_adapter, adapter_position_map):
    adapter_index = jnp.arange(adapter_position_map.shape[0], dtype=jnp.int32)
    matches = request_adapter[:, None] == adapter_index[None, :]
    return jnp.sum(jnp.where(matches, adapter_position_map[None, :], 0), axis=1)


def rank_in_slot(slot):
    order = jnp.arange(slot.shape[0], dtype=jnp.int32)
    same = slot[:, None] == slot[None, :]
    before = order[None, :] < order[:, None]
    return jnp.sum((same & before).astype(jnp.int32), axis=1)


def params(*semantics):
    return pltpu.CompilerParams(
        dimension_semantics=semantics, vmem_limit_bytes=40 * 1024 * 1024
    )


def cached_kernel(length_ref, q_ref, cache_ref, mixed_ref, log_ref):
    rows, context = cache_ref.shape[0], cache_ref.shape[1]
    keys = rows * context
    owner_q = lax.rem(lax.broadcasted_iota(jnp.int32, (GROUP * rows, keys), 0), rows)
    column = lax.broadcasted_iota(jnp.int32, (GROUP * rows, keys), 1)
    owner_k, position = column // context, lax.rem(column, context)
    lengths = jnp.concatenate([length_ref[...]] * GROUP, axis=0)
    included = (owner_q == owner_k) & (position < lengths)
    lane = lax.broadcasted_iota(jnp.int32, (rows, HEAD_SIZE), 1)
    logs = jnp.zeros((rows, HEAD_SIZE), jnp.float32)
    for head in range(KEY_VALUE_HEADS):
        first = head * GROUP
        q = jnp.concatenate(
            [
                q_ref[:, (first + g) * HEAD_SIZE : (first + g + 1) * HEAD_SIZE]
                for g in range(GROUP)
            ],
            axis=0,
        )
        k = cache_ref[:, :, head * HEAD_SIZE : (head + 1) * HEAD_SIZE].reshape(keys, HEAD_SIZE)
        v = cache_ref[
            :, :, SPLIT + head * HEAD_SIZE : SPLIT + (head + 1) * HEAD_SIZE
        ].reshape(keys, HEAD_SIZE)
        score = lax.dot_general(q, k, NT, preferred_element_type=jnp.float32) * score_scale
        score = jnp.where(included, score, score_floor)
        peak = jnp.max(score, axis=1, keepdims=True)
        weight = jnp.exp(score - peak)
        total = jnp.sum(weight, axis=1, keepdims=True)
        mixed = jnp.dot(weight.astype(jnp.bfloat16), v, preferred_element_type=jnp.float32)
        mixed = mixed / total
        log = peak + jnp.log(total)
        for g in range(GROUP):
            part = slice(g * rows, (g + 1) * rows)
            mixed_ref[:, (first + g) * HEAD_SIZE : (first + g + 1) * HEAD_SIZE] = mixed[part]
            logs = jnp.where(lane == first + g, log[part], logs)
    log_ref[...] = logs


def cached_attention(queries, cache, lengths):
    rows, context, width = cache.shape
    step = 16
    return pl.pallas_call(
        cached_kernel,
        grid=(rows // step,),
        in_specs=[
            pl.BlockSpec((step, 1), lambda i: (i, 0)),
            pl.BlockSpec((step, queries.shape[1]), lambda i: (i, 0)),
            pl.BlockSpec((step, context, width), lambda i: (i, 0, 0)),
        ],
        out_specs=[
            pl.BlockSpec((step, queries.shape[1]), lambda i: (i, 0)),
            pl.BlockSpec((step, HEAD_SIZE), lambda i: (i, 0)),
        ],
        out_shape=[
            jax.ShapeDtypeStruct(queries.shape, jnp.float32),
            jax.ShapeDtypeStruct((rows, HEAD_SIZE), jnp.float32),
        ],
        compiler_params=params("arbitrary"),
        cost_estimate=pl.CostEstimate(
            flops=2_000_000_000, bytes_accessed=30_000_000, transcendentals=1_000_000
        ),
        name="cached",
    )(lengths.reshape(rows, 1), queries, cache)


def finish_kernel(count, target_ref, base_ref, q_ref, mixed_ref, log_ref, *refs):
    pieces, (attention_ref, written_ref, place_ref) = refs[:count], refs[count:]
    head = pl.program_id(0)
    rows = base_ref.shape[0]

    @pl.when(head == 0)
    def _():
        spots = lax.broadcasted_iota(jnp.int32, place_ref.shape, 1)
        place_ref[...] = (spots == target_ref[...]).astype(jnp.float32).astype(jnp.bfloat16)

    def written(offset):
        columns = pl.ds(pl.multiple_of(offset, HEAD_SIZE), HEAD_SIZE)
        stack = jnp.concatenate([piece[:, columns] for piece in pieces], axis=0)
        delta = jnp.dot(place_ref[...], stack, preferred_element_type=jnp.float32)
        value = (base_ref[:, columns].astype(jnp.float32) + delta).astype(jnp.bfloat16)
        written_ref[:, columns] = value
        return value.astype(jnp.float32)

    new_key = written(head * HEAD_SIZE)
    new_value = written(SPLIT + head * HEAD_SIZE)
    lane = lax.broadcasted_iota(jnp.int32, (rows, HEAD_SIZE), 1)
    logs = log_ref[...]
    for g in range(GROUP):
        part = slice(g * HEAD_SIZE, (g + 1) * HEAD_SIZE)
        query = q_ref[:, part].astype(jnp.float32)
        score = jnp.sum(query * new_key, axis=1, keepdims=True) * score_scale
        log = jnp.sum(jnp.where(lane == head * GROUP + g, logs, 0.0), axis=1, keepdims=True)
        share = 1.0 / (1.0 + jnp.exp(score - log))
        out = new_value + share * (mixed_ref[:, part] - new_value)
        attention_ref[:, part] = out.astype(jnp.bfloat16)


def finish(target, base, queries, mixed, logs, pieces):
    rows = base.shape[0]
    wide = GROUP * HEAD_SIZE
    whole = lambda a: pl.BlockSpec(a.shape, lambda h: (0, 0))
    total = sum(piece.shape[0] for piece in pieces)
    target = target.reshape(rows, 1)
    return pl.pallas_call(
        functools.partial(finish_kernel, len(pieces)),
        grid=(KEY_VALUE_HEADS,),
        in_specs=[
            whole(target),
            whole(base),
            pl.BlockSpec((rows, wide), lambda h: (0, h)),
            pl.BlockSpec((rows, wide), lambda h: (0, h)),
            whole(logs),
        ]
        + [whole(piece) for piece in pieces],
        out_specs=[pl.BlockSpec((rows, wide), lambda h: (0, h)), whole(base)],
        out_shape=[
            jax.ShapeDtypeStruct(queries.shape, jnp.bfloat16),
            jax.ShapeDtypeStruct(base.shape, jnp.bfloat16),
        ],
        scratch_shapes=[pltpu.VMEM((rows, total), jnp.bfloat16)],
        compiler_params=params("arbitrary"),
        name="finish",
    )(target, base, queries, mixed, logs, *pieces)


def pack_kernel(capacity, target_ref, hidden_ref, *outs):
    rows = hidden_ref.shape[0]
    spots = 4 * PLANE * capacity
    spot = lax.broadcasted_iota(jnp.int32, (spots, rows), 0)
    place = (spot == target_ref[...]).astype(jnp.float32).astype(jnp.bfloat16)
    packed = jnp.dot(place, hidden_ref[...], preferred_element_type=jnp.float32)
    packed = packed.astype(jnp.bfloat16)
    start = 0
    for out in outs:
        out[...] = packed[start : start + out.shape[0]]
        start += out.shape[0]


def pack(target, hidden, capacity):
    rows, width = hidden.shape
    heights = [capacity] * PLANE + [3 * capacity] * PLANE
    return pl.pallas_call(
        functools.partial(pack_kernel, capacity),
        grid=(width // COLS,),
        in_specs=[
            pl.BlockSpec((1, rows), lambda c: (0, 0)),
            pl.BlockSpec((rows, COLS), lambda c: (0, c)),
        ],
        out_specs=[pl.BlockSpec((h, COLS), lambda c: (0, c)) for h in heights],
        out_shape=[jax.ShapeDtypeStruct((h, width), jnp.bfloat16) for h in heights],
        compiler_params=params("arbitrary"),
        name="pack",
    )(target.reshape(1, rows), hidden)


def expand(total, up):
    shrunk = total.astype(jnp.bfloat16)
    wide = jnp.dot(shrunk, up, preferred_element_type=jnp.float32)
    return (adapter_scale * wide).astype(jnp.bfloat16)


def early_kernel(capacity, inner_ref, *refs):
    first, rest = refs[:PLANE], refs[PLANE : 2 * PLANE]
    down_refs, up_refs = refs[2 * PLANE : 2 * PLANE + 3], refs[2 * PLANE + 3 : 2 * PLANE + 6]
    outs, totals = refs[2 * PLANE + 6 : 3 * PLANE + 6], refs[3 * PLANE + 6 :]
    step, steps = pl.program_id(0), pl.num_programs(0)
    inner = inner_ref[0] == 1

    def weights(three):
        own, outward, middle = three
        return outward[...], own[...], jnp.where(inner, middle[...], outward[...])

    stacks = [jnp.concatenate([r[...] for r in first], axis=0)]
    for slot in range(2):
        part = slice(slot * capacity, (slot + 1) * capacity)
        stacks.append(jnp.concatenate([r[part] for r in rest], axis=0))
    for total, stack, down in zip(totals, stacks, weights(down_refs)):
        product = lax.dot_general(stack, down, NT, preferred_element_type=jnp.float32)

        @pl.when(step == 0)
        def _():
            total[...] = product

        @pl.when(step > 0)
        def _():
            total[...] += product

    @pl.when(step == steps - 1)
    def _():
        for slot, (total, up) in enumerate(zip(totals, weights(up_refs))):
            wide = expand(total[...], up)
            for k, out in enumerate(outs):
                out[slot * capacity : (slot + 1) * capacity] = wide[
                    k * capacity : (k + 1) * capacity
                ]


def early(inner, first, rest, own_down, own_up, outward, middle, capacity):
    rank, width = own_down.shape
    out_width = own_up.shape[1]
    column = lambda a: pl.BlockSpec((a.shape[0], COLS), lambda c, s: (0, c))
    tail = pl.BlockSpec((rank, out_width), lambda c, s: (0, width // out_width))
    shape = jax.ShapeDtypeStruct((3 * capacity, out_width), jnp.bfloat16)
    return pl.pallas_call(
        functools.partial(early_kernel, capacity),
        grid_spec=pltpu.PrefetchScalarGridSpec(
            num_scalar_prefetch=1,
            grid=(width // COLS,),
            in_specs=[column(a) for a in (*first, *rest, own_down, outward, middle)]
            + [pl.BlockSpec((rank, out_width), lambda c, s: (0, 0)), tail, tail],
            out_specs=[pl.BlockSpec(shape.shape, lambda c, s: (0, 0))] * PLANE,
            scratch_shapes=[pltpu.VMEM((PLANE * capacity, rank), jnp.float32)] * 3,
        ),
        out_shape=[shape] * PLANE,
        compiler_params=params("arbitrary"),
        name="early",
    )(inner, *first, *rest, own_down, outward, middle, own_up, outward, middle)


def late_kernel(capacity, inner_ref, *refs):
    rest, passed = refs[:PLANE], refs[PLANE]
    down_refs, up_refs = refs[PLANE + 1 : PLANE + 3], refs[PLANE + 3 : PLANE + 5]
    outs, total = refs[PLANE + 5 : 3 * PLANE + 5], refs[3 * PLANE + 5]
    step, steps = pl.program_id(0), pl.num_programs(0)
    inner = inner_ref[0] == 1

    def weight(two):
        middle, outward = two
        return jnp.where(inner, middle[...], outward[...])

    stack = jnp.concatenate([r[...] for r in rest] + [passed[...]], axis=0)
    product = lax.dot_general(stack, weight(down_refs), NT, preferred_element_type=jnp.float32)

    @pl.when(step == 0)
    def _():
        total[...] = product

    @pl.when(step > 0)
    def _():
        total[...] += product

    @pl.when(step == steps - 1)
    def _():
        wide = expand(total[...], weight(up_refs))
        for k, out in enumerate(outs):
            out[...] = wide[k * capacity : (k + 1) * capacity]


def late(inner, rest, passed, middle, outward, width, capacity):
    rank = middle.shape[0]
    out_width = middle.shape[1] - width
    last = pl.BlockSpec((capacity, COLS), lambda c, s: (2, c))
    column = lambda a: pl.BlockSpec((a.shape[0], COLS), lambda c, s: (0, c))
    tail = pl.BlockSpec((rank, out_width), lambda c, s: (0, width // out_width))
    shape = jax.ShapeDtypeStruct((capacity, out_width), jnp.bfloat16)
    return pl.pallas_call(
        functools.partial(late_kernel, capacity),
        grid_spec=pltpu.PrefetchScalarGridSpec(
            num_scalar_prefetch=1,
            grid=(width // COLS,),
            in_specs=[last] * PLANE
            + [column(passed), column(middle), column(outward), tail, tail],
            out_specs=[pl.BlockSpec(shape.shape, lambda c, s: (0, 0))] * (2 * PLANE),
            scratch_shapes=[pltpu.VMEM((2 * PLANE * capacity, rank), jnp.float32)],
        ),
        out_shape=[shape] * (2 * PLANE),
        compiler_params=params("arbitrary"),
        name="late",
    )(inner, *rest, passed, middle, outward, middle, outward)


def by_planes(hidden, slot, down, up, capacity):
    devices = lax.axis_size("adapter")
    me = lax.axis_index("adapter")
    plane, place = me // PLANE, me % PLANE
    inner = (plane == 1) | (plane == 2)
    all_devices = range(devices)
    ends = [i for i in all_devices if i // PLANE in (0, 3)]
    middles = [i for i in all_devices if i // PLANE in (1, 2)]
    send = lambda a, pairs: lax.ppermute(a, "adapter", pairs)

    packed = jnp.concatenate([down, up], axis=1)
    outward = send(packed, [(i, i ^ PLANE) for i in all_devices])
    middle = send(packed, [(i, i ^ (3 * PLANE)) for i in middles])

    plane_of, place_of = slot // PLANE, slot % PLANE
    k = place_of ^ place
    distance = jnp.abs(plane_of - plane)
    at_end = (plane_of == 0) | (plane_of == 3)
    kind = jnp.where(
        distance == 0,
        1,
        jnp.where(distance == 2, 3, jnp.where((distance == 3) | at_end, 0, 2)),
    )
    rank = rank_in_slot(slot)
    target = jnp.where(
        kind == 0,
        k * capacity + rank,
        PLANE * capacity + k * 3 * capacity + (kind - 1) * capacity + rank,
    )
    back = jnp.where(
        (kind == 0) & ~inner,
        4 * PLANE * capacity + k * capacity + rank,
        jnp.where(
            kind == 3,
            3 * PLANE * capacity + k * capacity + rank,
            k * 3 * capacity + kind * capacity + rank,
        ),
    )
    outs = pack(target, hidden, capacity)
    first, rest = outs[:PLANE], outs[PLANE:]
    across = [
        [(i, (i // PLANE) * PLANE + ((i % PLANE) ^ k)) for i in all_devices] for k in range(PLANE)
    ]
    first = [first[0]] + [send(first[k], across[k]) for k in range(1, PLANE)]
    rest = [rest[0]] + [send(rest[k], across[k]) for k in range(1, PLANE)]
    outward2 = send(middle, [(i, i ^ PLANE) for i in middles])
    middle2 = send(outward, [(i, i ^ (3 * PLANE)) for i in middles])
    passed = jnp.concatenate(first, axis=0)
    passed, _ = lax.optimization_barrier((passed, outward))
    passed = send(passed, [(i, i ^ PLANE) for i in ends])

    inner_flag = inner.astype(jnp.int32).reshape(1)
    soon = early(inner_flag, first, rest, down, up, outward, middle, capacity)
    soon = [soon[0]] + [send(soon[k], across[k]) for k in range(1, PLANE)]
    outs = late(inner_flag, rest, passed, middle2, outward2, hidden.shape[1], capacity)
    last = [outs[0]] + [send(outs[k], across[k]) for k in range(1, PLANE)]
    far = [
        send(outs[PLANE + k], [(i, (i ^ PLANE) ^ k) for i in middles]) for k in range(PLANE)
    ]
    return back, [*soon, *last, *far]


def by_rows(hidden, slot, down, up, capacity):
    devices = lax.axis_size("adapter")
    target = slot * capacity + rank_in_slot(slot)
    spots = jnp.arange(devices * capacity, dtype=jnp.int32)
    placing = (target[None, :] == spots[:, None]).astype(jnp.bfloat16)
    outgoing = jnp.dot(placing, hidden, preferred_element_type=jnp.float32).astype(jnp.bfloat16)
    outgoing = outgoing.reshape(devices, capacity, hidden.shape[1])
    incoming = lax.all_to_all(outgoing, "adapter", split_axis=0, concat_axis=0, tiled=True)
    rows = incoming.reshape(-1, hidden.shape[1])
    shrunk = lax.dot_general(rows, down, NT, preferred_element_type=jnp.float32)
    wide = expand(shrunk, up)
    returned = lax.all_to_all(
        wide.reshape(devices, capacity, -1), "adapter", split_axis=0, concat_axis=0, tiled=True
    )
    return target, [returned.reshape(devices * capacity, -1)]


def on_device(
    hidden,
    queries,
    base_key_value,
    key_value_cache,
    lengths,
    request_adapter_index,
    adapter_position_map,
    adapter_down_weight,
    adapter_up_weight,
):
    devices = lax.axis_size("adapter")
    capacity = max(2, 2 * hidden.shape[0] // devices)
    slot = slot_lookup(request_adapter_index[:, 0], adapter_position_map)
    deliver = by_planes if devices == 4 * PLANE else by_rows
    target, pieces = deliver(
        hidden, slot, adapter_down_weight[0], adapter_up_weight[0], capacity
    )
    mixed, logs = cached_attention(queries, key_value_cache, lengths)
    return finish(target, base_key_value, queries, mixed, logs, pieces)


def solution(mesh):
    rows = P(("groups", "adapter"), None)
    deep = P(("groups", "adapter"), None, None)
    placed = (
        rows,
        rows,
        rows,
        deep,
        P(("groups", "adapter")),
        rows,
        P("groups"),
        deep,
        deep,
    )
    return jax.shard_map(
        on_device, mesh=mesh, in_specs=placed, out_specs=(rows, rows), check_vma=False
    )
```

time: 158 us -> 125 us (0.79)
  blocking collectives: 99.7 us -> 0 us
  waiting for transfers between devices: 0.01 us -> 46.1 us
  Pallas kernels: 0 us -> 28.4 us
  starting transfers between devices: 5.35 us -> 27.5 us
  matrix products: 17.4 us -> 0 us
  local copies, waits for them, and re-layouts: 30.1 us -> 16.6 us
    all_to_all x1 -> x0, blocking collectives: 99.7 us -> none  [on_device(): lax.all_to_all(outgoing, 'adapter', split_axis=0, concat_axis=0, tiled=True)]
    ppermute x0 -> x21, waiting for transfers between devices: none -> 46.1 us  [by_planes(): send = lambda a, pairs: lax.ppermute(a, 'adapter', pairs)]
    pallas_call x0 -> x5, Pallas kernels: none -> 28.4 us  [the longest x1 8.32 us: early(): pl.pallas_call(functools.partial(early_kernel, capacity), grid_spec=pltpu...]
    ppermute x0 -> x21, starting transfers between devices: none -> 27.5 us  [by_planes(): send = lambda a, pairs: lax.ppermute(a, 'adapter', pairs)]
    dot_general x6 -> x0, matrix products: 17.4 us -> none  [the longest x1 4.93 us: on_device(): jnp.dot(reduced_output, adapter_up_weight[0], preferred_element_type=jnp....]
    reshape x3 -> x1, local copies, waits for them, and re-layouts: 9.98 us -> 0.11 us  [cached_attention(): lengths.reshape(rows, 1)]
    all_to_all x1 -> x0, starting transfers between devices: 5.35 us -> none  [on_device(): lax.all_to_all(expanded_output.reshape(devices, item_count, expanded_outp...]
    slice x1 -> x0, local copies, waits for them, and re-layouts: 4.6 us -> none  [attend(): key_value_cache[:, :, :key_value_split]]
  transfers between devices with their start and end apart: 1 -> 21, of which waited for: 0 -> 3; matrix products, arithmetic and copies ran while one was open for 19% -> 3% of each run, Pallas kernels for 0% -> 20%
where the time goes in v1:
time: 125 us; the launch traced here: 124 us
  waiting for transfers between devices  46.1 us (37%)
  Pallas kernels  28.4 us (23%)
  starting transfers between devices  27.5 us (22%)
  local copies, waits for them, and re-layouts  16.6 us (13%)
  other arithmetic  3.94 us (3%)
    ppermute x21, waiting for transfers between devices, by_planes(): send = lambda a, pairs: lax.ppermute(a, 'adapter', pairs)  46.1 us
    ppermute x21, starting transfers between devices, by_planes(): send = lambda a, pairs: lax.ppermute(a, 'adapter', pairs)  27.5 us
    unnamed x54, local copies, waits for them, and re-layouts  15 us
    pallas_call x1, Pallas kernels, early(): pl.pallas_call(functools.partial(early_kernel, capacity), grid_spec=pltpu...  8.32 us
    pallas_call x1, Pallas kernels, late(): pl.pallas_call(functools.partial(late_kernel, capacity), grid_spec=pltpu....  5.8 us
    pallas_call x1, Pallas kernels, cached_attention(): pl.pallas_call(cached_kernel, grid=(rows // step,), in_specs=[pl.BlockSpe...  5.6 us
    pallas_call x1, Pallas kernels, pack(): pl.pallas_call(functools.partial(pack_kernel, capacity), grid=(width // C...  4.47 us
    pallas_call x1, Pallas kernels, finish(): pl.pallas_call(functools.partial(finish_kernel, len(pieces)), grid=(KEY_V...  4.17 us
  transfers between devices with their start and end apart: 21, of which 3 were waited for; matrix products, arithmetic and copies ran while one was open for 3% of the time, Pallas kernels for 20%

profile of v1, /device:TPU:0, one launch (start us, length us, event | category | flops | bytes accessed | tf_op | source)
XLA Modules:
  0.0 123.5 jit_solution(11840642636488763467)
XLA Ops:
  0.6 2.4 %pad_maximum_fusion = bf16[64,9216]{1,0:T(8,128)(2,1)} fusion(bf16[64,1024]{1,0:T(8,128)(2,1)} %bitcast.29, bf16[64,8192]{1,0:T(8,128)(2,1)} %bitcast.27), kind=kLoop, calls=%fused_computation | loop fusion | flops 2359296 | bytes 2359296 | tf_op jit(solution)/shard_map/concatenate | solution.py:325
  3.1 3.0 %collective-permute-start.6 = (bf16[64,9216]{1,0:T(8,128)(2,1)}, bf16[64,9216]{1,0:T(8,128)(2,1)S(1)}, u32[]{:S(2)}, u32[]{:S(2)}) collective-permute-start(bf16[64,9216]{1,0:T(8,128)(2,1)} %pad_maximum_fusion), channel_id=1, source_target_pairs={{0,4},{1,5},{2,6},{3,7},{4,0},{5,1},{6,2},{7,3},{8,12},{9,13},{10,... | collective-permute-start | bytes 3538952 | tf_op jit(solution)/shard_map/ppermute | solution.py:323
  6.1 0.7 collective-permute-start.7
  6.9 0.1 select_reduce_fusion
  7.0 0.2 convert_reduce_fusion
  7.2 0.0 copy-start.7
  7.2 1.6 %copy-done.7 = bf16[128,8192]{1,0:T(8,128)(2,1)S(1)} copy-done((bf16[128,8192]{1,0:T(8,128)(2,1)S(1)}, bf16[128,8192]{1,0:T(8,128)(2,1)}, u32[]{:S(2)}) %copy-start.7) | copy-done | bytes 2097176
  8.8 4.5 %pack.1 = (bf16[16,8192]{1,0:T(8,128)(2,1)S(1)}, bf16[16,8192]{1,0:T(8,128)(2,1)S(1)}, bf16[16,8192]{1,0:T(8,128)(2,1)S(1)}, bf16[16,8192]{1,0:T(8,128)(2,1)S(1)...) custom-call(s32[1,128]{1,0:T(1,128)S(1)} %compare_select_fusion.targ, ...), custom_call_target="tpu_custom_call" | custom-call | tf_op jit(solution)/shard_map/pack/pallas_call | solution.py:185
  13.2 0.9 copy-done.1
  14.1 1.5 %collective-permute-start.1 = (bf16[16,8192]{1,0:T(8,128)(2,1)S(1)}, bf16[16,8192]{1,0:T(8,128)(2,1)S(1)}, u32[]{:S(2)}, u32[]{:S(2)}) collective-permute-start(bf16[16,8192]{1,0:T(8,128)(2,1)S(1)} %get-tuple-element.29), channel_id=1, source_target_pairs={{0,2},{1,3},{2,0},{3,1},{4,6},{5,7},{6,4},{7,5},{8,10},{9,11},{10,... | collective-permute-start | bytes 786440 | tf_op jit(solution)/shard_map/ppermute | solution.py:323
  15.6 0.4 collective-permute-start.2
  16.0 0.0 collective-permute-done.refs_1_
  16.0 0.3 collective-permute-start.3
  16.3 16.0 %collective-permute-done.6.refs_9_.refs_12_ = bf16[64,9216]{1,0:T(8,128)(2,1)S(1)} collective-permute-done((bf16[64,9216]{1,0:T(8,128)(2,1)}, bf16[64,9216]{1,0:T(8,128)(2,1)S(1)}, u32[]{:S(2)}, u32[]{:S(2)}) %collective-permute-start.6) | collective-permute-done | bytes 1179680 | tf_op jit(solution)/shard_map/ppermute | solution.py:323
  32.3 0.7 collective-permute-start.12
  33.0 0.0 collective-permute-done.7.refs_10_.refs_13_
  33.0 1.3 %collective-permute-start.13 = (bf16[64,9216]{1,0:T(8,128)(2,1)S(1)}, bf16[64,9216]{1,0:T(8,128)(2,1)}, u32[]{:S(2)}, u32[]{:S(2)}) collective-permute-start(bf16[64,9216]{1,0:T(8,128)(2,1)S(1)} %collective-permute-done.7.refs_10_.refs_13_), channel_id=1, source_target_pairs={{4,0},{5,1},{6,2},{7,3},{8,12},{9,13},{10,14},{11,15},{20,16},{21,... | collective-permute-start | bytes 3538952 | tf_op jit(solution)/shard_map/ppermute | solution.py:323
  34.3 0.0 collective-permute-done.2.refs_3_
  34.4 1.1 pad_maximum_fusion.1
  35.5 8.4 %collective-permute-start.11 = (bf16[64,8192]{1,0:T(8,128)(2,1)}, bf16[64,8192]{1,0:T(8,128)(2,1)}, u32[]{:S(2)}, u32[]{:S(2)}) collective-permute-start(bf16[64,8192]{1,0:T(8,128)(2,1)} %pad_maximum_fusion.1), channel_id=1, source_target_pairs={{0,4},{1,5},{2,6},{3,7},{12,8},{13,9},{14,10},{15,11},{16,20},{17,... | collective-permute-start | bytes 3145736 | tf_op jit(solution)/shard_map/ppermute | solution.py:323
  43.9 1.5 %collective-permute-start.4 = (bf16[48,8192]{1,0:T(8,128)(2,1)}, bf16[48,8192]{1,0:T(8,128)(2,1)}, u32[]{:S(2)}, u32[]{:S(2)}) collective-permute-start(bf16[48,8192]{1,0:T(8,128)(2,1)} %get-tuple-element.33), channel_id=1, source_target_pairs={{0,2},{1,3},{2,0},{3,1},{4,6},{5,7},{6,4},{7,5},{8,10},{9,11},{10,... | collective-permute-start | bytes 2359304 | tf_op jit(solution)/shard_map/ppermute | solution.py:323
  45.4 0.0 collective-permute-done.3.refs_5_.refs_1_
  45.4 0.9 copy-done.4
  46.3 0.1 collective-permute-start.5
  46.4 0.7 copy.23
  47.1 0.7 copy.19
  47.8 16.8 %collective-permute-done.4.refs_6_.refs_2_ = bf16[48,8192]{1,0:T(8,128)(2,1)} collective-permute-done((bf16[48,8192]{1,0:T(8,128)(2,1)}, bf16[48,8192]{1,0:T(8,128)(2,1)}, u32[]{:S(2)}, u32[]{:S(2)}) %collective-permute-start.4) | collective-permute-done | bytes 786464 | tf_op jit(solution)/shard_map/ppermute | solution.py:323
  64.7 13.2 %collective-permute-done.5.refs_7_.refs_3_ = bf16[48,8192]{1,0:T(8,128)(2,1)} collective-permute-done((bf16[48,8192]{1,0:T(8,128)(2,1)}, bf16[48,8192]{1,0:T(8,128)(2,1)}, u32[]{:S(2)}, u32[]{:S(2)}) %collective-permute-start.5) | collective-permute-done | bytes 786464 | tf_op jit(solution)/shard_map/ppermute | solution.py:323
  77.9 1.2 copy-done
  79.1 1.1 copy-done.2
  80.3 1.1 copy-done.5
  81.4 0.9 copy-done.10
  82.3 0.9 copy-done.12
  83.3 0.9 copy-done.14
  84.2 0.9 copy-done.16
  85.2 0.9 copy-done.17
  86.1 8.3 %early.1 = (bf16[48,1024]{1,0:T(8,128)(2,1)S(1)}, bf16[48,1024]{1,0:T(8,128)(2,1)}, bf16[48,1024]{1,0:T(8,128)(2,1)}, bf16[48,1024]{1,0:T(8,128)(2,1)}) custom-call(s32[1]{0:T(128)} %bitcast.4.inner_ref, bf16[16,8192]{1,0:T(8,128)(2,1)S(1)} %copy-done.10, bf16[16,8192]{1,0:T(8,128)(2,1)S(1)} %copy-done.12, bf16[16,8192]{1,0:T(8,128)(2,1)S(1)} %copy-done.14, ...), custom_call_target="tpu_custom_call" | custom-call | tf_op jit(solution)/shard_map/early/pallas_call | solution.py:247
  94.4 1.9 %collective-permute-start.10 = (bf16[48,1024]{1,0:T(8,128)(2,1)}, bf16[48,1024]{1,0:T(8,128)(2,1)}, u32[]{:S(2)}, u32[]{:S(2)}) collective-permute-start(bf16[48,1024]{1,0:T(8,128)(2,1)} %get-tuple-element.38), channel_id=1, source_target_pairs={{0,3},{1,2},{2,1},{3,0},{4,7},{5,6},{6,5},{7,4},{8,11},{9,10},{10,... | collective-permute-start | bytes 294920 | tf_op jit(solution)/shard_map/ppermute | solution.py:323
  96.3 0.0 collective-permute-start.8
  96.3 0.0 collective-permute-done.11.refs_4_
  96.3 0.0 copy-start.24
  96.4 0.6 collective-permute-start.9
  97.0 0.0 collective-permute-done.12.refs_5_.refs_7_
  97.0 0.0 collective-permute-done.13.refs_6_.refs_8_
  97.0 5.8 %late.1 = (bf16[16,1024]{1,0:T(8,128)(2,1)S(1)}, bf16[16,1024]{1,0:T(8,128)(2,1)S(1)}, bf16[16,1024]{1,0:T(8,128)(2,1)S(1)}, bf16[16,1024]{1,0:T(8,128)(2,1)S(1)...) custom-call(s32[1]{0:T(128)} %bitcast.4.inner_ref, ...), custom_call_target="tpu_custom_call" | custom-call | tf_op jit(solution)/shard_map/late/pallas_call | solution.py:299
  102.8 0.3 collective-permute-start.14
  103.1 1.5 %collective-permute-start.15 = (bf16[16,1024]{1,0:T(8,128)(2,1)S(1)}, bf16[16,1024]{1,0:T(8,128)(2,1)S(1)}, u32[]{:S(2)}, u32[]{:S(2)}) collective-permute-start(bf16[16,1024]{1,0:T(8,128)(2,1)S(1)} %get-tuple-element.42), channel_id=1, source_target_pairs={{0,2},{1,3},{2,0},{3,1},{4,6},{5,7},{6,4},{7,5},{8,10},{9,11},{10,... | collective-permute-start | bytes 98312 | tf_op jit(solution)/shard_map/ppermute | solution.py:323
  104.6 0.1 select_select_fusion.target_ref
  104.7 0.1 copy.26.length_ref
  104.8 0.2 collective-permute-start.16
  105.1 1.3 %collective-permute-start.17 = (bf16[16,1024]{1,0:T(8,128)(2,1)S(1)}, bf16[16,1024]{1,0:T(8,128)(2,1)S(1)}, u32[]{:S(2)}, u32[]{:S(2)}) collective-permute-start(bf16[16,1024]{1,0:T(8,128)(2,1)S(1)} %get-tuple-element.44), channel_id=1, source_target_pairs={{4,0},{5,1},{6,2},{7,3},{8,12},{9,13},{10,14},{11,15},{20,16},{21,... | collective-permute-start | bytes 98312 | tf_op jit(solution)/shard_map/ppermute | solution.py:323
  106.3 0.0 collective-permute-done.9.refs_2_
  106.4 1.3 %collective-permute-start.18 = (bf16[16,1024]{1,0:T(8,128)(2,1)S(1)}, bf16[16,1024]{1,0:T(8,128)(2,1)S(1)}, u32[]{:S(2)}, u32[]{:S(2)}) collective-permute-start(bf16[16,1024]{1,0:T(8,128)(2,1)S(1)} %get-tuple-element.45), channel_id=1, source_target_pairs={{4,1},{5,0},{6,3},{7,2},{8,13},{9,12},{10,15},{11,14},{20,17},{21,... | collective-permute-start | bytes 98312 | tf_op jit(solution)/shard_map/ppermute | solution.py:323
  107.7 0.0 collective-permute-done.14.refs_5_
  107.7 1.3 %collective-permute-start.19 = (bf16[16,1024]{1,0:T(8,128)(2,1)S(1)}, bf16[16,1024]{1,0:T(8,128)(2,1)S(1)}, u32[]{:S(2)}, u32[]{:S(2)}) collective-permute-start(bf16[16,1024]{1,0:T(8,128)(2,1)S(1)} %get-tuple-element.46), channel_id=1, source_target_pairs={{4,2},{5,3},{6,0},{7,1},{8,14},{9,15},{10,12},{11,13},{20,18},{21,... | collective-permute-start | bytes 98312 | tf_op jit(solution)/shard_map/ppermute | solution.py:323
  109.0 1.3 %collective-permute-start.20 = (bf16[16,1024]{1,0:T(8,128)(2,1)S(1)}, bf16[16,1024]{1,0:T(8,128)(2,1)S(1)}, u32[]{:S(2)}, u32[]{:S(2)}) collective-permute-start(bf16[16,1024]{1,0:T(8,128)(2,1)S(1)} %get-tuple-element.47), channel_id=1, source_target_pairs={{4,3},{5,2},{6,1},{7,0},{8,15},{9,14},{10,13},{11,12},{20,19},{21,... | collective-permute-start | bytes 98312 | tf_op jit(solution)/shard_map/ppermute | solution.py:323
  110.3 0.0 copy-start.8
  110.3 1.2 copy-done.8
  111.5 2.2 %copy-done.21 = bf16[128,16,1024]{2,1,0:T(8,128)(2,1)S(1)} copy-done((bf16[128,16,1024]{2,1,0:T(8,128)(2,1)S(1)}, bf16[128,16,1024]{2,1,0:T(8,128)(2,1)}, u32[]{:S(2)}) %copy-start.21) | copy-done | bytes 4194328
  113.7 5.6 %cached.1 = (f32[128,4096]{1,0:T(8,128)S(1)}, f32[128,128]{1,0:T(8,128)S(1)}) custom-call(s32[128,1]{1,0:T(8,128)S(1)} %copy.26.length_ref, bf16[128,4096]{1,0:T(8,128)(2,1)S(1)} %copy-done.8, bf16[128,16,1024]{2,1,0:T(8,128)(2,1)S(1)} %copy-done.21), custom_call_target="tpu_custom_call" | custom-call | flops 2000000000 | bytes 30000000 | tf_op jit(solution)/shard_map/cached/pallas_call | solution.py:85
  119.3 0.0 collective-permute-done.16.refs_7_
  119.3 0.0 collective-permute-done.19.refs_10_
  119.3 0.0 collective-permute-done.20.refs_11_
  119.4 4.2 %finish.1 = (bf16[128,4096]{1,0:T(8,128)(2,1)}, bf16[128,1024]{1,0:T(8,128)(2,1)}) custom-call(s32[128,1]{1,0:T(8,128)S(1)} %select_select_fusion.target_ref, bf16[128,1024]{1,0:T(8,128)(2,1)S(1)} %copy-done.18, bf16[128,4096]{1,0:T(8,128)(2,1)S(1)} %copy-done.8, f32[128,4096]{1,0:T(8,128)S(1)} %get-tuple-element.25.mixed_ref, ...), custom_call_target="tpu_custom_call" | custom-call | tf_op jit(solution)/shard_map/finish/pallas_call | solution.py:147
  (46 shorter events, 0.1 us)
Async XLA Ops:
  0.6 6.2 %copy-start.26 = (s32[128,1]{0,1:T(1,128)S(1)}, s32[128,1]{0,1:T(1,128)}, u32[]{:S(2)}) copy-start(s32[128,1]{0,1:T(1,128)} %param.14) | copy-start | bytes 1540
  0.6 6.2 %copy-start.25 = (s32[16]{0:T(128)S(1)}, s32[16]{0:T(128)}, u32[]{:S(2)}) copy-start(s32[16]{0:T(128)} %param.15) | copy-start | bytes 196
  3.1 29.2 %collective-permute-start.6 = (bf16[64,9216]{1,0:T(8,128)(2,1)}, bf16[64,9216]{1,0:T(8,128)(2,1)S(1)}, u32[]{:S(2)}, u32[]{:S(2)}) collective-permute-start(bf16[64,9216]{1,0:T(8,128)(2,1)} %pad_maximum_fusion), channel_id=1, source_target_pairs={{0,4},{1,5},{2,6},{3,7},{4,0},{5,1},{6,2},{7,3},{8,12},{9,13},{10,... | collective-permute-start | bytes 3538952 | tf_op jit(solution)/shard_map/ppermute | solution.py:323
  6.1 26.9 %collective-permute-start.7 = (bf16[64,9216]{1,0:T(8,128)(2,1)}, bf16[64,9216]{1,0:T(8,128)(2,1)S(1)}, u32[]{:S(2)}, u32[]{:S(2)}) collective-permute-start(bf16[64,9216]{1,0:T(8,128)(2,1)} %pad_maximum_fusion), channel_id=1, source_target_pairs={{4,8},{5,9},{6,10},{7,11},{8,4},{9,5},{10,6},{11,7},{20,24},{21,25... | collective-permute-start | bytes 3538952 | tf_op jit(solution)/shard_map/ppermute | solution.py:323
  7.2 1.6 %copy-start.7 = (bf16[128,8192]{1,0:T(8,128)(2,1)S(1)}, bf16[128,8192]{1,0:T(8,128)(2,1)}, u32[]{:S(2)}) copy-start(bf16[128,8192]{1,0:T(8,128)(2,1)} %hidden_ref.1) | copy-start | bytes 6291460
  13.2 0.9 copy-start.1
  14.1 31.2 %copy-start.9 = (bf16[16,8192]{1,0:T(8,128)(2,1)}, bf16[16,8192]{1,0:T(8,128)(2,1)S(1)}, u32[]{:S(2)}) copy-start(bf16[16,8192]{1,0:T(8,128)(2,1)S(1)} %get-tuple-element.27.refs_0_) | copy-start | bytes 786436
  14.1 1.9 %collective-permute-start = (bf16[16,8192]{1,0:T(8,128)(2,1)S(1)}, bf16[16,8192]{1,0:T(8,128)(2,1)S(1)}, u32[]{:S(2)}, u32[]{:S(2)}) collective-permute-start(bf16[16,8192]{1,0:T(8,128)(2,1)S(1)} %get-tuple-element.28), channel_id=1, source_target_pairs={{0,1},{1,0},{2,3},{3,2},{4,5},{5,4},{6,7},{7,6},{8,9},{9,8},{10,11... | collective-permute-start | bytes 786440 | tf_op jit(solution)/shard_map/ppermute | solution.py:323
  14.1 20.2 %collective-permute-start.1 = (bf16[16,8192]{1,0:T(8,128)(2,1)S(1)}, bf16[16,8192]{1,0:T(8,128)(2,1)S(1)}, u32[]{:S(2)}, u32[]{:S(2)}) collective-permute-start(bf16[16,8192]{1,0:T(8,128)(2,1)S(1)} %get-tuple-element.29), channel_id=1, source_target_pairs={{0,2},{1,3},{2,0},{3,1},{4,6},{5,7},{6,4},{7,5},{8,10},{9,11},{10,... | collective-permute-start | bytes 786440 | tf_op jit(solution)/shard_map/ppermute | solution.py:323
  15.6 18.7 %collective-permute-start.2 = (bf16[16,8192]{1,0:T(8,128)(2,1)S(1)}, bf16[16,8192]{1,0:T(8,128)(2,1)S(1)}, u32[]{:S(2)}, u32[]{:S(2)}) collective-permute-start(bf16[16,8192]{1,0:T(8,128)(2,1)S(1)} %get-tuple-element.30), channel_id=1, source_target_pairs={{0,3},{1,2},{2,1},{3,0},{4,7},{5,6},{6,5},{7,4},{8,11},{9,10},{10,... | collective-permute-start | bytes 786440 | tf_op jit(solution)/shard_map/ppermute | solution.py:323
  16.0 30.3 %copy-start.11 = (bf16[16,8192]{1,0:T(8,128)(2,1)}, bf16[16,8192]{1,0:T(8,128)(2,1)S(1)}, u32[]{:S(2)}) copy-start(bf16[16,8192]{1,0:T(8,128)(2,1)S(1)} %collective-permute-done.refs_1_) | copy-start | bytes 786436
  16.0 29.4 %collective-permute-start.3 = (bf16[48,8192]{1,0:T(8,128)(2,1)S(1)}, bf16[48,8192]{1,0:T(8,128)(2,1)S(1)}, u32[]{:S(2)}, u32[]{:S(2)}) collective-permute-start(bf16[48,8192]{1,0:T(8,128)(2,1)S(1)} %get-tuple-element.32), channel_id=1, source_target_pairs={{0,1},{1,0},{2,3},{3,2},{4,5},{5,4},{6,7},{7,6},{8,9},{9,8},{10,11... | collective-permute-start | bytes 2359304 | tf_op jit(solution)/shard_map/ppermute | solution.py:323
  32.3 64.7 %collective-permute-start.12 = (bf16[64,9216]{1,0:T(8,128)(2,1)S(1)}, bf16[64,9216]{1,0:T(8,128)(2,1)S(1)}, u32[]{:S(2)}, u32[]{:S(2)}) collective-permute-start(bf16[64,9216]{1,0:T(8,128)(2,1)S(1)} %collective-permute-done.6.refs_9_.refs_12_), channel_id=1, source_target_pairs={{4,8},{5,9},{6,10},{7,11},{8,4},{9,5},{10,6},{11,7},{20,24},{21,25... | collective-permute-start | bytes 3538952 | tf_op jit(solution)/shard_map/ppermute | solution.py:323
  33.0 63.9 %collective-permute-start.13 = (bf16[64,9216]{1,0:T(8,128)(2,1)S(1)}, bf16[64,9216]{1,0:T(8,128)(2,1)}, u32[]{:S(2)}, u32[]{:S(2)}) collective-permute-start(bf16[64,9216]{1,0:T(8,128)(2,1)S(1)} %collective-permute-done.7.refs_10_.refs_13_), channel_id=1, source_target_pairs={{4,0},{5,1},{6,2},{7,3},{8,12},{9,13},{10,14},{11,15},{20,16},{21,... | collective-permute-start | bytes 3538952 | tf_op jit(solution)/shard_map/ppermute | solution.py:323
  34.3 12.0 %copy-start.13 = (bf16[16,8192]{1,0:T(8,128)(2,1)}, bf16[16,8192]{1,0:T(8,128)(2,1)S(1)}, u32[]{:S(2)}) copy-start(bf16[16,8192]{1,0:T(8,128)(2,1)S(1)} %collective-permute-done.1.refs_2_) | copy-start | bytes 786436
  34.3 11.9 %copy-start.15 = (bf16[16,8192]{1,0:T(8,128)(2,1)}, bf16[16,8192]{1,0:T(8,128)(2,1)S(1)}, u32[]{:S(2)}) copy-start(bf16[16,8192]{1,0:T(8,128)(2,1)S(1)} %collective-permute-done.2.refs_3_) | copy-start | bytes 786436
  35.5 60.9 %collective-permute-start.11 = (bf16[64,8192]{1,0:T(8,128)(2,1)}, bf16[64,8192]{1,0:T(8,128)(2,1)}, u32[]{:S(2)}, u32[]{:S(2)}) collective-permute-start(bf16[64,8192]{1,0:T(8,128)(2,1)} %pad_maximum_fusion.1), channel_id=1, source_target_pairs={{0,4},{1,5},{2,6},{3,7},{12,8},{13,9},{14,10},{15,11},{16,20},{17,... | collective-permute-start | bytes 3145736 | tf_op jit(solution)/shard_map/ppermute | solution.py:323
  43.9 20.8 %collective-permute-start.4 = (bf16[48,8192]{1,0:T(8,128)(2,1)}, bf16[48,8192]{1,0:T(8,128)(2,1)}, u32[]{:S(2)}, u32[]{:S(2)}) collective-permute-start(bf16[48,8192]{1,0:T(8,128)(2,1)} %get-tuple-element.33), channel_id=1, source_target_pairs={{0,2},{1,3},{2,0},{3,1},{4,6},{5,7},{6,4},{7,5},{8,10},{9,11},{10,... | collective-permute-start | bytes 2359304 | tf_op jit(solution)/shard_map/ppermute | solution.py:323
  45.4 0.9 copy-start.4
  46.3 31.6 %collective-permute-start.5 = (bf16[48,8192]{1,0:T(8,128)(2,1)}, bf16[48,8192]{1,0:T(8,128)(2,1)}, u32[]{:S(2)}, u32[]{:S(2)}) collective-permute-start(bf16[48,8192]{1,0:T(8,128)(2,1)} %get-tuple-element.34), channel_id=1, source_target_pairs={{0,3},{1,2},{2,1},{3,0},{4,7},{5,6},{6,5},{7,4},{8,11},{9,10},{10,... | collective-permute-start | bytes 2359304 | tf_op jit(solution)/shard_map/ppermute | solution.py:323
  77.9 1.2 copy-start
  79.1 1.1 copy-start.2
  80.2 1.1 copy-start.5
  81.4 0.9 copy-start.10
  82.3 0.9 copy-start.12
  83.3 0.9 copy-start.14
  84.2 0.9 copy-start.16
  85.2 0.9 copy-start.17
  86.1 10.9 %copy-start.3 = (bf16[48,8192]{1,0:T(8,128)(2,1)S(1)}, bf16[48,8192]{1,0:T(8,128)(2,1)}, u32[]{:S(2)}) copy-start(bf16[48,8192]{1,0:T(8,128)(2,1)} %copy-done.1) | copy-start | bytes 2359300
  86.1 10.9 %copy-start.6 = (bf16[48,8192]{1,0:T(8,128)(2,1)S(1)}, bf16[48,8192]{1,0:T(8,128)(2,1)}, u32[]{:S(2)}) copy-start(bf16[48,8192]{1,0:T(8,128)(2,1)} %copy-done.4) | copy-start | bytes 2359300
  94.4 8.4 %copy-start.19 = (bf16[48,1024]{1,0:T(8,128)(2,1)}, bf16[48,1024]{1,0:T(8,128)(2,1)S(1)}, u32[]{:S(2)}) copy-start(bf16[48,1024]{1,0:T(8,128)(2,1)S(1)} %get-tuple-element.35.refs_0_) | copy-start | bytes 294916
  94.4 10.4 %collective-permute-start.10 = (bf16[48,1024]{1,0:T(8,128)(2,1)}, bf16[48,1024]{1,0:T(8,128)(2,1)}, u32[]{:S(2)}, u32[]{:S(2)}) collective-permute-start(bf16[48,1024]{1,0:T(8,128)(2,1)} %get-tuple-element.38), channel_id=1, source_target_pairs={{0,3},{1,2},{2,1},{3,0},{4,7},{5,6},{6,5},{7,4},{8,11},{9,10},{10,... | collective-permute-start | bytes 294920 | tf_op jit(solution)/shard_map/ppermute | solution.py:323
  96.3 8.7 %collective-permute-start.8 = (bf16[48,1024]{1,0:T(8,128)(2,1)}, bf16[48,1024]{1,0:T(8,128)(2,1)}, u32[]{:S(2)}, u32[]{:S(2)}) collective-permute-start(bf16[48,1024]{1,0:T(8,128)(2,1)} %get-tuple-element.36), channel_id=1, source_target_pairs={{0,1},{1,0},{2,3},{3,2},{4,5},{5,4},{6,7},{7,6},{8,9},{9,8},{10,11... | collective-permute-start | bytes 294920 | tf_op jit(solution)/shard_map/ppermute | solution.py:323
  96.3 8.2 %copy-start.22 = (s32[128,1]{1,0:T(8,128)S(1)}, s32[128,1]{1,0:T(8,128)}, u32[]{:S(2)}) copy-start(s32[128,1]{1,0:T(8,128)} %copy.23) | copy-start | bytes 1540
  96.3 8.2 %copy-start.23 = (s32[128,1]{1,0:T(8,128)S(1)}, s32[128,1]{1,0:T(8,128)}, u32[]{:S(2)}) copy-start(s32[128,1]{1,0:T(8,128)} %copy.19) | copy-start | bytes 1540
  96.3 8.4 %copy-start.24 = (s32[128]{0:T(128)S(1)}, s32[128]{0:T(128)}, u32[]{:S(2)}) copy-start(s32[128]{0:T(128)} %param.13) | copy-start | bytes 1540
  96.4 10.0 %collective-permute-start.9 = (bf16[48,1024]{1,0:T(8,128)(2,1)}, bf16[48,1024]{1,0:T(8,128)(2,1)}, u32[]{:S(2)}, u32[]{:S(2)}) collective-permute-start(bf16[48,1024]{1,0:T(8,128)(2,1)} %get-tuple-element.37), channel_id=1, source_target_pairs={{0,2},{1,3},{2,0},{3,1},{4,6},{5,7},{6,4},{7,5},{8,10},{9,11},{10,... | collective-permute-start | bytes 294920 | tf_op jit(solution)/shard_map/ppermute | solution.py:323
  102.8 4.9 %collective-permute-start.14 = (bf16[16,1024]{1,0:T(8,128)(2,1)S(1)}, bf16[16,1024]{1,0:T(8,128)(2,1)S(1)}, u32[]{:S(2)}, u32[]{:S(2)}) collective-permute-start(bf16[16,1024]{1,0:T(8,128)(2,1)S(1)} %get-tuple-element.41), channel_id=1, source_target_pairs={{0,1},{1,0},{2,3},{3,2},{4,5},{5,4},{6,7},{7,6},{8,9},{9,8},{10,11... | collective-permute-start | bytes 98312 | tf_op jit(solution)/shard_map/ppermute | solution.py:323
  103.1 5.9 %collective-permute-start.15 = (bf16[16,1024]{1,0:T(8,128)(2,1)S(1)}, bf16[16,1024]{1,0:T(8,128)(2,1)S(1)}, u32[]{:S(2)}, u32[]{:S(2)}) collective-permute-start(bf16[16,1024]{1,0:T(8,128)(2,1)S(1)} %get-tuple-element.42), channel_id=1, source_target_pairs={{0,2},{1,3},{2,0},{3,1},{4,6},{5,7},{6,4},{7,5},{8,10},{9,11},{10,... | collective-permute-start | bytes 98312 | tf_op jit(solution)/shard_map/ppermute | solution.py:323
  104.8 14.5 %collective-permute-start.16 = (bf16[16,1024]{1,0:T(8,128)(2,1)S(1)}, bf16[16,1024]{1,0:T(8,128)(2,1)S(1)}, u32[]{:S(2)}, u32[]{:S(2)}) collective-permute-start(bf16[16,1024]{1,0:T(8,128)(2,1)S(1)} %get-tuple-element.43), channel_id=1, source_target_pairs={{0,3},{1,2},{2,1},{3,0},{4,7},{5,6},{6,5},{7,4},{8,11},{9,10},{10,... | collective-permute-start | bytes 98312 | tf_op jit(solution)/shard_map/ppermute | solution.py:323
  105.1 14.3 %collective-permute-start.17 = (bf16[16,1024]{1,0:T(8,128)(2,1)S(1)}, bf16[16,1024]{1,0:T(8,128)(2,1)S(1)}, u32[]{:S(2)}, u32[]{:S(2)}) collective-permute-start(bf16[16,1024]{1,0:T(8,128)(2,1)S(1)} %get-tuple-element.44), channel_id=1, source_target_pairs={{4,0},{5,1},{6,2},{7,3},{8,12},{9,13},{10,14},{11,15},{20,16},{21,... | collective-permute-start | bytes 98312 | tf_op jit(solution)/shard_map/ppermute | solution.py:323
  106.4 13.0 %collective-permute-start.18 = (bf16[16,1024]{1,0:T(8,128)(2,1)S(1)}, bf16[16,1024]{1,0:T(8,128)(2,1)S(1)}, u32[]{:S(2)}, u32[]{:S(2)}) collective-permute-start(bf16[16,1024]{1,0:T(8,128)(2,1)S(1)} %get-tuple-element.45), channel_id=1, source_target_pairs={{4,1},{5,0},{6,3},{7,2},{8,13},{9,12},{10,15},{11,14},{20,17},{21,... | collective-permute-start | bytes 98312 | tf_op jit(solution)/shard_map/ppermute | solution.py:323
  107.7 11.7 %collective-permute-start.19 = (bf16[16,1024]{1,0:T(8,128)(2,1)S(1)}, bf16[16,1024]{1,0:T(8,128)(2,1)S(1)}, u32[]{:S(2)}, u32[]{:S(2)}) collective-permute-start(bf16[16,1024]{1,0:T(8,128)(2,1)S(1)} %get-tuple-element.46), channel_id=1, source_target_pairs={{4,2},{5,3},{6,0},{7,1},{8,14},{9,15},{10,12},{11,13},{20,18},{21,... | collective-permute-start | bytes 98312 | tf_op jit(solution)/shard_map/ppermute | solution.py:323
  109.0 10.4 %collective-permute-start.20 = (bf16[16,1024]{1,0:T(8,128)(2,1)S(1)}, bf16[16,1024]{1,0:T(8,128)(2,1)S(1)}, u32[]{:S(2)}, u32[]{:S(2)}) collective-permute-start(bf16[16,1024]{1,0:T(8,128)(2,1)S(1)} %get-tuple-element.47), channel_id=1, source_target_pairs={{4,3},{5,2},{6,1},{7,0},{8,15},{9,14},{10,13},{11,12},{20,19},{21,... | collective-permute-start | bytes 98312 | tf_op jit(solution)/shard_map/ppermute | solution.py:323
  110.3 1.2 copy-start.8
  111.5 2.2 %copy-start.21 = (bf16[128,16,1024]{2,1,0:T(8,128)(2,1)S(1)}, bf16[128,16,1024]{2,1,0:T(8,128)(2,1)}, u32[]{:S(2)}) copy-start(bf16[128,16,1024]{2,1,0:T(8,128)(2,1)} %cache_ref.1) | copy-start | bytes 12582916
  113.7 5.7 %copy-start.18 = (bf16[128,1024]{1,0:T(8,128)(2,1)S(1)}, bf16[128,1024]{1,0:T(8,128)(2,1)}, u32[]{:S(2)}) copy-start(bf16[128,1024]{1,0:T(8,128)(2,1)} %base_ref.1) | copy-start | bytes 786436
  113.7 5.7 %copy-start.20 = (bf16[48,1024]{1,0:T(8,128)(2,1)S(1)}, bf16[48,1024]{1,0:T(8,128)(2,1)}, u32[]{:S(2)}) copy-start(bf16[48,1024]{1,0:T(8,128)(2,1)} %copy-done.19) | copy-start | bytes 294916

commit v2 on v0

v2 whole, which is shorter than its diff:
```python
import functools

import jax
import jax.numpy as jnp
from jax import lax
from jax.experimental import pallas as pl
from jax.experimental.pallas import tpu as pltpu
from jax.sharding import PartitionSpec as P

QUERY_HEADS = 32
KEY_VALUE_HEADS = 4
HEAD_SIZE = 128
GROUP = QUERY_HEADS // KEY_VALUE_HEADS
SPLIT = KEY_VALUE_HEADS * HEAD_SIZE
PLANE = 4
COLS = 1024
LONG = 20_000_000_000

adapter_scale = 2.0
score_floor = -1e30
score_scale = HEAD_SIZE ** (-0.5)

NT = (((1,), (1,)), ((), ()))


def slot_lookup(request_adapter, adapter_position_map):
    adapter_index = jnp.arange(adapter_position_map.shape[0], dtype=jnp.int32)
    matches = request_adapter[:, None] == adapter_index[None, :]
    return jnp.sum(jnp.where(matches, adapter_position_map[None, :], 0), axis=1)


def rank_in_slot(slot):
    order = jnp.arange(slot.shape[0], dtype=jnp.int32)
    same = slot[:, None] == slot[None, :]
    before = order[None, :] < order[:, None]
    return jnp.sum((same & before).astype(jnp.int32), axis=1)


VMEM = pl.BlockSpec(memory_space=pltpu.VMEM)
SMEM = pl.BlockSpec(memory_space=pltpu.SMEM)
HBM = pl.BlockSpec(memory_space=pltpu.HBM)


def options(name, cost=None):
    chosen = dict(
        name=name, compiler_params=pltpu.CompilerParams(vmem_limit_bytes=12 * 1024 * 1024)
    )
    if cost is not None:
        chosen["cost_estimate"] = pl.CostEstimate(
            flops=1000, bytes_accessed=cost, transcendentals=0
        )
    return chosen


def chunks(width):
    return [slice(c, c + COLS) for c in range(0, width, COLS)]


def cached_kernel(step, length_ref, q_ref, cache_ref, mixed_ref, log_ref):
    total, context = cache_ref.shape[0], cache_ref.shape[1]
    keys = step * context
    owner_q = lax.rem(lax.broadcasted_iota(jnp.int32, (GROUP * step, keys), 0), step)
    column = lax.broadcasted_iota(jnp.int32, (GROUP * step, keys), 1)
    owner_k, position = column // context, lax.rem(column, context)
    lane = lax.broadcasted_iota(jnp.int32, (step, HEAD_SIZE), 1)

    def requests(i, carry):
        rows = pl.ds(pl.multiple_of(i * step, step), step)
        lengths = jnp.concatenate([length_ref[rows, :]] * GROUP, axis=0)
        included = (owner_q == owner_k) & (position < lengths)
        logs = jnp.zeros((step, HEAD_SIZE), jnp.float32)
        for head in range(KEY_VALUE_HEADS):
            first = head * GROUP
            q = jnp.concatenate(
                [
                    q_ref[rows, (first + g) * HEAD_SIZE : (first + g + 1) * HEAD_SIZE]
                    for g in range(GROUP)
                ],
                axis=0,
            )
            k = cache_ref[rows, :, head * HEAD_SIZE : (head + 1) * HEAD_SIZE]
            v = cache_ref[rows, :, SPLIT + head * HEAD_SIZE : SPLIT + (head + 1) * HEAD_SIZE]
            k, v = k.reshape(keys, HEAD_SIZE), v.reshape(keys, HEAD_SIZE)
            score = lax.dot_general(q, k, NT, preferred_element_type=jnp.float32) * score_scale
            score = jnp.where(included, score, score_floor)
            peak = jnp.max(score, axis=1, keepdims=True)
            weight = jnp.exp(score - peak)
            denominator = jnp.sum(weight, axis=1, keepdims=True)
            mixed = jnp.dot(weight.astype(jnp.bfloat16), v, preferred_element_type=jnp.float32)
            mixed = mixed / denominator
            log = peak + jnp.log(denominator)
            for g in range(GROUP):
                part = slice(g * step, (g + 1) * step)
                mixed_ref[rows, (first + g) * HEAD_SIZE : (first + g + 1) * HEAD_SIZE] = mixed[
                    part
                ]
                logs = jnp.where(lane == first + g, log[part], logs)
        log_ref[rows, :] = logs
        return carry

    lax.fori_loop(0, total // step, requests, 0)


def cached_attention(queries, cache, lengths):
    rows = cache.shape[0]
    return pl.pallas_call(
        functools.partial(cached_kernel, 16),
        in_specs=[VMEM] * 3,
        out_specs=[VMEM] * 2,
        out_shape=[
            jax.ShapeDtypeStruct(queries.shape, jnp.float32),
            jax.ShapeDtypeStruct((rows, HEAD_SIZE), jnp.float32),
        ],
        **options("cached", LONG),
    )(lengths.reshape(rows, 1), queries, cache)


def finish_kernel(count, target_ref, base_ref, q_ref, mixed_ref, log_ref, *refs):
    pieces, refs = refs[:count], refs[count:]
    attention_hbm, written_hbm, attention_ref, written_ref, stack_ref, sems, piece_sems = refs
    rows = base_ref.shape[0]
    total = stack_ref.shape[0]
    arrivals, start = [], 0
    for i, piece in enumerate(pieces):
        spot = stack_ref.at[start : start + piece.shape[0]]
        arrivals.append(pltpu.make_async_copy(piece, spot, piece_sems.at[i]))
        arrivals[-1].start()
        start += piece.shape[0]
    spots = lax.broadcasted_iota(jnp.int32, (rows, total), 1)
    place = (spots == target_ref[...]).astype(jnp.float32).astype(jnp.bfloat16)
    for arrival in arrivals:
        arrival.wait()
    delta = jnp.dot(place, stack_ref[...], preferred_element_type=jnp.float32)
    written_ref[...] = (base_ref[...].astype(jnp.float32) + delta).astype(jnp.bfloat16)
    copies = [pltpu.make_async_copy(written_ref, written_hbm, sems.at[KEY_VALUE_HEADS])]
    copies[0].start()
    lane = lax.broadcasted_iota(jnp.int32, (rows, HEAD_SIZE), 1)
    logs = log_ref[...]
    for head in range(KEY_VALUE_HEADS):
        own = slice(head * HEAD_SIZE, (head + 1) * HEAD_SIZE)
        new_key = written_ref[:, own].astype(jnp.float32)
        own = slice(SPLIT + head * HEAD_SIZE, SPLIT + (head + 1) * HEAD_SIZE)
        new_value = written_ref[:, own].astype(jnp.float32)
        for i in range(head * GROUP, (head + 1) * GROUP):
            part = slice(i * HEAD_SIZE, (i + 1) * HEAD_SIZE)
            query = q_ref[:, part].astype(jnp.float32)
            score = jnp.sum(query * new_key, axis=1, keepdims=True) * score_scale
            log = jnp.sum(jnp.where(lane == i, logs, 0.0), axis=1, keepdims=True)
            share = 1.0 / (1.0 + jnp.exp(score - log))
            out = new_value + share * (mixed_ref[:, part] - new_value)
            attention_ref[:, part] = out.astype(jnp.bfloat16)
        wide = slice(head * GROUP * HEAD_SIZE, (head + 1) * GROUP * HEAD_SIZE)
        copies.append(
            pltpu.make_async_copy(
                attention_ref.at[:, wide], attention_hbm.at[:, wide], sems.at[head]
            )
        )
        copies[-1].start()
    for copy in copies:
        copy.wait()


def finish(target, base, queries, mixed, logs, pieces):
    rows = base.shape[0]
    return pl.pallas_call(
        functools.partial(finish_kernel, len(pieces)),
        in_specs=[VMEM] * 5 + [HBM] * len(pieces),
        out_specs=[HBM] * 2,
        out_shape=[
            jax.ShapeDtypeStruct(queries.shape, jnp.bfloat16),
            jax.ShapeDtypeStruct(base.shape, jnp.bfloat16),
        ],
        scratch_shapes=[
            pltpu.VMEM(queries.shape, jnp.bfloat16),
            pltpu.VMEM(base.shape, jnp.bfloat16),
            pltpu.VMEM((sum(piece.shape[0] for piece in pieces), base.shape[1]), jnp.bfloat16),
            pltpu.SemaphoreType.DMA((KEY_VALUE_HEADS + 1,)),
            pltpu.SemaphoreType.DMA((len(pieces),)),
        ],
        **options("finish"),
    )(target.reshape(rows, 1), base, queries, mixed, logs, *pieces)


def pack_kernel(target_ref, hidden_ref, *outs):
    height = outs[0].shape[0]
    spots = height * len(outs)
    spot = lax.broadcasted_iota(jnp.int32, (spots, hidden_ref.shape[0]), 0)
    place = (spot == target_ref[...]).astype(jnp.float32).astype(jnp.bfloat16)
    for part in chunks(hidden_ref.shape[1]):
        packed = jnp.dot(place, hidden_ref[:, part], preferred_element_type=jnp.float32)
        packed = packed.astype(jnp.bfloat16)
        for k, out in enumerate(outs):
            out[:, part] = packed[k * height : (k + 1) * height]


def pack(target, hidden, height, cost):
    rows, width = hidden.shape
    return pl.pallas_call(
        pack_kernel,
        in_specs=[VMEM] * 2,
        out_specs=[VMEM] * PLANE,
        out_shape=[jax.ShapeDtypeStruct((height, width), jnp.bfloat16)] * PLANE,
        **options("pack", cost),
    )(target.reshape(1, rows), hidden)


def expand(total, up):
    shrunk = total.astype(jnp.bfloat16)
    wide = jnp.dot(shrunk, up, preferred_element_type=jnp.float32)
    return (adapter_scale * wide).astype(jnp.bfloat16)


def shrink(row_parts, downs):
    total = None
    for part in chunks(row_parts[0].shape[1]):
        rows = jnp.concatenate([ref[:, part] for ref in row_parts], axis=0)
        down = jnp.concatenate([ref[:, part] for ref in downs], axis=0)
        product = lax.dot_general(rows, down, NT, preferred_element_type=jnp.float32)
        total = product if total is None else total + product
    return total


def both_slots(capacity, total, ups, outs, first=0):
    for slot, up in enumerate(ups):
        rank = up.shape[0]
        lanes = slice(slot * rank, (slot + 1) * rank)
        starts = [(2 * k + slot) * capacity for k in range(PLANE)]
        sums = jnp.concatenate([total[i : i + capacity, lanes] for i in starts], axis=0)
        wide = expand(sums, up)
        start = (first + slot) * capacity
        for k, out in enumerate(outs):
            out[start : start + capacity] = wide[k * capacity : (k + 1) * capacity]


def join_kernel(down_hbm, up_hbm, out_ref, sems):
    width = down_hbm.shape[1]
    down = pltpu.make_async_copy(down_hbm, out_ref.at[:, :width], sems.at[0])
    up = pltpu.make_async_copy(up_hbm, out_ref.at[:, width:], sems.at[1])
    down.start()
    up.start()
    down.wait()
    up.wait()


def join(down, up):
    return pl.pallas_call(
        join_kernel,
        in_specs=[HBM] * 2,
        out_specs=VMEM,
        out_shape=jax.ShapeDtypeStruct((down.shape[0], down.shape[1] + up.shape[1]), down.dtype),
        scratch_shapes=[pltpu.SemaphoreType.DMA((2,))],
        **options("join"),
    )(down, up)


def early_kernel(capacity, *refs):
    rows, (outward, own), out = refs[:PLANE], refs[PLANE : PLANE + 2], refs[PLANE + 2]
    width = rows[0].shape[1]
    total = shrink(rows, [outward, own])
    outs = [out.at[2 * k * capacity : 2 * (k + 1) * capacity] for k in range(PLANE)]
    both_slots(capacity, total, (outward[:, width:], own[:, width:]), outs)


def early(rows, outward, own, capacity):
    out_width = own.shape[1] - rows[0].shape[1]
    return pl.pallas_call(
        functools.partial(early_kernel, capacity),
        in_specs=[VMEM] * (PLANE + 2),
        out_specs=VMEM,
        out_shape=jax.ShapeDtypeStruct((2 * PLANE * capacity, out_width), jnp.bfloat16),
        **options("early"),
    )(*rows, outward, own)


def late_kernel(capacity, where_ref, soon_ref, *refs):
    rows, refs = refs[:PLANE], refs[PLANE:]
    outward, middle, middle2, swapped = refs[:4]
    outs, fars = refs[4 : 4 + PLANE], refs[4 + PLANE :]
    width = rows[0].shape[1]
    for k, out in enumerate(outs):
        out[: 2 * capacity] = soon_ref[2 * k * capacity : 2 * (k + 1) * capacity]

    @pl.when(where_ref[0] == 1)
    def _():
        total = shrink([*rows, swapped], [middle, middle2])
        both_slots(capacity, total, (middle[:, width:], middle2[:, width:]), outs, 2)
        wide = expand(total[2 * PLANE * capacity :, middle.shape[0] :], middle2[:, width:])
        for k, far in enumerate(fars):
            far[...] = wide[k * capacity : (k + 1) * capacity]

    @pl.when(where_ref[0] == 0)
    def _():
        total = shrink(rows, [outward, swapped])
        both_slots(capacity, total, (outward[:, width:], swapped[:, width:]), outs, 2)
        for far in fars:
            far[...] = jnp.zeros(far.shape, far.dtype)


def late(where, soon, rows, weights, capacity):
    out_width = weights[0].shape[1] - rows[0].shape[1]
    near = jax.ShapeDtypeStruct((4 * capacity, out_width), jnp.bfloat16)
    far = jax.ShapeDtypeStruct((capacity, out_width), jnp.bfloat16)
    return pl.pallas_call(
        functools.partial(late_kernel, capacity),
        in_specs=[SMEM] + [VMEM] * (PLANE + 5),
        out_specs=[VMEM] * (2 * PLANE),
        out_shape=[near] * PLANE + [far] * PLANE,
        **options("late"),
    )(where, soon, *rows, *weights)


def choose_kernel(where_ref, weights_ref, *refs):
    rows, out = refs[:PLANE], refs[PLANE]
    capacity, width = out.shape[0] // PLANE, rows[0].shape[1]

    @pl.when(where_ref[0] == 1)
    def _():
        out[...] = weights_ref[...]

    @pl.when(where_ref[0] == 0)
    def _():
        for k, ref in enumerate(rows):
            out[k * capacity : (k + 1) * capacity, :width] = ref[:capacity]
        out[:, width:] = jnp.zeros((out.shape[0], out.shape[1] - width), out.dtype)


def choose(where, weights, rows):
    return pl.pallas_call(
        choose_kernel,
        in_specs=[SMEM] + [VMEM] * (1 + PLANE),
        out_specs=VMEM,
        out_shape=jax.ShapeDtypeStruct(weights.shape, weights.dtype),
        **options("choose"),
    )(where, weights, *rows)


def by_planes(hidden, slot, down, up, capacity, meanwhile):
    devices = lax.axis_size("adapter")
    me = lax.axis_index("adapter")
    plane, place = me // PLANE, me % PLANE
    inner = (plane == 1) | (plane == 2)
    where = inner.astype(jnp.int32).reshape(1)
    all_devices = range(devices)
    middles = [i for i in all_devices if i // PLANE in (1, 2)]
    across = [
        [(i, (i // PLANE) * PLANE + ((i % PLANE) ^ k)) for i in all_devices] for k in range(PLANE)
    ]
    to_outward = [(i, i ^ PLANE) for i in all_devices]
    to_middle = [(i, i ^ (3 * PLANE)) for i in middles]
    send = lambda a, pairs: lax.ppermute(a, "adapter", pairs)
    exchange = lambda parts: [parts[0]] + [send(parts[k], across[k]) for k in range(1, PLANE)]

    plane_of, place_of = slot // PLANE, slot % PLANE
    distance = jnp.abs(plane_of - plane)
    at_end = (plane_of == 0) | (plane_of == 3)
    kind = jnp.where(
        distance == 0,
        1,
        jnp.where(distance == 2, 3, jnp.where((distance == 3) | at_end, 0, 2)),
    )
    rank = rank_in_slot(slot)
    k = place_of ^ place
    spot = (k * 2 + kind % 2) * capacity + rank
    spots = 2 * PLANE * capacity
    back = jnp.where(
        (kind == 0) & ~inner,
        2 * spots + k * capacity + rank,
        (k * 4 + kind) * capacity + rank,
    )

    weights = join(down, up)
    outward, middle = send(weights, to_outward), send(weights, to_middle)
    near = exchange(pack(jnp.where(kind < 2, spot, -1), hidden, 2 * capacity, None))
    away = pack(jnp.where(kind < 2, -1, spot), hidden, 2 * capacity, LONG)
    near, away, outward, middle = lax.optimization_barrier((near, away, outward, middle))
    middle2 = send(outward, to_middle)
    swapped = send(choose(where, middle, near), to_outward)
    away = exchange(away)

    done = meanwhile()
    near, done = lax.optimization_barrier((near, done))
    soon = early(near, outward, weights, capacity)
    where, done, soon = lax.optimization_barrier((where, done, soon))
    outs = late(where, soon, away, [outward, middle, middle2, swapped], capacity)
    last = exchange(outs[:PLANE])
    far = [send(outs[PLANE + k], [(i, (i ^ PLANE) ^ k) for i in middles]) for k in range(PLANE)]
    return back, [*last, *far], done


def by_rows(hidden, slot, down, up, capacity, meanwhile):
    devices = lax.axis_size("adapter")
    target = slot * capacity + rank_in_slot(slot)
    spots = jnp.arange(devices * capacity, dtype=jnp.int32)
    placing = (target[None, :] == spots[:, None]).astype(jnp.bfloat16)
    outgoing = jnp.dot(placing, hidden, preferred_element_type=jnp.float32).astype(jnp.bfloat16)
    outgoing = outgoing.reshape(devices, capacity, hidden.shape[1])
    incoming = lax.all_to_all(outgoing, "adapter", split_axis=0, concat_axis=0, tiled=True)
    rows = incoming.reshape(-1, hidden.shape[1])
    shrunk = lax.dot_general(rows, down, NT, preferred_element_type=jnp.float32)
    wide = expand(shrunk, up)
    returned = lax.all_to_all(
        wide.reshape(devices, capacity, -1), "adapter", split_axis=0, concat_axis=0, tiled=True
    )
    return target, [returned.reshape(devices * capacity, -1)], meanwhile()


def on_device(
    hidden,
    queries,
    base_key_value,
    key_value_cache,
    lengths,
    request_adapter_index,
    adapter_position_map,
    adapter_down_weight,
    adapter_up_weight,
):
    devices = lax.axis_size("adapter")
    capacity = max(2, 2 * hidden.shape[0] // devices)
    slot = slot_lookup(request_adapter_index[:, 0], adapter_position_map)
    deliver = by_planes if devices == 4 * PLANE else by_rows
    meanwhile = lambda: cached_attention(queries, key_value_cache, lengths)
    target, pieces, (mixed, logs) = deliver(
        hidden, slot, adapter_down_weight[0], adapter_up_weight[0], capacity, meanwhile
    )
    return finish(target, base_key_value, queries, mixed, logs, pieces)


def solution(mesh):
    rows = P(("groups", "adapter"), None)
    deep = P(("groups", "adapter"), None, None)
    placed = (
        rows,
        rows,
        rows,
        deep,
        P(("groups", "adapter")),
        rows,
        P("groups"),
        deep,
        deep,
    )
    return jax.shard_map(
        on_device, mesh=mesh, in_specs=placed, out_specs=(rows, rows), check_vma=False
    )
```

time: 158 us -> 94.4 us (0.60)
  blocking collectives: 99.7 us -> 0 us
  waiting for transfers between devices: 0.01 us -> 39.6 us
  Pallas kernels: 0 us -> 23.5 us
  local copies, waits for them, and re-layouts: 30.1 us -> 8.93 us
  matrix products: 17.4 us -> 0 us
  starting transfers between devices: 5.35 us -> 20.6 us
  other arithmetic: 3.82 us -> 0.4 us
    all_to_all x1 -> x0, blocking collectives: 99.7 us -> none  [on_device(): lax.all_to_all(outgoing, 'adapter', split_axis=0, concat_axis=0, tiled=True)]
    ppermute x0 -> x17, waiting for transfers between devices: none -> 39.6 us  [by_planes(): send = lambda a, pairs: lax.ppermute(a, 'adapter', pairs)]
    pallas_call x0 -> x8, Pallas kernels: none -> 23.5 us  [the longest x1 5.62 us: cached_attention(): pl.pallas_call(functools.partial(cached_kernel, 16), in_specs=[VMEM] * 3,...]
    ppermute x0 -> x17, starting transfers between devices: none -> 20.6 us  [by_planes(): send = lambda a, pairs: lax.ppermute(a, 'adapter', pairs)]
    dot_general x6 -> x0, matrix products: 17.4 us -> none  [the longest x1 4.93 us: on_device(): jnp.dot(reduced_output, adapter_up_weight[0], preferred_element_type=jnp....]
    reshape x3 -> x1, local copies, waits for them, and re-layouts: 9.98 us -> 0.11 us  [cached_attention(): lengths.reshape(rows, 1)]
    all_to_all x1 -> x0, starting transfers between devices: 5.35 us -> none  [on_device(): lax.all_to_all(expanded_output.reshape(devices, item_count, expanded_outp...]
    slice x1 -> x0, local copies, waits for them, and re-layouts: 4.6 us -> none  [attend(): key_value_cache[:, :, :key_value_split]]
  transfers between devices with their start and end apart: 1 -> 17, of which waited for: 0 -> 7; matrix products, arithmetic and copies ran while one was open for 19% -> 1% of each run, Pallas kernels for 0% -> 14%
where the time goes in v2:
time: 94.4 us; the launch traced here: 94 us
  waiting for transfers between devices  39.6 us (42%)
  Pallas kernels  23.5 us (25%)
  starting transfers between devices  20.6 us (22%)
  local copies, waits for them, and re-layouts  8.93 us (9%)
    ppermute x17, waiting for transfers between devices, by_planes(): send = lambda a, pairs: lax.ppermute(a, 'adapter', pairs)  39.6 us
    ppermute x17, starting transfers between devices, by_planes(): send = lambda a, pairs: lax.ppermute(a, 'adapter', pairs)  20.6 us
    unnamed x32, local copies, waits for them, and re-layouts  8.6 us
    pallas_call x1, Pallas kernels, cached_attention(): pl.pallas_call(functools.partial(cached_kernel, 16), in_specs=[VMEM] * 3,...  5.62 us
    pallas_call x1, Pallas kernels, early(): pl.pallas_call(functools.partial(early_kernel, capacity), in_specs=[VMEM]...  3.87 us
    pallas_call x2, Pallas kernels, pack(): pl.pallas_call(pack_kernel, in_specs=[VMEM] * 2, out_specs=[VMEM] * PLANE...  3.68 us
    pallas_call x1, Pallas kernels, late(): pl.pallas_call(functools.partial(late_kernel, capacity), in_specs=[SMEM]...  3.51 us
    pallas_call x1, Pallas kernels, finish(): pl.pallas_call(functools.partial(finish_kernel, len(pieces)), in_specs=[V...  3.06 us
  transfers between devices with their start and end apart: 17, of which 7 were waited for; matrix products, arithmetic and copies ran while one was open for 1% of the time, Pallas kernels for 14%

profile of v2, /device:TPU:0, one launch (start us, length us, event | category | flops | bytes accessed | tf_op | source)
XLA Modules:
  0.0 94.0 jit_solution(17037634942480882892)
XLA Ops:
  0.6 0.0 copy-start.8
  0.6 1.2 %copy-done.8 = bf16[1,64,8192]{2,1,0:T(8,128)(2,1)S(1)} copy-done((bf16[1,64,8192]{2,1,0:T(8,128)(2,1)S(1)}, bf16[1,64,8192]{2,1,0:T(8,128)(2,1)}, u32[]{:S(2)}) %copy-start.8) | copy-done | bytes 1048600
  1.9 0.9 copy-done.12
  2.8 1.1 %join.1.refs_5_ = bf16[64,9216]{1,0:T(8,128)(2,1)} custom-call(bf16[64,8192]{1,0:T(8,128)(2,1)S(1)} %bitcast.40, bf16[64,1024]{1,0:T(8,128)(2,1)S(1)} %bitcast.41), custom_call_target="tpu_custom_call" | custom-call | tf_op jit(solution)/shard_map/join/pallas_call | solution.py:246
  3.9 3.1 %collective-permute-start.3 = (bf16[64,9216]{1,0:T(8,128)(2,1)}, bf16[64,9216]{1,0:T(8,128)(2,1)}, u32[]{:S(2)}, u32[]{:S(2)}) collective-permute-start(bf16[64,9216]{1,0:T(8,128)(2,1)} %join.1.refs_5_), channel_id=1, source_target_pairs={{0,4},{1,5},{2,6},{3,7},{4,0},{5,1},{6,2},{7,3},{8,12},{9,13},{10,... | collective-permute-start | bytes 3538952 | tf_op jit(solution)/shard_map/ppermute | solution.py:350
  7.0 0.7 collective-permute-start.4
  7.8 0.0 copy-done.14
  7.8 0.1 select_reduce_fusion
  7.9 0.2 convert_reduce_fusion
  8.1 1.8 %pack.2 = (bf16[32,8192]{1,0:T(8,128)(2,1)S(1)}, bf16[32,8192]{1,0:T(8,128)(2,1)}, bf16[32,8192]{1,0:T(8,128)(2,1)}, bf16[32,8192]{1,0:T(8,128)(2,1)}) custom-call(s32[1,128]{1,0:T(1,128)S(1)} %get-tuple-element.79.target_ref, bf16[128,8192]{1,0:T(8,128)(2,1)S(1)} %copy-done), custom_call_target="tpu_custom_call" | custom-call | tf_op jit(solution)/shard_map/pack/pallas_call | solution.py:198
  9.9 0.8 copy-done.3
  10.7 0.0 collective-permute-start
  10.7 1.5 %collective-permute-start.1 = (bf16[32,8192]{1,0:T(8,128)(2,1)}, bf16[32,8192]{1,0:T(8,128)(2,1)}, u32[]{:S(2)}, u32[]{:S(2)}) collective-permute-start(bf16[32,8192]{1,0:T(8,128)(2,1)} %get-tuple-element.42), channel_id=1, source_target_pairs={{0,2},{1,3},{2,0},{3,1},{4,6},{5,7},{6,4},{7,5},{8,10},{9,11},{10,... | collective-permute-start | bytes 1572872 | tf_op jit(solution)/shard_map/ppermute | solution.py:350
  12.2 0.4 collective-permute-start.2
  12.6 1.8 %pack.3 = (bf16[32,8192]{1,0:T(8,128)(2,1)S(1)}, bf16[32,8192]{1,0:T(8,128)(2,1)}, bf16[32,8192]{1,0:T(8,128)(2,1)}, bf16[32,8192]{1,0:T(8,128)(2,1)}) custom-call(s32[1,128]{1,0:T(1,128)S(1)} %get-tuple-element.78.target_ref, bf16[128,8192]{1,0:T(8,128)(2,1)S(1)} %copy-done), custom_call_target="tpu_custom_call" | custom-call | flops 1000 | bytes 20000000000 | tf_op jit(solution)/shard_map/pack/pallas_call | solution.py:198
  14.4 0.8 copy-done.9
  15.3 0.0 collective-permute-done.refs_1_
  15.3 10.5 %collective-permute-done.1.refs_2_ = bf16[32,8192]{1,0:T(8,128)(2,1)} collective-permute-done((bf16[32,8192]{1,0:T(8,128)(2,1)}, bf16[32,8192]{1,0:T(8,128)(2,1)}, u32[]{:S(2)}, u32[]{:S(2)}) %collective-permute-start.1) | collective-permute-done | bytes 524320 | tf_op jit(solution)/shard_map/ppermute | solution.py:350
  25.8 10.5 %collective-permute-done.2.refs_3_ = bf16[32,8192]{1,0:T(8,128)(2,1)} collective-permute-done((bf16[32,8192]{1,0:T(8,128)(2,1)}, bf16[32,8192]{1,0:T(8,128)(2,1)}, u32[]{:S(2)}, u32[]{:S(2)}) %collective-permute-start.2) | collective-permute-done | bytes 524320 | tf_op jit(solution)/shard_map/ppermute | solution.py:350
  36.2 0.0 collective-permute-done.3.refs_4_
  36.2 0.0 collective-permute-done.4.weights_ref.refs_5_
  36.2 1.0 %copy-done.4 = bf16[32,8192]{1,0:T(8,128)(2,1)S(1)} copy-done((bf16[32,8192]{1,0:T(8,128)(2,1)S(1)}, bf16[32,8192]{1,0:T(8,128)(2,1)}, u32[]{:S(2)}) %copy-start.4) | copy-done | bytes 524312
  37.3 2.6 %choose.1 = bf16[64,9216]{1,0:T(8,128)(2,1)} custom-call(s32[1]{0:T(128)} %bitcast.3.where_ref, bf16[64,9216]{1,0:T(8,128)(2,1)S(1)} %collective-permute-done.4.weights_ref.refs_5_, bf16[32,8192]{1,0:T(8,128)(2,1)S(1)} %copy-done.4, bf16[32,8192]{1,0:T(8,128)(2,1)} %collective-permute-done.refs_1_, bf16[32,8192]{1,0:T(8,128)(2,1)} %collective-permute-done.1.refs_2_, ...), custom_call_target="tpu_custom_call" | custom-call | tf_op jit(solution)/shard_map/choose/pallas_call | solution.py:328
  39.9 4.3 %collective-permute-start.9 = (bf16[64,9216]{1,0:T(8,128)(2,1)}, bf16[64,9216]{1,0:T(8,128)(2,1)}, u32[]{:S(2)}, u32[]{:S(2)}) collective-permute-start(bf16[64,9216]{1,0:T(8,128)(2,1)} %choose.1), channel_id=1, source_target_pairs={{0,4},{1,5},{2,6},{3,7},{4,0},{5,1},{6,2},{7,3},{8,12},{9,13},{10,... | collective-permute-start | bytes 3538952 | tf_op jit(solution)/shard_map/ppermute | solution.py:350
  44.2 1.7 %collective-permute-start.8 = (bf16[64,9216]{1,0:T(8,128)(2,1)}, bf16[64,9216]{1,0:T(8,128)(2,1)}, u32[]{:S(2)}, u32[]{:S(2)}) collective-permute-start(bf16[64,9216]{1,0:T(8,128)(2,1)} %collective-permute-done.3.refs_4_), channel_id=1, source_target_pairs={{4,8},{5,9},{6,10},{7,11},{8,4},{9,5},{10,6},{11,7},{20,24},{21,25... | collective-permute-start | bytes 3538952 | tf_op jit(solution)/shard_map/ppermute | solution.py:350
  45.9 0.0 collective-permute-start.5
  45.9 1.5 %collective-permute-start.6 = (bf16[32,8192]{1,0:T(8,128)(2,1)}, bf16[32,8192]{1,0:T(8,128)(2,1)}, u32[]{:S(2)}, u32[]{:S(2)}) collective-permute-start(bf16[32,8192]{1,0:T(8,128)(2,1)} %get-tuple-element.67), channel_id=1, source_target_pairs={{0,2},{1,3},{2,0},{3,1},{4,6},{5,7},{6,4},{7,5},{8,10},{9,11},{10,... | collective-permute-start | bytes 1572872 | tf_op jit(solution)/shard_map/ppermute | solution.py:350
  47.4 0.4 collective-permute-start.7
  47.7 0.0 copy-done.13
  47.7 0.1 copy.24.length_ref
  47.9 0.0 copy-start.1
  47.9 2.2 %copy-done.1 = bf16[128,16,1024]{2,1,0:T(8,128)(2,1)S(1)} copy-done((bf16[128,16,1024]{2,1,0:T(8,128)(2,1)S(1)}, bf16[128,16,1024]{2,1,0:T(8,128)(2,1)}, u32[]{:S(2)}) %copy-start.1) | copy-done | bytes 4194328
  50.1 5.6 %cached.1 = (f32[128,4096]{1,0:T(8,128)S(1)}, f32[128,128]{1,0:T(8,128)S(1)}) custom-call(s32[128,1]{1,0:T(8,128)S(1)} %copy.24.length_ref, bf16[128,4096]{1,0:T(8,128)(2,1)S(1)} %copy-done.2, bf16[128,16,1024]{2,1,0:T(8,128)(2,1)S(1)} %copy-done.1), custom_call_target="tpu_custom_call" | custom-call | flops 1000 | bytes 20000000000 | tf_op jit(solution)/shard_map/cached/pallas_call | solution.py:106
  55.7 0.0 copy-start.6
  55.7 0.0 copy-done.5
  55.7 0.0 copy-start.10
  55.7 3.9 %early.1.soon_ref = bf16[128,1024]{1,0:T(8,128)(2,1)S(1)} custom-call(bf16[32,8192]{1,0:T(8,128)(2,1)S(1)} %copy-done.5, bf16[32,8192]{1,0:T(8,128)(2,1)} %collective-permute-done.refs_1_, bf16[32,8192]{1,0:T(8,128)(2,1)} %collective-permute-done.1.refs_2_, bf16[32,8192]{1,0:T(8,128)(2,1)} %collective-permute-done.2.refs_3_, ...), custom_call_target="tpu_custom_call" | custom-call | tf_op jit(solution)/shard_map/early/pallas_call | solution.py:266
  59.6 0.0 copy-done.6
  59.6 0.0 copy-start.11
  59.6 0.0 collective-permute-done.5.refs_1_
  59.6 1.3 %collective-permute-done.6.refs_2_ = bf16[32,8192]{1,0:T(8,128)(2,1)} collective-permute-done((bf16[32,8192]{1,0:T(8,128)(2,1)}, bf16[32,8192]{1,0:T(8,128)(2,1)}, u32[]{:S(2)}, u32[]{:S(2)}) %collective-permute-start.6) | collective-permute-done | bytes 524320 | tf_op jit(solution)/shard_map/ppermute | solution.py:350
  60.9 10.5 %collective-permute-done.7.refs_3_ = bf16[32,8192]{1,0:T(8,128)(2,1)} collective-permute-done((bf16[32,8192]{1,0:T(8,128)(2,1)}, bf16[32,8192]{1,0:T(8,128)(2,1)}, u32[]{:S(2)}, u32[]{:S(2)}) %collective-permute-start.7) | collective-permute-done | bytes 524320 | tf_op jit(solution)/shard_map/ppermute | solution.py:350
  71.4 0.0 collective-permute-done.9.refs_7_
  71.4 0.0 collective-permute-done.8.refs_6_
  71.4 3.5 %late.1 = (bf16[64,1024]{1,0:T(8,128)(2,1)S(1)}, bf16[64,1024]{1,0:T(8,128)(2,1)S(1)}, bf16[64,1024]{1,0:T(8,128)(2,1)S(1)}, bf16[64,1024]{1,0:T(8,128)(2,1)S(1)...) custom-call(s32[1]{0:T(128)} %bitcast.3.where_ref, ...), custom_call_target="tpu_custom_call" | custom-call | tf_op jit(solution)/shard_map/late/pallas_call | solution.py:303
  74.9 1.3 %collective-permute-start.13 = (bf16[16,1024]{1,0:T(8,128)(2,1)S(1)}, bf16[16,1024]{1,0:T(8,128)(2,1)S(1)}, u32[]{:S(2)}, u32[]{:S(2)}) collective-permute-start(bf16[16,1024]{1,0:T(8,128)(2,1)S(1)} %get-tuple-element.74), channel_id=1, source_target_pairs={{4,0},{5,1},{6,2},{7,3},{8,12},{9,13},{10,14},{11,15},{20,16},{21,... | collective-permute-start | bytes 98312 | tf_op jit(solution)/shard_map/ppermute | solution.py:350
  76.2 1.3 %collective-permute-start.14 = (bf16[16,1024]{1,0:T(8,128)(2,1)S(1)}, bf16[16,1024]{1,0:T(8,128)(2,1)S(1)}, u32[]{:S(2)}, u32[]{:S(2)}) collective-permute-start(bf16[16,1024]{1,0:T(8,128)(2,1)S(1)} %get-tuple-element.75), channel_id=1, source_target_pairs={{4,1},{5,0},{6,3},{7,2},{8,13},{9,12},{10,15},{11,14},{20,17},{21,... | collective-permute-start | bytes 98312 | tf_op jit(solution)/shard_map/ppermute | solution.py:350
  77.5 0.1 copy.22
  77.6 0.1 copy.18
  77.7 0.3 collective-permute-start.10
  78.0 1.5 %collective-permute-start.11 = (bf16[64,1024]{1,0:T(8,128)(2,1)S(1)}, bf16[64,1024]{1,0:T(8,128)(2,1)S(1)}, u32[]{:S(2)}, u32[]{:S(2)}) collective-permute-start(bf16[64,1024]{1,0:T(8,128)(2,1)S(1)} %get-tuple-element.72), channel_id=1, source_target_pairs={{0,2},{1,3},{2,0},{3,1},{4,6},{5,7},{6,4},{7,5},{8,10},{9,11},{10,... | collective-permute-start | bytes 393224 | tf_op jit(solution)/shard_map/ppermute | solution.py:350
  79.5 0.2 collective-permute-start.12
  79.7 2.2 %collective-permute-done.13.refs_4_ = bf16[16,1024]{1,0:T(8,128)(2,1)S(1)} collective-permute-done((bf16[16,1024]{1,0:T(8,128)(2,1)S(1)}, bf16[16,1024]{1,0:T(8,128)(2,1)S(1)}, u32[]{:S(2)}, u32[]{:S(2)}) %collective-permute-start.13) | collective-permute-done | bytes 32800 | tf_op jit(solution)/shard_map/ppermute | solution.py:350
  81.8 1.3 %collective-permute-start.15 = (bf16[16,1024]{1,0:T(8,128)(2,1)S(1)}, bf16[16,1024]{1,0:T(8,128)(2,1)S(1)}, u32[]{:S(2)}, u32[]{:S(2)}) collective-permute-start(bf16[16,1024]{1,0:T(8,128)(2,1)S(1)} %get-tuple-element.76), channel_id=1, source_target_pairs={{4,2},{5,3},{6,0},{7,1},{8,14},{9,15},{10,12},{11,13},{20,18},{21,... | collective-permute-start | bytes 98312 | tf_op jit(solution)/shard_map/ppermute | solution.py:350
  83.1 0.0 collective-permute-done.14.refs_5_
  83.1 1.3 %collective-permute-start.16 = (bf16[16,1024]{1,0:T(8,128)(2,1)S(1)}, bf16[16,1024]{1,0:T(8,128)(2,1)S(1)}, u32[]{:S(2)}, u32[]{:S(2)}) collective-permute-start(bf16[16,1024]{1,0:T(8,128)(2,1)S(1)} %get-tuple-element.77), channel_id=1, source_target_pairs={{4,3},{5,2},{6,1},{7,0},{8,15},{9,14},{10,13},{11,12},{20,19},{21,... | collective-permute-start | bytes 98312 | tf_op jit(solution)/shard_map/ppermute | solution.py:350
  84.4 0.1 add_select_fusion.2.target_ref
  84.6 4.0 %collective-permute-done.15.refs_6_ = bf16[16,1024]{1,0:T(8,128)(2,1)S(1)} collective-permute-done((bf16[16,1024]{1,0:T(8,128)(2,1)S(1)}, bf16[16,1024]{1,0:T(8,128)(2,1)S(1)}, u32[]{:S(2)}, u32[]{:S(2)}) %collective-permute-start.15) | collective-permute-done | bytes 32800 | tf_op jit(solution)/shard_map/ppermute | solution.py:350
  88.5 0.7 collective-permute-done.16.refs_7_
  89.3 0.0 collective-permute-done.10.refs_1_
  89.3 0.0 collective-permute-done.11.refs_2_
  89.3 0.0 collective-permute-done.12.refs_3_
  89.3 1.6 %copy-done.7 = f32[128,4096]{1,0:T(8,128)S(1)} copy-done((f32[128,4096]{1,0:T(8,128)S(1)}, f32[128,4096]{1,0:T(8,128)}, u32[]{:S(2)}) %copy-start.7) | copy-done | bytes 2097176
  90.9 3.1 %finish.1 = (bf16[128,4096]{1,0:T(8,128)(2,1)}, bf16[128,1024]{1,0:T(8,128)(2,1)}) custom-call(s32[128,1]{1,0:T(8,128)S(1)} %add_select_fusion.2.target_ref, bf16[128,1024]{1,0:T(8,128)(2,1)S(1)} %copy-done.11, bf16[128,4096]{1,0:T(8,128)(2,1)S(1)} %copy-done.2, f32[128,4096]{1,0:T(8,128)S(1)} %copy-done.7, f32[128,128]{1,0:T(8,128)S(1)} %get-tuple-element.62.log_ref, ...), custom_call_target="tpu_custom_call" | custom-call | tf_op jit(solution)/shard_map/finish/pallas_call | solution.py:165
  (17 shorter events, 0.1 us)
Async XLA Ops:
  0.6 1.2 %copy-start.8 = (bf16[1,64,8192]{2,1,0:T(8,128)(2,1)S(1)}, bf16[1,64,8192]{2,1,0:T(8,128)(2,1)}, u32[]{:S(2)}) copy-start(bf16[1,64,8192]{2,1,0:T(8,128)(2,1)} %param.16) | copy-start | bytes 3145732
  1.9 0.9 copy-start.12
  2.8 5.0 %copy-start.14 = (s32[16]{0:T(128)S(1)}, s32[16]{0:T(128)}, u32[]{:S(2)}) copy-start(s32[16]{0:T(128)} %param.15) | copy-start | bytes 196
  2.8 5.0 %copy-start.15 = (s32[128,1]{0,1:T(1,128)S(1)}, s32[128,1]{0,1:T(1,128)}, u32[]{:S(2)}) copy-start(s32[128,1]{0,1:T(1,128)} %param.14) | copy-start | bytes 1540
  2.8 5.3 %copy-start = (bf16[128,8192]{1,0:T(8,128)(2,1)S(1)}, bf16[128,8192]{1,0:T(8,128)(2,1)}, u32[]{:S(2)}) copy-start(bf16[128,8192]{1,0:T(8,128)(2,1)} %hidden_ref.3) | copy-start | bytes 6291460
  3.9 32.3 %collective-permute-start.3 = (bf16[64,9216]{1,0:T(8,128)(2,1)}, bf16[64,9216]{1,0:T(8,128)(2,1)}, u32[]{:S(2)}, u32[]{:S(2)}) collective-permute-start(bf16[64,9216]{1,0:T(8,128)(2,1)} %join.1.refs_5_), channel_id=1, source_target_pairs={{0,4},{1,5},{2,6},{3,7},{4,0},{5,1},{6,2},{7,3},{8,12},{9,13},{10,... | collective-permute-start | bytes 3538952 | tf_op jit(solution)/shard_map/ppermute | solution.py:350
  7.0 29.2 %collective-permute-start.4 = (bf16[64,9216]{1,0:T(8,128)(2,1)}, bf16[64,9216]{1,0:T(8,128)(2,1)S(1)}, u32[]{:S(2)}, u32[]{:S(2)}) collective-permute-start(bf16[64,9216]{1,0:T(8,128)(2,1)} %join.1.refs_5_), channel_id=1, source_target_pairs={{4,8},{5,9},{6,10},{7,11},{8,4},{9,5},{10,6},{11,7},{20,24},{21,25... | collective-permute-start | bytes 3538952 | tf_op jit(solution)/shard_map/ppermute | solution.py:350
  9.9 0.8 copy-start.3
  10.7 4.5 %collective-permute-start = (bf16[32,8192]{1,0:T(8,128)(2,1)}, bf16[32,8192]{1,0:T(8,128)(2,1)}, u32[]{:S(2)}, u32[]{:S(2)}) collective-permute-start(bf16[32,8192]{1,0:T(8,128)(2,1)} %get-tuple-element.41), channel_id=1, source_target_pairs={{0,1},{1,0},{2,3},{3,2},{4,5},{5,4},{6,7},{7,6},{8,9},{9,8},{10,11... | collective-permute-start | bytes 1572872 | tf_op jit(solution)/shard_map/ppermute | solution.py:350
  10.7 15.0 %collective-permute-start.1 = (bf16[32,8192]{1,0:T(8,128)(2,1)}, bf16[32,8192]{1,0:T(8,128)(2,1)}, u32[]{:S(2)}, u32[]{:S(2)}) collective-permute-start(bf16[32,8192]{1,0:T(8,128)(2,1)} %get-tuple-element.42), channel_id=1, source_target_pairs={{0,2},{1,3},{2,0},{3,1},{4,6},{5,7},{6,4},{7,5},{8,10},{9,11},{10,... | collective-permute-start | bytes 1572872 | tf_op jit(solution)/shard_map/ppermute | solution.py:350
  12.2 24.0 %collective-permute-start.2 = (bf16[32,8192]{1,0:T(8,128)(2,1)}, bf16[32,8192]{1,0:T(8,128)(2,1)}, u32[]{:S(2)}, u32[]{:S(2)}) collective-permute-start(bf16[32,8192]{1,0:T(8,128)(2,1)} %get-tuple-element.43), channel_id=1, source_target_pairs={{0,3},{1,2},{2,1},{3,0},{4,7},{5,6},{6,5},{7,4},{8,11},{9,10},{10,... | collective-permute-start | bytes 1572872 | tf_op jit(solution)/shard_map/ppermute | solution.py:350
  14.4 0.8 copy-start.9
  36.2 1.0 %copy-start.4 = (bf16[32,8192]{1,0:T(8,128)(2,1)S(1)}, bf16[32,8192]{1,0:T(8,128)(2,1)}, u32[]{:S(2)}) copy-start(bf16[32,8192]{1,0:T(8,128)(2,1)} %copy-done.3) | copy-start | bytes 1572868
  37.3 10.5 %copy-start.13 = (s32[128]{0:T(128)S(1)}, s32[128]{0:T(128)}, u32[]{:S(2)}) copy-start(s32[128]{0:T(128)} %param.13) | copy-start | bytes 1540
  37.3 10.6 %copy-start.2 = (bf16[128,4096]{1,0:T(8,128)(2,1)S(1)}, bf16[128,4096]{1,0:T(8,128)(2,1)}, u32[]{:S(2)}) copy-start(bf16[128,4096]{1,0:T(8,128)(2,1)} %q_ref.3) | copy-start | bytes 3145732
  39.9 31.5 %collective-permute-start.9 = (bf16[64,9216]{1,0:T(8,128)(2,1)}, bf16[64,9216]{1,0:T(8,128)(2,1)}, u32[]{:S(2)}, u32[]{:S(2)}) collective-permute-start(bf16[64,9216]{1,0:T(8,128)(2,1)} %choose.1), channel_id=1, source_target_pairs={{0,4},{1,5},{2,6},{3,7},{4,0},{5,1},{6,2},{7,3},{8,12},{9,13},{10,... | collective-permute-start | bytes 3538952 | tf_op jit(solution)/shard_map/ppermute | solution.py:350
  44.2 27.2 %collective-permute-start.8 = (bf16[64,9216]{1,0:T(8,128)(2,1)}, bf16[64,9216]{1,0:T(8,128)(2,1)}, u32[]{:S(2)}, u32[]{:S(2)}) collective-permute-start(bf16[64,9216]{1,0:T(8,128)(2,1)} %collective-permute-done.3.refs_4_), channel_id=1, source_target_pairs={{4,8},{5,9},{6,10},{7,11},{8,4},{9,5},{10,6},{11,7},{20,24},{21,25... | collective-permute-start | bytes 3538952 | tf_op jit(solution)/shard_map/ppermute | solution.py:350
  45.9 13.7 %collective-permute-start.5 = (bf16[32,8192]{1,0:T(8,128)(2,1)}, bf16[32,8192]{1,0:T(8,128)(2,1)}, u32[]{:S(2)}, u32[]{:S(2)}) collective-permute-start(bf16[32,8192]{1,0:T(8,128)(2,1)} %get-tuple-element.66), channel_id=1, source_target_pairs={{0,1},{1,0},{2,3},{3,2},{4,5},{5,4},{6,7},{7,6},{8,9},{9,8},{10,11... | collective-permute-start | bytes 1572872 | tf_op jit(solution)/shard_map/ppermute | solution.py:350
  45.9 15.0 %collective-permute-start.6 = (bf16[32,8192]{1,0:T(8,128)(2,1)}, bf16[32,8192]{1,0:T(8,128)(2,1)}, u32[]{:S(2)}, u32[]{:S(2)}) collective-permute-start(bf16[32,8192]{1,0:T(8,128)(2,1)} %get-tuple-element.67), channel_id=1, source_target_pairs={{0,2},{1,3},{2,0},{3,1},{4,6},{5,7},{6,4},{7,5},{8,10},{9,11},{10,... | collective-permute-start | bytes 1572872 | tf_op jit(solution)/shard_map/ppermute | solution.py:350
  47.4 24.0 %collective-permute-start.7 = (bf16[32,8192]{1,0:T(8,128)(2,1)}, bf16[32,8192]{1,0:T(8,128)(2,1)}, u32[]{:S(2)}, u32[]{:S(2)}) collective-permute-start(bf16[32,8192]{1,0:T(8,128)(2,1)} %get-tuple-element.68), channel_id=1, source_target_pairs={{0,3},{1,2},{2,1},{3,0},{4,7},{5,6},{6,5},{7,4},{8,11},{9,10},{10,... | collective-permute-start | bytes 1572872 | tf_op jit(solution)/shard_map/ppermute | solution.py:350
  47.9 2.2 %copy-start.1 = (bf16[128,16,1024]{2,1,0:T(8,128)(2,1)S(1)}, bf16[128,16,1024]{2,1,0:T(8,128)(2,1)}, u32[]{:S(2)}) copy-start(bf16[128,16,1024]{2,1,0:T(8,128)(2,1)} %cache_ref.1) | copy-start | bytes 12582916
  50.1 5.6 %copy-start.5 = (bf16[32,8192]{1,0:T(8,128)(2,1)S(1)}, bf16[32,8192]{1,0:T(8,128)(2,1)}, u32[]{:S(2)}) copy-start(bf16[32,8192]{1,0:T(8,128)(2,1)} %copy-done.3) | copy-start | bytes 1572868
  55.7 3.9 %copy-start.6 = (f32[128,4096]{1,0:T(8,128)}, f32[128,4096]{1,0:T(8,128)S(1)}, u32[]{:S(2)}) copy-start(f32[128,4096]{1,0:T(8,128)S(1)} %get-tuple-element.61.mixed_ref) | copy-start | bytes 6291460
  55.7 15.7 %copy-start.10 = (bf16[32,8192]{1,0:T(8,128)(2,1)S(1)}, bf16[32,8192]{1,0:T(8,128)(2,1)}, u32[]{:S(2)}) copy-start(bf16[32,8192]{1,0:T(8,128)(2,1)} %copy-done.9) | copy-start | bytes 1572868
  59.6 29.7 %copy-start.11 = (bf16[128,1024]{1,0:T(8,128)(2,1)S(1)}, bf16[128,1024]{1,0:T(8,128)(2,1)}, u32[]{:S(2)}) copy-start(bf16[128,1024]{1,0:T(8,128)(2,1)} %base_ref.1) | copy-start | bytes 786436
  74.9 6.9 %collective-permute-start.13 = (bf16[16,1024]{1,0:T(8,128)(2,1)S(1)}, bf16[16,1024]{1,0:T(8,128)(2,1)S(1)}, u32[]{:S(2)}, u32[]{:S(2)}) collective-permute-start(bf16[16,1024]{1,0:T(8,128)(2,1)S(1)} %get-tuple-element.74), channel_id=1, source_target_pairs={{4,0},{5,1},{6,2},{7,3},{8,12},{9,13},{10,14},{11,15},{20,16},{21,... | collective-permute-start | bytes 98312 | tf_op jit(solution)/shard_map/ppermute | solution.py:350
  76.2 6.9 %collective-permute-start.14 = (bf16[16,1024]{1,0:T(8,128)(2,1)S(1)}, bf16[16,1024]{1,0:T(8,128)(2,1)S(1)}, u32[]{:S(2)}, u32[]{:S(2)}) collective-permute-start(bf16[16,1024]{1,0:T(8,128)(2,1)S(1)} %get-tuple-element.75), channel_id=1, source_target_pairs={{4,1},{5,0},{6,3},{7,2},{8,13},{9,12},{10,15},{11,14},{20,17},{21,... | collective-permute-start | bytes 98312 | tf_op jit(solution)/shard_map/ppermute | solution.py:350
  77.7 11.5 %collective-permute-start.10 = (bf16[64,1024]{1,0:T(8,128)(2,1)S(1)}, bf16[64,1024]{1,0:T(8,128)(2,1)S(1)}, u32[]{:S(2)}, u32[]{:S(2)}) collective-permute-start(bf16[64,1024]{1,0:T(8,128)(2,1)S(1)} %get-tuple-element.71), channel_id=1, source_target_pairs={{0,1},{1,0},{2,3},{3,2},{4,5},{5,4},{6,7},{7,6},{8,9},{9,8},{10,11... | collective-permute-start | bytes 393224 | tf_op jit(solution)/shard_map/ppermute | solution.py:350
  78.0 11.3 %collective-permute-start.11 = (bf16[64,1024]{1,0:T(8,128)(2,1)S(1)}, bf16[64,1024]{1,0:T(8,128)(2,1)S(1)}, u32[]{:S(2)}, u32[]{:S(2)}) collective-permute-start(bf16[64,1024]{1,0:T(8,128)(2,1)S(1)} %get-tuple-element.72), channel_id=1, source_target_pairs={{0,2},{1,3},{2,0},{3,1},{4,6},{5,7},{6,4},{7,5},{8,10},{9,11},{10,... | collective-permute-start | bytes 393224 | tf_op jit(solution)/shard_map/ppermute | solution.py:350
  79.5 9.8 %collective-permute-start.12 = (bf16[64,1024]{1,0:T(8,128)(2,1)S(1)}, bf16[64,1024]{1,0:T(8,128)(2,1)S(1)}, u32[]{:S(2)}, u32[]{:S(2)}) collective-permute-start(bf16[64,1024]{1,0:T(8,128)(2,1)S(1)} %get-tuple-element.73), channel_id=1, source_target_pairs={{0,3},{1,2},{2,1},{3,0},{4,7},{5,6},{6,5},{7,4},{8,11},{9,10},{10,... | collective-permute-start | bytes 393224 | tf_op jit(solution)/shard_map/ppermute | solution.py:350
  81.8 6.7 %collective-permute-start.15 = (bf16[16,1024]{1,0:T(8,128)(2,1)S(1)}, bf16[16,1024]{1,0:T(8,128)(2,1)S(1)}, u32[]{:S(2)}, u32[]{:S(2)}) collective-permute-start(bf16[16,1024]{1,0:T(8,128)(2,1)S(1)} %get-tuple-element.76), channel_id=1, source_target_pairs={{4,2},{5,3},{6,0},{7,1},{8,14},{9,15},{10,12},{11,13},{20,18},{21,... | collective-permute-start | bytes 98312 | tf_op jit(solution)/shard_map/ppermute | solution.py:350
  83.1 6.1 %collective-permute-start.16 = (bf16[16,1024]{1,0:T(8,128)(2,1)S(1)}, bf16[16,1024]{1,0:T(8,128)(2,1)S(1)}, u32[]{:S(2)}, u32[]{:S(2)}) collective-permute-start(bf16[16,1024]{1,0:T(8,128)(2,1)S(1)} %get-tuple-element.77), channel_id=1, source_target_pairs={{4,3},{5,2},{6,1},{7,0},{8,15},{9,14},{10,13},{11,12},{20,19},{21,... | collective-permute-start | bytes 98312 | tf_op jit(solution)/shard_map/ppermute | solution.py:350
  89.3 1.6 %copy-start.7 = (f32[128,4096]{1,0:T(8,128)S(1)}, f32[128,4096]{1,0:T(8,128)}, u32[]{:S(2)}) copy-start(f32[128,4096]{1,0:T(8,128)} %copy-done.6) | copy-start | bytes 6291460

commit v3 on v2

--- a/solution.py
+++ b/solution.py
@@ -13,7 +13,7 @@
 GROUP = QUERY_HEADS // KEY_VALUE_HEADS
 SPLIT = KEY_VALUE_HEADS * HEAD_SIZE
 PLANE = 4
-COLS = 1024
+COLS = 2048
 LONG = 20_000_000_000
 
 adapter_scale = 2.0
@@ -41,9 +41,10 @@
 HBM = pl.BlockSpec(memory_space=pltpu.HBM)
 
 
-def options(name, cost=None):
+def options(name, cost=None, mebibytes=12):
     chosen = dict(
-        name=name, compiler_params=pltpu.CompilerParams(vmem_limit_bytes=12 * 1024 * 1024)
+        name=name,
+        compiler_params=pltpu.CompilerParams(vmem_limit_bytes=mebibytes * 1024 * 1024),
     )
     if cost is not None:
         chosen["cost_estimate"] = pl.CostEstimate(
@@ -87,7 +88,7 @@
             weight = jnp.exp(score - peak)
             denominator = jnp.sum(weight, axis=1, keepdims=True)
             mixed = jnp.dot(weight.astype(jnp.bfloat16), v, preferred_element_type=jnp.float32)
-            mixed = mixed / denominator
+            mixed = (mixed / denominator).astype(jnp.bfloat16)
             log = peak + jnp.log(denominator)
             for g in range(GROUP):
                 part = slice(g * step, (g + 1) * step)
@@ -108,16 +109,17 @@
         in_specs=[VMEM] * 3,
         out_specs=[VMEM] * 2,
         out_shape=[
-            jax.ShapeDtypeStruct(queries.shape, jnp.float32),
+            jax.ShapeDtypeStruct(queries.shape, jnp.bfloat16),
             jax.ShapeDtypeStruct((rows, HEAD_SIZE), jnp.float32),
         ],
         **options("cached", LONG),
     )(lengths.reshape(rows, 1), queries, cache)
 
 
-def finish_kernel(count, target_ref, base_ref, q_ref, mixed_ref, log_ref, *refs):
+def finish_kernel(count, target_ref, base_ref, q_ref, log_ref, mixed_hbm, *refs):
     pieces, refs = refs[:count], refs[count:]
-    attention_hbm, written_hbm, attention_ref, written_ref, stack_ref, sems, piece_sems = refs
+    attention_hbm, written_hbm, attention_ref, written_ref, stack_ref, mixed_ref = refs[:6]
+    sems, piece_sems, mixed_sems = refs[6:]
     rows = base_ref.shape[0]
     total = stack_ref.shape[0]
     arrivals, start = [], 0
@@ -128,6 +130,15 @@
         start += piece.shape[0]
     spots = lax.broadcasted_iota(jnp.int32, (rows, total), 1)
     place = (spots == target_ref[...]).astype(jnp.float32).astype(jnp.bfloat16)
+    mixes = []
+    for head in range(KEY_VALUE_HEADS):
+        wide = slice(head * GROUP * HEAD_SIZE, (head + 1) * GROUP * HEAD_SIZE)
+        mixes.append(
+            pltpu.make_async_copy(
+                mixed_hbm.at[:, wide], mixed_ref.at[:, wide], mixed_sems.at[head]
+            )
+        )
+        mixes[-1].start()
     for arrival in arrivals:
         arrival.wait()
     delta = jnp.dot(place, stack_ref[...], preferred_element_type=jnp.float32)
@@ -141,13 +152,14 @@
         new_key = written_ref[:, own].astype(jnp.float32)
         own = slice(SPLIT + head * HEAD_SIZE, SPLIT + (head + 1) * HEAD_SIZE)
         new_value = written_ref[:, own].astype(jnp.float32)
+        mixes[head].wait()
         for i in range(head * GROUP, (head + 1) * GROUP):
             part = slice(i * HEAD_SIZE, (i + 1) * HEAD_SIZE)
             query = q_ref[:, part].astype(jnp.float32)
             score = jnp.sum(query * new_key, axis=1, keepdims=True) * score_scale
             log = jnp.sum(jnp.where(lane == i, logs, 0.0), axis=1, keepdims=True)
             share = 1.0 / (1.0 + jnp.exp(score - log))
-            out = new_value + share * (mixed_ref[:, part] - new_value)
+            out = new_value + share * (mixed_ref[:, part].astype(jnp.float32) - new_value)
             attention_ref[:, part] = out.astype(jnp.bfloat16)
         wide = slice(head * GROUP * HEAD_SIZE, (head + 1) * GROUP * HEAD_SIZE)
         copies.append(
@@ -164,7 +176,7 @@
     rows = base.shape[0]
     return pl.pallas_call(
         functools.partial(finish_kernel, len(pieces)),
-        in_specs=[VMEM] * 5 + [HBM] * len(pieces),
+        in_specs=[VMEM] * 4 + [HBM] * (1 + len(pieces)),
         out_specs=[HBM] * 2,
         out_shape=[
             jax.ShapeDtypeStruct(queries.shape, jnp.bfloat16),
@@ -174,33 +186,80 @@
             pltpu.VMEM(queries.shape, jnp.bfloat16),
             pltpu.VMEM(base.shape, jnp.bfloat16),
             pltpu.VMEM((sum(piece.shape[0] for piece in pieces), base.shape[1]), jnp.bfloat16),
+            pltpu.VMEM(mixed.shape, mixed.dtype),
             pltpu.SemaphoreType.DMA((KEY_VALUE_HEADS + 1,)),
             pltpu.SemaphoreType.DMA((len(pieces),)),
+            pltpu.SemaphoreType.DMA((KEY_VALUE_HEADS,)),
         ],
-        **options("finish"),
-    )(target.reshape(rows, 1), base, queries, mixed, logs, *pieces)
-
-
-def pack_kernel(target_ref, hidden_ref, *outs):
+        **options("finish", 1000),
+    )(target.reshape(rows, 1), base, queries, logs, mixed, *pieces)
+
+
+def pack_kernel(target_ref, hidden_hbm, *refs):
+    outs, (hidden_ref, packed_ref, hidden_sems, sems) = refs[:-4], refs[-4:]
+    spots = packed_ref.shape[0]
+    parts = chunks(hidden_ref.shape[1])
+    fetches, stores = [], []
+    for i, part in enumerate(parts):
+        fetches.append(
+            pltpu.make_async_copy(
+                hidden_hbm.at[:, part], hidden_ref.at[:, part], hidden_sems.at[i]
+            )
+        )
+        fetches[-1].start()
+    spot = lax.broadcasted_iota(jnp.int32, (spots, hidden_ref.shape[0]), 0)
+    place = (spot == target_ref[...]).astype(jnp.float32).astype(jnp.bfloat16)
+    for i, part in enumerate(parts):
+        fetches[i].wait()
+        packed = jnp.dot(place, hidden_ref[:, part], preferred_element_type=jnp.float32)
+        packed_ref[:, part] = packed.astype(jnp.bfloat16)
+        start = 0
+        for j, out in enumerate(outs):
+            own = packed_ref.at[start : start + out.shape[0], part]
+            stores.append(pltpu.make_async_copy(own, out.at[:, part], sems.at[i, j]))
+            stores[-1].start()
+            start += out.shape[0]
+    for store in stores:
+        store.wait()
+
+
+def pack(target, hidden, heights, cost):
+    rows, width = hidden.shape
+    steps = len(chunks(width))
+    return pl.pallas_call(
+        pack_kernel,
+        in_specs=[VMEM, HBM],
+        out_specs=[HBM] * len(heights),
+        out_shape=[jax.ShapeDtypeStruct((height, width), jnp.bfloat16) for height in heights],
+        scratch_shapes=[
+            pltpu.VMEM(hidden.shape, jnp.bfloat16),
+            pltpu.VMEM((sum(heights), width), jnp.bfloat16),
+            pltpu.SemaphoreType.DMA((steps,)),
+            pltpu.SemaphoreType.DMA((steps, len(heights))),
+        ],
+        **options("pack", cost, 60),
+    )(target.reshape(1, rows), hidden)
+
+
+def pack_first_kernel(target_ref, hidden_ref, *outs):
     height = outs[0].shape[0]
-    spots = height * len(outs)
-    spot = lax.broadcasted_iota(jnp.int32, (spots, hidden_ref.shape[0]), 0)
+    spot = lax.broadcasted_iota(jnp.int32, (height * len(outs), hidden_ref.shape[0]), 0)
     place = (spot == target_ref[...]).astype(jnp.float32).astype(jnp.bfloat16)
     for part in chunks(hidden_ref.shape[1]):
         packed = jnp.dot(place, hidden_ref[:, part], preferred_element_type=jnp.float32)
         packed = packed.astype(jnp.bfloat16)
-        for k, out in enumerate(outs):
-            out[:, part] = packed[k * height : (k + 1) * height]
-
-
-def pack(target, hidden, height, cost):
+        for i, out in enumerate(outs):
+            out[:, part] = packed[i * height : (i + 1) * height]
+
+
+def pack_first(target, hidden, height, count):
     rows, width = hidden.shape
     return pl.pallas_call(
-        pack_kernel,
+        pack_first_kernel,
         in_specs=[VMEM] * 2,
-        out_specs=[VMEM] * PLANE,
-        out_shape=[jax.ShapeDtypeStruct((height, width), jnp.bfloat16)] * PLANE,
-        **options("pack", cost),
+        out_specs=[VMEM] * count,
+        out_shape=[jax.ShapeDtypeStruct((height, width), jnp.bfloat16)] * count,
+        **options("first"),
     )(target.reshape(1, rows), hidden)
 
 
@@ -220,16 +279,10 @@
     return total
 
 
-def both_slots(capacity, total, ups, outs, first=0):
-    for slot, up in enumerate(ups):
-        rank = up.shape[0]
-        lanes = slice(slot * rank, (slot + 1) * rank)
-        starts = [(2 * k + slot) * capacity for k in range(PLANE)]
-        sums = jnp.concatenate([total[i : i + capacity, lanes] for i in starts], axis=0)
-        wide = expand(sums, up)
-        start = (first + slot) * capacity
-        for k, out in enumerate(outs):
-            out[start : start + capacity] = wide[k * capacity : (k + 1) * capacity]
+def put(out, dest, slots, slot, rows):
+    height = rows.shape[0]
+    start = pl.multiple_of((dest * slots + slot) * height, height)
+    out[pl.ds(start, height), :] = rows
 
 
 def join_kernel(down_hbm, up_hbm, out_ref, sems):
@@ -249,88 +302,108 @@
         out_specs=VMEM,
         out_shape=jax.ShapeDtypeStruct((down.shape[0], down.shape[1] + up.shape[1]), down.dtype),
         scratch_shapes=[pltpu.SemaphoreType.DMA((2,))],
-        **options("join"),
+        **options("join", 1000, 60),
     )(down, up)
 
 
-def early_kernel(capacity, *refs):
-    rows, (outward, own), out = refs[:PLANE], refs[PLANE : PLANE + 2], refs[PLANE + 2]
+def early_kernel(capacity, where_ref, *refs):
+    rows, (outward, middle, own, *outs) = refs[: 3 * PLANE], refs[3 * PLANE :]
+    width, rank = rows[0].shape[1], own.shape[0]
+
+    def run(weights):
+        total = shrink(rows, weights)
+        for slot, weight in enumerate(weights):
+            start = slot * PLANE * capacity
+            sums = total[start : start + PLANE * capacity, slot * rank : (slot + 1) * rank]
+            wide = expand(sums, weight[:, width:])
+            for k, out in enumerate(outs):
+                out[slot * capacity : (slot + 1) * capacity] = wide[
+                    k * capacity : (k + 1) * capacity
+                ]
+
+    pl.when(where_ref[0] == 1)(lambda: run([outward, own, middle]))
+    pl.when(where_ref[0] == 0)(lambda: run([outward, own, outward]))
+
+
+def early(where, rows, outward, middle, own, capacity):
+    out_width = own.shape[1] - rows[0].shape[1]
+    return pl.pallas_call(
+        functools.partial(early_kernel, capacity),
+        in_specs=[SMEM] + [VMEM] * (3 * PLANE + 3),
+        out_specs=[VMEM] * PLANE,
+        out_shape=[jax.ShapeDtypeStruct((3 * capacity, out_width), jnp.bfloat16)] * PLANE,
+        **options("early", LONG),
+    )(where, *rows, outward, middle, own)
+
+
+def late_kernel(capacity, where_ref, *refs):
+    rows, (middle2, swapped, out) = refs[:PLANE], refs[PLANE:]
     width = rows[0].shape[1]
-    total = shrink(rows, [outward, own])
-    outs = [out.at[2 * k * capacity : 2 * (k + 1) * capacity] for k in range(PLANE)]
-    both_slots(capacity, total, (outward[:, width:], own[:, width:]), outs)
-
-
-def early(rows, outward, own, capacity):
-    out_width = own.shape[1] - rows[0].shape[1]
-    return pl.pallas_call(
-        functools.partial(early_kernel, capacity),
-        in_specs=[VMEM] * (PLANE + 2),
+    place, here, there = where_ref[1], where_ref[2], where_ref[3]
+
+    def spread(first, wide):
+        for k in range(PLANE):
+            put(out, first + (place ^ k), 1, 0, wide[k * capacity : (k + 1) * capacity])
+
+    @pl.when(where_ref[0] == 1)
+    def _():
+        total = shrink([*rows, swapped], [middle2])
+        wide = expand(total, middle2[:, width:])
+        spread(here, wide)
+        spread(there, wide[PLANE * capacity :])
+
+    @pl.when(where_ref[0] == 0)
+    def _():
+        wide = expand(shrink(rows, [swapped]), swapped[:, width:])
+        spread(here, wide)
+        spread(there, jnp.zeros(wide.shape, wide.dtype))
+
+
+def late(where, rows, middle2, swapped, capacity):
+    out_width = swapped.shape[1] - rows[0].shape[1]
+    return pl.pallas_call(
+        functools.partial(late_kernel, capacity),
+        in_specs=[SMEM] + [VMEM] * (PLANE + 2),
         out_specs=VMEM,
         out_shape=jax.ShapeDtypeStruct((2 * PLANE * capacity, out_width), jnp.bfloat16),
-        **options("early"),
-    )(*rows, outward, own)
-
-
-def late_kernel(capacity, where_ref, soon_ref, *refs):
-    rows, refs = refs[:PLANE], refs[PLANE:]
-    outward, middle, middle2, swapped = refs[:4]
-    outs, fars = refs[4 : 4 + PLANE], refs[4 + PLANE :]
-    width = rows[0].shape[1]
-    for k, out in enumerate(outs):
-        out[: 2 * capacity] = soon_ref[2 * k * capacity : 2 * (k + 1) * capacity]
-
-    @pl.when(where_ref[0] == 1)
-    def _():
-        total = shrink([*rows, swapped], [middle, middle2])
-        both_slots(capacity, total, (middle[:, width:], middle2[:, width:]), outs, 2)
-        wide = expand(total[2 * PLANE * capacity :, middle.shape[0] :], middle2[:, width:])
-        for k, far in enumerate(fars):
-            far[...] = wide[k * capacity : (k + 1) * capacity]
+        **options("late"),
+    )(where, *rows, middle2, swapped)
+
+
+def choose_kernel(where_ref, weights_hbm, *refs):
+    rows, (out_hbm, stack_ref, sems) = refs[:PLANE], refs[PLANE:]
+    capacity, width = stack_ref.shape[0] // PLANE, stack_ref.shape[1]
 
     @pl.when(where_ref[0] == 0)
     def _():
-        total = shrink(rows, [outward, swapped])
-        both_slots(capacity, total, (outward[:, width:], swapped[:, width:]), outs, 2)
-        for far in fars:
-            far[...] = jnp.zeros(far.shape, far.dtype)
-
-
-def late(where, soon, rows, weights, capacity):
-    out_width = weights[0].shape[1] - rows[0].shape[1]
-    near = jax.ShapeDtypeStruct((4 * capacity, out_width), jnp.bfloat16)
-    far = jax.ShapeDtypeStruct((capacity, out_width), jnp.bfloat16)
-    return pl.pallas_call(
-        functools.partial(late_kernel, capacity),
-        in_specs=[SMEM] + [VMEM] * (PLANE + 5),
-        out_specs=[VMEM] * (2 * PLANE),
-        out_shape=[near] * PLANE + [far] * PLANE,
-        **options("late"),
-    )(where, soon, *rows, *weights)
-
-
-def choose_kernel(where_ref, weights_ref, *refs):
-    rows, out = refs[:PLANE], refs[PLANE]
-    capacity, width = out.shape[0] // PLANE, rows[0].shape[1]
-
-    @pl.when(where_ref[0] == 1)
-    def _():
-        out[...] = weights_ref[...]
-
-    @pl.when(where_ref[0] == 0)
-    def _():
+        copies = []
         for k, ref in enumerate(rows):
-            out[k * capacity : (k + 1) * capacity, :width] = ref[:capacity]
-        out[:, width:] = jnp.zeros((out.shape[0], out.shape[1] - width), out.dtype)
+            for i, part in enumerate(chunks(width)):
+                here = stack_ref.at[k * capacity : (k + 1) * capacity, part]
+                there = out_hbm.at[k * capacity : (k + 1) * capacity, part]
+                fetch = pltpu.make_async_copy(ref.at[:, part], here, sems.at[0, k, i])
+                copies.append((fetch, pltpu.make_async_copy(here, there, sems.at[1, k, i])))
+                fetch.start()
+        for fetch, store in copies:
+            fetch.wait()
+            store.start()
+        for _, store in copies:
+            store.wait()
 
 
 def choose(where, weights, rows):
+    height, width = rows[0].shape
     return pl.pallas_call(
         choose_kernel,
-        in_specs=[SMEM] + [VMEM] * (1 + PLANE),
-        out_specs=VMEM,
+        in_specs=[SMEM] + [HBM] * (1 + PLANE),
+        out_specs=HBM,
         out_shape=jax.ShapeDtypeStruct(weights.shape, weights.dtype),
-        **options("choose"),
+        scratch_shapes=[
+            pltpu.VMEM((height * PLANE, width), weights.dtype),
+            pltpu.SemaphoreType.DMA((2, PLANE, len(chunks(width)))),
+        ],
+        input_output_aliases={1: 0},
+        **options("choose", 1000, 60),
     )(where, weights, *rows)
 
 
@@ -339,7 +412,8 @@
     me = lax.axis_index("adapter")
     plane, place = me // PLANE, me % PLANE
     inner = (plane == 1) | (plane == 2)
-    where = inner.astype(jnp.int32).reshape(1)
+    here = plane % 2 * PLANE
+    where = jnp.stack([inner.astype(jnp.int32), place, here, PLANE - here]).astype(jnp.int32)
     all_devices = range(devices)
     middles = [i for i in all_devices if i // PLANE in (1, 2)]
     across = [
@@ -348,6 +422,13 @@
     to_outward = [(i, i ^ PLANE) for i in all_devices]
     to_middle = [(i, i ^ (3 * PLANE)) for i in middles]
     send = lambda a, pairs: lax.ppermute(a, "adapter", pairs)
+
+    def gather(rows, size):
+        parts = rows.reshape(size, -1, rows.shape[1])
+        groups = [list(range(i, i + size)) for i in range(0, devices, size)]
+        parts = lax.all_to_all(parts, "adapter", 0, 0, axis_index_groups=groups, tiled=True)
+        return parts.reshape(rows.shape)
+
     exchange = lambda parts: [parts[0]] + [send(parts[k], across[k]) for k in range(1, PLANE)]
 
     plane_of, place_of = slot // PLANE, slot % PLANE
@@ -360,31 +441,38 @@
     )
     rank = rank_in_slot(slot)
     k = place_of ^ place
-    spot = (k * 2 + kind % 2) * capacity + rank
-    spots = 2 * PLANE * capacity
     back = jnp.where(
-        (kind == 0) & ~inner,
-        2 * spots + k * capacity + rank,
-        (k * 4 + kind) * capacity + rank,
-    )
+        kind < 3,
+        (k * 3 + kind) * capacity + rank,
+        (3 * PLANE + here + place_of) * capacity + rank,
+    )
+    passed = (3 * PLANE + PLANE - here + place_of) * capacity + rank
+    back = jnp.where((kind == 0) & ~inner, passed, back)
 
     weights = join(down, up)
     outward, middle = send(weights, to_outward), send(weights, to_middle)
-    near = exchange(pack(jnp.where(kind < 2, spot, -1), hidden, 2 * capacity, None))
-    away = pack(jnp.where(kind < 2, -1, spot), hidden, 2 * capacity, LONG)
-    near, away, outward, middle = lax.optimization_barrier((near, away, outward, middle))
-    middle2 = send(outward, to_middle)
-    swapped = send(choose(where, middle, near), to_outward)
-    away = exchange(away)
-
+    first = pack_first(
+        jnp.where(kind == 0, (k - 1) * capacity + rank, -1), hidden, capacity, PLANE - 1
+    )
+    to_rest = jnp.where(kind == 0, jnp.where(k == 0, 0, -1), 1 + (kind - 1) * PLANE + k)
+    to_rest = jnp.where(to_rest < 0, -1, to_rest * capacity + rank)
+    kept, *rest = pack(to_rest, hidden, [capacity] * (1 + 3 * PLANE), LONG)
+    own, near, far = (rest[i * PLANE : (i + 1) * PLANE] for i in range(3))
+    first, own = lax.optimization_barrier((exchange([kept, *first]), own))
+    own = exchange(own)
     done = meanwhile()
-    near, done = lax.optimization_barrier((near, done))
-    soon = early(near, outward, weights, capacity)
-    where, done, soon = lax.optimization_barrier((where, done, soon))
-    outs = late(where, soon, away, [outward, middle, middle2, swapped], capacity)
-    last = exchange(outs[:PLANE])
-    far = [send(outs[PLANE + k], [(i, (i ^ PLANE) ^ k) for i in middles]) for k in range(PLANE)]
-    return back, [*last, *far], done
+    outward, middle, done = lax.optimization_barrier((outward, middle, done))
+    middle = choose(where, middle, first)
+    own, near, outward, middle = lax.optimization_barrier((own, near, outward, middle))
+    middle2, swapped = send(outward, to_middle), send(middle, to_outward)
+    near, far = lax.optimization_barrier((exchange(near), far))
+    far = exchange(far)
+    rows = [*first, *own, *near]
+    soon = early(where, rows, outward, middle, weights, capacity)
+    soon, where = lax.optimization_barrier((soon, where))
+    soon = exchange(soon)
+    last = gather(late(where, far, middle2, swapped, capacity), 2 * PLANE)
+    return back, [*soon, last], done
 
 
 def by_rows(hidden, slot, down, up, capacity, meanwhile):

time: 94.4 us -> 91.1 us (0.965)
  waiting for transfers between devices: 39.6 us -> 31.5 us
  Pallas kernels: 23.5 us -> 25.7 us
  starting transfers between devices: 20.6 us -> 21.7 us
  other arithmetic: 0.4 us -> 1.49 us
    ppermute x17 -> x19, waiting for transfers between devices: 39.6 us -> 31.5 us  [by_planes(): send = lambda a, pairs: lax.ppermute(a, 'adapter', pairs)]
    all_to_all x0 -> x1, starting transfers between devices: none -> 3.41 us  [gather(): lax.all_to_all(parts, 'adapter', 0, 0, axis_index_groups=groups, tiled=True)]
    ppermute x17 -> x19, starting transfers between devices: 20.6 us -> 18.3 us  [by_planes(): send = lambda a, pairs: lax.ppermute(a, 'adapter', pairs)]
    pallas_call x4, Pallas kernels: 10.1 us -> 12.4 us  [the longest x1 4.53 us: pack(): pl.pallas_call(pack_kernel, in_specs=[VMEM, HBM], out_specs=[HBM] * len(h...]
    pallas_call x1, Pallas kernels: 3.51 us -> 1.9 us  [late(): pl.pallas_call(functools.partial(late_kernel, capacity), in_specs=[SMEM]...]
    pallas_call x1, Pallas kernels: 1.14 us -> 2.42 us  [join(): pl.pallas_call(join_kernel, in_specs=[HBM] * 2, out_specs=VMEM, out_shape...]
    unnamed x32 -> x46, local copies, waits for them, and re-layouts: 8.6 us -> 8.97 us
  transfers between devices with their start and end apart: 17 -> 20, of which waited for: 7 -> 7; matrix products, arithmetic and copies ran while one was open for 1% -> 2% of each run, Pallas kernels for 14% -> 20%
where the time goes in v3:
time: 91.1 us; the launch traced here: 90.6 us
  waiting for transfers between devices  31.5 us (35%)
  Pallas kernels  25.7 us (28%)
  starting transfers between devices  21.7 us (24%)
  local copies, waits for them, and re-layouts  9.3 us (10%)
  other arithmetic  1.49 us (2%)
  between operations  0.92 us (1%)
    ppermute x19, waiting for transfers between devices, by_planes(): send = lambda a, pairs: lax.ppermute(a, 'adapter', pairs)  31.5 us
    ppermute x19, starting transfers between devices, by_planes(): send = lambda a, pairs: lax.ppermute(a, 'adapter', pairs)  18.3 us
    unnamed x46, local copies, waits for them, and re-layouts  8.97 us
    pallas_call x1, Pallas kernels, cached_attention(): pl.pallas_call(functools.partial(cached_kernel, 16), in_specs=[VMEM] * 3,...  5.62 us
    pallas_call x1, Pallas kernels, pack(): pl.pallas_call(pack_kernel, in_specs=[VMEM, HBM], out_specs=[HBM] * len(h...  4.53 us
    pallas_call x1, Pallas kernels, early(): pl.pallas_call(functools.partial(early_kernel, capacity), in_specs=[SMEM]...  3.74 us
    all_to_all x1, starting transfers between devices, gather(): lax.all_to_all(parts, 'adapter', 0, 0, axis_index_groups=groups, tiled=True)  3.41 us
    pallas_call x1, Pallas kernels, finish(): pl.pallas_call(functools.partial(finish_kernel, len(pieces)), in_specs=[V...  3.35 us
  transfers between devices with their start and end apart: 20, of which 7 were waited for; matrix products, arithmetic and copies ran while one was open for 2% of the time, Pallas kernels for 20%

profile of v3, /device:TPU:0, one launch (start us, length us, event | category | flops | bytes accessed | tf_op | source)
XLA Modules:
  0.0 90.6 jit_solution(14707846780846926460)
XLA Ops:
  0.7 0.0 copy-start
  0.7 2.4 %join.1.refs_14_ = bf16[64,9216]{1,0:T(8,128)(2,1)} custom-call(bf16[64,8192]{1,0:T(8,128)(2,1)} %bitcast.45, bf16[64,1024]{1,0:T(8,128)(2,1)} %bitcast.46), custom_call_target="tpu_custom_call" | custom-call | flops 1000 | bytes 1000 | tf_op jit(solution)/shard_map/join/pallas_call | solution.py:299
  3.1 3.1 %collective-permute-start = (bf16[64,9216]{1,0:T(8,128)(2,1)}, bf16[64,9216]{1,0:T(8,128)(2,1)}, u32[]{:S(2)}, u32[]{:S(2)}) collective-permute-start(bf16[64,9216]{1,0:T(8,128)(2,1)} %join.1.refs_14_), channel_id=1, source_target_pairs={{0,4},{1,5},{2,6},{3,7},{4,0},{5,1},{6,2},{7,3},{8,12},{9,13},{10,... | collective-permute-start | bytes 3538952 | tf_op jit(solution)/shard_map/ppermute | solution.py:424
  6.2 0.7 collective-permute-start.1
  7.0 0.1 select_reduce_fusion
  7.0 0.2 convert_reduce_fusion
  7.2 0.6 compare_select_fusion.7
  7.8 1.1 %first.1 = (bf16[16,8192]{1,0:T(8,128)(2,1)}, bf16[16,8192]{1,0:T(8,128)(2,1)S(1)}, bf16[16,8192]{1,0:T(8,128)(2,1)S(1)}) custom-call(s32[1,128]{1,0:T(1,128)S(1)} %get-tuple-element.116.target_ref, bf16[128,8192]{1,0:T(8,128)(2,1)S(1)} %copy-done), custom_call_target="tpu_custom_call" | custom-call | tf_op jit(solution)/shard_map/first/pallas_call | solution.py:257
  8.9 0.0 collective-permute-start.2
  8.9 1.5 %collective-permute-start.3 = (bf16[16,8192]{1,0:T(8,128)(2,1)S(1)}, bf16[16,8192]{1,0:T(8,128)(2,1)S(1)}, u32[]{:S(2)}, u32[]{:S(2)}) collective-permute-start(bf16[16,8192]{1,0:T(8,128)(2,1)S(1)} %get-tuple-element.65), channel_id=1, source_target_pairs={{0,2},{1,3},{2,0},{3,1},{4,6},{5,7},{6,4},{7,5},{8,10},{9,11},{10,... | collective-permute-start | bytes 786440 | tf_op jit(solution)/shard_map/ppermute | solution.py:424
  10.4 0.4 collective-permute-start.4
  10.8 4.5 %pack.1 = (bf16[16,8192]{1,0:T(8,128)(2,1)}, bf16[16,8192]{1,0:T(8,128)(2,1)}, bf16[16,8192]{1,0:T(8,128)(2,1)}, bf16[16,8192]{1,0:T(8,128)(2,1)}, bf16[16,8192]...) custom-call(s32[1,128]{1,0:T(1,128)} %get-tuple-element.117.target_r, ...), custom_call_target="tpu_custom_call" | custom-call | flops 1000 | bytes 20000000000 | tf_op jit(solution)/shard_map/pack/pallas_call | solution.py:229
  15.3 0.0 collective-permute-done.2.refs_1_
  15.3 2.7 %collective-permute-done.3.refs_2_ = bf16[16,8192]{1,0:T(8,128)(2,1)S(1)} collective-permute-done((bf16[16,8192]{1,0:T(8,128)(2,1)S(1)}, bf16[16,8192]{1,0:T(8,128)(2,1)S(1)}, u32[]{:S(2)}, u32[]{:S(2)}) %collective-permute-start.3) | collective-permute-done | bytes 262176 | tf_op jit(solution)/shard_map/ppermute | solution.py:424
  18.0 4.9 %collective-permute-done.4.refs_3_ = bf16[16,8192]{1,0:T(8,128)(2,1)} collective-permute-done((bf16[16,8192]{1,0:T(8,128)(2,1)S(1)}, bf16[16,8192]{1,0:T(8,128)(2,1)}, u32[]{:S(2)}, u32[]{:S(2)}) %collective-permute-start.4) | collective-permute-done | bytes 262176 | tf_op jit(solution)/shard_map/ppermute | solution.py:424
  22.9 0.5 collective-permute-start.5
  23.5 1.5 %collective-permute-start.6 = (bf16[16,8192]{1,0:T(8,128)(2,1)}, bf16[16,8192]{1,0:T(8,128)(2,1)}, u32[]{:S(2)}, u32[]{:S(2)}) collective-permute-start(bf16[16,8192]{1,0:T(8,128)(2,1)} %get-tuple-element.77), channel_id=1, source_target_pairs={{0,2},{1,3},{2,0},{3,1},{4,6},{5,7},{6,4},{7,5},{8,10},{9,11},{10,... | collective-permute-start | bytes 786440 | tf_op jit(solution)/shard_map/ppermute | solution.py:424
  24.9 0.0 collective-permute-start.7
  24.9 0.1 copy.27.length_ref
  25.1 0.0 copy-start.4
  25.1 2.2 %copy-done.4 = bf16[128,16,1024]{2,1,0:T(8,128)(2,1)S(1)} copy-done((bf16[128,16,1024]{2,1,0:T(8,128)(2,1)S(1)}, bf16[128,16,1024]{2,1,0:T(8,128)(2,1)}, u32[]{:S(2)}) %copy-start.4) | copy-done | bytes 4194328
  27.3 5.6 %cached.1 = (bf16[128,4096]{1,0:T(8,128)(2,1)S(1)}, f32[128,128]{1,0:T(8,128)S(1)}) custom-call(s32[128,1]{1,0:T(8,128)S(1)} %copy.27.length_ref, bf16[128,4096]{1,0:T(8,128)(2,1)S(1)} %copy-done.5, bf16[128,16,1024]{2,1,0:T(8,128)(2,1)S(1)} %copy-done.4), custom_call_target="tpu_custom_call" | custom-call | flops 1000 | bytes 20000000000 | tf_op jit(solution)/shard_map/cached/pallas_call | solution.py:107
  32.9 0.0 copy-start.6
  32.9 1.0 %copy-done.6 = bf16[128,4096]{1,0:T(8,128)(2,1)} copy-done((bf16[128,4096]{1,0:T(8,128)(2,1)}, bf16[128,4096]{1,0:T(8,128)(2,1)S(1)}, u32[]{:S(2)}) %copy-start.6) | copy-done | bytes 1048600
  33.9 0.6 copy-done.17
  34.5 0.6 pad_add_fusion.where_ref
  35.1 0.0 collective-permute-done.refs_12_
  35.1 0.0 collective-permute-done.1.weights_hbm
  35.1 1.0 %copy-done.2 = bf16[64,9216]{1,0:T(8,128)(2,1)} copy-done((bf16[64,9216]{1,0:T(8,128)(2,1)}, bf16[64,9216]{1,0:T(8,128)(2,1)S(1)}, u32[]{:S(2)}) %copy-start.2) | copy-done | bytes 1179672
  36.1 3.0 %choose.1.refs_13_ = bf16[64,9216]{1,0:T(8,128)(2,1)} custom-call(s32[4]{0:T(128)} %pad_add_fusion.where_ref, bf16[64,9216]{1,0:T(8,128)(2,1)} %copy-done.2, bf16[16,8192]{1,0:T(8,128)(2,1)} %get-tuple-element.71.refs_0_, bf16[16,8192]{1,0:T(8,128)(2,1)} %copy-done.8, bf16[16,8192]{1,0:T(8,128)(2,1)} %copy-done.10, ...), custom_call_target="tpu_custom_call", output_to_operand_aliasing={{}: (1, {})} | custom-call | flops 1000 | bytes 1000 | tf_op jit(solution)/shard_map/choose/pallas_call | solution.py:396
  39.1 0.0 collective-permute-done.5.refs_5_
  39.1 0.0 collective-permute-done.6.refs_6_
  39.1 0.0 collective-permute-done.7.refs_7_
  39.1 0.7 collective-permute-start.17
  39.9 3.7 %collective-permute-start.18 = (bf16[64,9216]{1,0:T(8,128)(2,1)}, bf16[64,9216]{1,0:T(8,128)(2,1)S(1)}, u32[]{:S(2)}, u32[]{:S(2)}) collective-permute-start(bf16[64,9216]{1,0:T(8,128)(2,1)} %choose.1.refs_13_), channel_id=1, source_target_pairs={{0,4},{1,5},{2,6},{3,7},{4,0},{5,1},{6,2},{7,3},{8,12},{9,13},{10,... | collective-permute-start | bytes 3538952 | tf_op jit(solution)/shard_map/ppermute | solution.py:424
  43.6 1.5 %collective-permute-start.10 = (bf16[16,8192]{1,0:T(8,128)(2,1)}, bf16[16,8192]{1,0:T(8,128)(2,1)S(1)}, u32[]{:S(2)}, u32[]{:S(2)}) collective-permute-start(bf16[16,8192]{1,0:T(8,128)(2,1)} %get-tuple-element.92), channel_id=1, source_target_pairs={{0,3},{1,2},{2,1},{3,0},{4,7},{5,6},{6,5},{7,4},{8,11},{9,10},{10,... | collective-permute-start | bytes 786440 | tf_op jit(solution)/shard_map/ppermute | solution.py:424
  45.1 0.0 collective-permute-start.8
  45.1 0.7 collective-permute-start.9
  45.8 6.3 %collective-permute-done.10.refs_11_ = bf16[16,8192]{1,0:T(8,128)(2,1)S(1)} collective-permute-done((bf16[16,8192]{1,0:T(8,128)(2,1)}, bf16[16,8192]{1,0:T(8,128)(2,1)S(1)}, u32[]{:S(2)}, u32[]{:S(2)}) %collective-permute-start.10) | collective-permute-done | bytes 262176 | tf_op jit(solution)/shard_map/ppermute | solution.py:424
  52.0 6.0 %collective-permute-done.9.refs_10_ = bf16[16,8192]{1,0:T(8,128)(2,1)S(1)} collective-permute-done((bf16[16,8192]{1,0:T(8,128)(2,1)}, bf16[16,8192]{1,0:T(8,128)(2,1)S(1)}, u32[]{:S(2)}, u32[]{:S(2)}) %collective-permute-start.9) | collective-permute-done | bytes 262176 | tf_op jit(solution)/shard_map/ppermute | solution.py:424
  58.1 1.3 %collective-permute-start.15 = (bf16[16,8192]{1,0:T(8,128)(2,1)}, bf16[16,8192]{1,0:T(8,128)(2,1)S(1)}, u32[]{:S(2)}, u32[]{:S(2)}) collective-permute-start(bf16[16,8192]{1,0:T(8,128)(2,1)} %get-tuple-element.114), channel_id=1, source_target_pairs={{0,2},{1,3},{2,0},{3,1},{4,6},{5,7},{6,4},{7,5},{8,10},{9,11},{10,... | collective-permute-start | bytes 786440 | tf_op jit(solution)/shard_map/ppermute | solution.py:424
  59.4 0.5 collective-permute-start.16
  59.9 1.3 %copy-done.3 = bf16[64,9216]{1,0:T(8,128)(2,1)S(1)} copy-done((bf16[64,9216]{1,0:T(8,128)(2,1)S(1)}, bf16[64,9216]{1,0:T(8,128)(2,1)}, u32[]{:S(2)}) %copy-start.3) | copy-done | bytes 1179672
  61.2 0.9 %copy-done.12 = bf16[16,8192]{1,0:T(8,128)(2,1)S(1)} copy-done((bf16[16,8192]{1,0:T(8,128)(2,1)S(1)}, bf16[16,8192]{1,0:T(8,128)(2,1)}, u32[]{:S(2)}) %copy-start.12) | copy-done | bytes 262168
  62.2 0.9 %copy-done.15 = bf16[16,8192]{1,0:T(8,128)(2,1)S(1)} copy-done((bf16[16,8192]{1,0:T(8,128)(2,1)S(1)}, bf16[16,8192]{1,0:T(8,128)(2,1)}, u32[]{:S(2)}) %copy-start.15) | copy-done | bytes 262168
  63.1 0.9 %copy-done.16 = bf16[16,8192]{1,0:T(8,128)(2,1)S(1)} copy-done((bf16[16,8192]{1,0:T(8,128)(2,1)S(1)}, bf16[16,8192]{1,0:T(8,128)(2,1)}, u32[]{:S(2)}) %copy-start.16) | copy-done | bytes 262168
  64.1 3.7 %early.1 = (bf16[48,1024]{1,0:T(8,128)(2,1)S(1)}, bf16[48,1024]{1,0:T(8,128)(2,1)}, bf16[48,1024]{1,0:T(8,128)(2,1)}, bf16[48,1024]{1,0:T(8,128)(2,1)S(1)}) custom-call(s32[4]{0:T(128)S(1)} %copy-done.19, bf16[16,8192]{1,0:T(8,128)(2,1)S(1)} %copy-done.12, bf16[16,8192]{1,0:T(8,128)(2,1)S(1)} %copy-done.9, bf16[16,8192]{1,0:T(8,128)(2,1)S(1)} %copy-done.11, ...), custom_call_target="tpu_custom_call" | custom-call | flops 1000 | bytes 20000000000 | tf_op jit(solution)/shard_map/early/pallas_call | solution.py:330
  67.8 0.0 collective-permute-done.15.refs_2_
  67.8 4.4 %collective-permute-done.16.refs_3_ = bf16[16,8192]{1,0:T(8,128)(2,1)S(1)} collective-permute-done((bf16[16,8192]{1,0:T(8,128)(2,1)}, bf16[16,8192]{1,0:T(8,128)(2,1)S(1)}, u32[]{:S(2)}, u32[]{:S(2)}) %collective-permute-start.16) | collective-permute-done | bytes 262176 | tf_op jit(solution)/shard_map/ppermute | solution.py:424
  72.2 0.0 collective-permute-done.17.refs_4_
  72.2 0.0 collective-permute-done.18.refs_5_
  72.2 0.0 copy-start.7
  72.2 1.9 %late.1 = bf16[128,1024]{1,0:T(8,128)(2,1)} custom-call(s32[4]{0:T(128)S(1)} %copy-done.19, bf16[16,8192]{1,0:T(8,128)(2,1)S(1)} %copy-done.14, bf16[16,8192]{1,0:T(8,128)(2,1)S(1)} %collective-permute-done.14.refs_1_, bf16[16,8192]{1,0:T(8,128)(2,1)S(1)} %collective-permute-done.15.refs_2_, bf16[16,8192]{1,0:T(8,128)(2,1)S(1)} %collective-permute-done.16.refs_3_, ...), custom_call_target="tpu_custom_call" | custom-call | tf_op jit(solution)/shard_map/late/pallas_call | solution.py:364
  74.1 3.4 %all-to-all-start = ((bf16[8,16,1024]{2,1,0:T(8,128)(2,1)}), bf16[8,16,1024]{2,1,0:T(8,128)(2,1)S(1)}, u32[]{:S(2)}, u32[]{:S(2)}) async-start(bf16[8,16,1024]{2,1,0:T(8,128)(2,1)} %bitcast.12), calls=%async_computation | async-start | bytes 524288 | tf_op jit(solution)/shard_map/all_to_all | solution.py:429
  77.6 0.1 copy.24
  77.7 0.1 copy.20
  77.8 0.5 collective-permute-start.11
  78.2 1.7 %collective-permute-start.12 = (bf16[48,1024]{1,0:T(8,128)(2,1)}, bf16[48,1024]{1,0:T(8,128)(2,1)S(1)}, u32[]{:S(2)}, u32[]{:S(2)}) collective-permute-start(bf16[48,1024]{1,0:T(8,128)(2,1)} %get-tuple-element.109), channel_id=1, source_target_pairs={{0,2},{1,3},{2,0},{3,1},{4,6},{5,7},{6,4},{7,5},{8,10},{9,11},{10,... | collective-permute-start | bytes 294920 | tf_op jit(solution)/shard_map/ppermute | solution.py:424
  79.9 0.0 collective-permute-start.13
  79.9 0.1 select_select_fusion.target_ref
  80.1 6.0 %collective-permute-done.12.refs_2_ = bf16[48,1024]{1,0:T(8,128)(2,1)S(1)} collective-permute-done((bf16[48,1024]{1,0:T(8,128)(2,1)}, bf16[48,1024]{1,0:T(8,128)(2,1)S(1)}, u32[]{:S(2)}, u32[]{:S(2)}) %collective-permute-start.12) | collective-permute-done | bytes 98336 | tf_op jit(solution)/shard_map/ppermute | solution.py:424
  86.1 1.2 %collective-permute-done.13.refs_3_ = bf16[48,1024]{1,0:T(8,128)(2,1)S(1)} collective-permute-done((bf16[48,1024]{1,0:T(8,128)(2,1)S(1)}, bf16[48,1024]{1,0:T(8,128)(2,1)S(1)}, u32[]{:S(2)}, u32[]{:S(2)}) %collective-permute-start.13) | collective-permute-done | bytes 98336 | tf_op jit(solution)/shard_map/ppermute | solution.py:424
  87.2 0.0 all-to-all-done
  87.3 3.4 %finish.1 = (bf16[128,4096]{1,0:T(8,128)(2,1)}, bf16[128,1024]{1,0:T(8,128)(2,1)}) custom-call(s32[128,1]{1,0:T(8,128)S(1)} %select_select_fusion.target_ref, bf16[128,1024]{1,0:T(8,128)(2,1)S(1)} %copy-done.13, bf16[128,4096]{1,0:T(8,128)(2,1)S(1)} %copy-done.5, f32[128,128]{1,0:T(8,128)S(1)} %copy-done.18, bf16[128,4096]{1,0:T(8,128)(2,1)S(1)} %copy-done.7, ...), custom_call_target="tpu_custom_call" | custom-call | flops 1000 | bytes 1000 | tf_op jit(solution)/shard_map/finish/pallas_call | solution.py:177
  (38 shorter events, 0.1 us)
Async XLA Ops:
  0.6 6.3 %copy-start.21 = (s32[16]{0:T(128)S(1)}, s32[16]{0:T(128)}, u32[]{:S(2)}) copy-start(s32[16]{0:T(128)} %param.15) | copy-start | bytes 196
  0.6 6.3 %copy-start.22 = (s32[128,1]{0,1:T(1,128)S(1)}, s32[128,1]{0,1:T(1,128)}, u32[]{:S(2)}) copy-start(s32[128,1]{0,1:T(1,128)} %param.14) | copy-start | bytes 1540
  0.7 7.1 %copy-start = (bf16[128,8192]{1,0:T(8,128)(2,1)S(1)}, bf16[128,8192]{1,0:T(8,128)(2,1)}, u32[]{:S(2)}) copy-start(bf16[128,8192]{1,0:T(8,128)(2,1)} %hidden_ref.1) | copy-start | bytes 6291460
  3.1 32.0 %collective-permute-start = (bf16[64,9216]{1,0:T(8,128)(2,1)}, bf16[64,9216]{1,0:T(8,128)(2,1)}, u32[]{:S(2)}, u32[]{:S(2)}) collective-permute-start(bf16[64,9216]{1,0:T(8,128)(2,1)} %join.1.refs_14_), channel_id=1, source_target_pairs={{0,4},{1,5},{2,6},{3,7},{4,0},{5,1},{6,2},{7,3},{8,12},{9,13},{10,... | collective-permute-start | bytes 3538952 | tf_op jit(solution)/shard_map/ppermute | solution.py:424
  6.2 28.9 %collective-permute-start.1 = (bf16[64,9216]{1,0:T(8,128)(2,1)}, bf16[64,9216]{1,0:T(8,128)(2,1)S(1)}, u32[]{:S(2)}, u32[]{:S(2)}) collective-permute-start(bf16[64,9216]{1,0:T(8,128)(2,1)} %join.1.refs_14_), channel_id=1, source_target_pairs={{4,8},{5,9},{6,10},{7,11},{8,4},{9,5},{10,6},{11,7},{20,24},{21,25... | collective-permute-start | bytes 3538952 | tf_op jit(solution)/shard_map/ppermute | solution.py:424
  8.9 16.1 %copy-start.20 = (s32[128]{0:T(128)S(1)}, s32[128]{0:T(128)}, u32[]{:S(2)}) copy-start(s32[128]{0:T(128)} %param.13) | copy-start | bytes 1540
  8.9 16.2 %copy-start.5 = (bf16[128,4096]{1,0:T(8,128)(2,1)S(1)}, bf16[128,4096]{1,0:T(8,128)(2,1)}, u32[]{:S(2)}) copy-start(bf16[128,4096]{1,0:T(8,128)(2,1)} %q_ref.3) | copy-start | bytes 3145732
  8.9 6.4 %collective-permute-start.2 = (bf16[16,8192]{1,0:T(8,128)(2,1)}, bf16[16,8192]{1,0:T(8,128)(2,1)S(1)}, u32[]{:S(2)}, u32[]{:S(2)}) collective-permute-start(bf16[16,8192]{1,0:T(8,128)(2,1)} %get-tuple-element.64), channel_id=1, source_target_pairs={{0,1},{1,0},{2,3},{3,2},{4,5},{5,4},{6,7},{7,6},{8,9},{9,8},{10,11... | collective-permute-start | bytes 786440 | tf_op jit(solution)/shard_map/ppermute | solution.py:424
  8.9 9.1 %collective-permute-start.3 = (bf16[16,8192]{1,0:T(8,128)(2,1)S(1)}, bf16[16,8192]{1,0:T(8,128)(2,1)S(1)}, u32[]{:S(2)}, u32[]{:S(2)}) collective-permute-start(bf16[16,8192]{1,0:T(8,128)(2,1)S(1)} %get-tuple-element.65), channel_id=1, source_target_pairs={{0,2},{1,3},{2,0},{3,1},{4,6},{5,7},{6,4},{7,5},{8,10},{9,11},{10,... | collective-permute-start | bytes 786440 | tf_op jit(solution)/shard_map/ppermute | solution.py:424
  10.4 12.6 %collective-permute-start.4 = (bf16[16,8192]{1,0:T(8,128)(2,1)S(1)}, bf16[16,8192]{1,0:T(8,128)(2,1)}, u32[]{:S(2)}, u32[]{:S(2)}) collective-permute-start(bf16[16,8192]{1,0:T(8,128)(2,1)S(1)} %get-tuple-element.66), channel_id=1, source_target_pairs={{0,3},{1,2},{2,1},{3,0},{4,7},{5,6},{6,5},{7,4},{8,11},{9,10},{10,... | collective-permute-start | bytes 786440 | tf_op jit(solution)/shard_map/ppermute | solution.py:424
  15.3 17.6 %copy-start.8 = (bf16[16,8192]{1,0:T(8,128)(2,1)}, bf16[16,8192]{1,0:T(8,128)(2,1)S(1)}, u32[]{:S(2)}) copy-start(bf16[16,8192]{1,0:T(8,128)(2,1)S(1)} %collective-permute-done.2.refs_1_) | copy-start | bytes 786436
  18.0 14.9 %copy-start.10 = (bf16[16,8192]{1,0:T(8,128)(2,1)}, bf16[16,8192]{1,0:T(8,128)(2,1)S(1)}, u32[]{:S(2)}) copy-start(bf16[16,8192]{1,0:T(8,128)(2,1)S(1)} %collective-permute-done.3.refs_2_) | copy-start | bytes 786436
  22.9 16.1 %collective-permute-start.5 = (bf16[16,8192]{1,0:T(8,128)(2,1)}, bf16[16,8192]{1,0:T(8,128)(2,1)}, u32[]{:S(2)}, u32[]{:S(2)}) collective-permute-start(bf16[16,8192]{1,0:T(8,128)(2,1)} %get-tuple-element.76), channel_id=1, source_target_pairs={{0,1},{1,0},{2,3},{3,2},{4,5},{5,4},{6,7},{7,6},{8,9},{9,8},{10,11... | collective-permute-start | bytes 786440 | tf_op jit(solution)/shard_map/ppermute | solution.py:424
  23.5 15.6 %collective-permute-start.6 = (bf16[16,8192]{1,0:T(8,128)(2,1)}, bf16[16,8192]{1,0:T(8,128)(2,1)}, u32[]{:S(2)}, u32[]{:S(2)}) collective-permute-start(bf16[16,8192]{1,0:T(8,128)(2,1)} %get-tuple-element.77), channel_id=1, source_target_pairs={{0,2},{1,3},{2,0},{3,1},{4,6},{5,7},{6,4},{7,5},{8,10},{9,11},{10,... | collective-permute-start | bytes 786440 | tf_op jit(solution)/shard_map/ppermute | solution.py:424
  24.9 14.2 %collective-permute-start.7 = (bf16[16,8192]{1,0:T(8,128)(2,1)}, bf16[16,8192]{1,0:T(8,128)(2,1)}, u32[]{:S(2)}, u32[]{:S(2)}) collective-permute-start(bf16[16,8192]{1,0:T(8,128)(2,1)} %get-tuple-element.78), channel_id=1, source_target_pairs={{0,3},{1,2},{2,1},{3,0},{4,7},{5,6},{6,5},{7,4},{8,11},{9,10},{10,... | collective-permute-start | bytes 786440 | tf_op jit(solution)/shard_map/ppermute | solution.py:424
  25.1 2.2 %copy-start.4 = (bf16[128,16,1024]{2,1,0:T(8,128)(2,1)S(1)}, bf16[128,16,1024]{2,1,0:T(8,128)(2,1)}, u32[]{:S(2)}) copy-start(bf16[128,16,1024]{2,1,0:T(8,128)(2,1)} %cache_ref.1) | copy-start | bytes 12582916
  32.9 1.0 %copy-start.6 = (bf16[128,4096]{1,0:T(8,128)(2,1)}, bf16[128,4096]{1,0:T(8,128)(2,1)S(1)}, u32[]{:S(2)}) copy-start(bf16[128,4096]{1,0:T(8,128)(2,1)S(1)} %get-tuple-element.62.mixed_hbm) | copy-start | bytes 3145732
  33.9 0.6 copy-start.17
  35.1 1.0 %copy-start.2 = (bf16[64,9216]{1,0:T(8,128)(2,1)}, bf16[64,9216]{1,0:T(8,128)(2,1)S(1)}, u32[]{:S(2)}) copy-start(bf16[64,9216]{1,0:T(8,128)(2,1)S(1)} %collective-permute-done.1.weights_hbm) | copy-start | bytes 3538948
  36.1 23.8 %copy-start.1 = (bf16[64,9216]{1,0:T(8,128)(2,1)S(1)}, bf16[64,9216]{1,0:T(8,128)(2,1)}, u32[]{:S(2)}) copy-start(bf16[64,9216]{1,0:T(8,128)(2,1)} %join.1.refs_14_) | copy-start | bytes 3538948
  36.1 23.8 %copy-start.9 = (bf16[16,8192]{1,0:T(8,128)(2,1)S(1)}, bf16[16,8192]{1,0:T(8,128)(2,1)}, u32[]{:S(2)}) copy-start(bf16[16,8192]{1,0:T(8,128)(2,1)} %copy-done.8) | copy-start | bytes 786436
  36.1 23.8 %copy-start.11 = (bf16[16,8192]{1,0:T(8,128)(2,1)S(1)}, bf16[16,8192]{1,0:T(8,128)(2,1)}, u32[]{:S(2)}) copy-start(bf16[16,8192]{1,0:T(8,128)(2,1)} %copy-done.10) | copy-start | bytes 786436
  36.1 23.8 %copy-start.19 = (s32[4]{0:T(128)S(1)}, s32[4]{0:T(128)}, u32[]{:S(2)}) copy-start(s32[4]{0:T(128)} %pad_add_fusion.where_ref) | copy-start | bytes 52
  39.1 33.1 %collective-permute-start.17 = (bf16[64,9216]{1,0:T(8,128)(2,1)}, bf16[64,9216]{1,0:T(8,128)(2,1)S(1)}, u32[]{:S(2)}, u32[]{:S(2)}) collective-permute-start(bf16[64,9216]{1,0:T(8,128)(2,1)} %collective-permute-done.refs_12_), channel_id=1, source_target_pairs={{4,8},{5,9},{6,10},{7,11},{8,4},{9,5},{10,6},{11,7},{20,24},{21,25... | collective-permute-start | bytes 3538952 | tf_op jit(solution)/shard_map/ppermute | solution.py:424
  39.9 32.4 %collective-permute-start.18 = (bf16[64,9216]{1,0:T(8,128)(2,1)}, bf16[64,9216]{1,0:T(8,128)(2,1)S(1)}, u32[]{:S(2)}, u32[]{:S(2)}) collective-permute-start(bf16[64,9216]{1,0:T(8,128)(2,1)} %choose.1.refs_13_), channel_id=1, source_target_pairs={{0,4},{1,5},{2,6},{3,7},{4,0},{5,1},{6,2},{7,3},{8,12},{9,13},{10,... | collective-permute-start | bytes 3538952 | tf_op jit(solution)/shard_map/ppermute | solution.py:424
  43.6 8.4 %collective-permute-start.10 = (bf16[16,8192]{1,0:T(8,128)(2,1)}, bf16[16,8192]{1,0:T(8,128)(2,1)S(1)}, u32[]{:S(2)}, u32[]{:S(2)}) collective-permute-start(bf16[16,8192]{1,0:T(8,128)(2,1)} %get-tuple-element.92), channel_id=1, source_target_pairs={{0,3},{1,2},{2,1},{3,0},{4,7},{5,6},{6,5},{7,4},{8,11},{9,10},{10,... | collective-permute-start | bytes 786440 | tf_op jit(solution)/shard_map/ppermute | solution.py:424
  45.1 7.0 %collective-permute-start.8 = (bf16[16,8192]{1,0:T(8,128)(2,1)}, bf16[16,8192]{1,0:T(8,128)(2,1)S(1)}, u32[]{:S(2)}, u32[]{:S(2)}) collective-permute-start(bf16[16,8192]{1,0:T(8,128)(2,1)} %get-tuple-element.90), channel_id=1, source_target_pairs={{0,1},{1,0},{2,3},{3,2},{4,5},{5,4},{6,7},{7,6},{8,9},{9,8},{10,11... | collective-permute-start | bytes 786440 | tf_op jit(solution)/shard_map/ppermute | solution.py:424
  45.1 13.0 %collective-permute-start.9 = (bf16[16,8192]{1,0:T(8,128)(2,1)}, bf16[16,8192]{1,0:T(8,128)(2,1)S(1)}, u32[]{:S(2)}, u32[]{:S(2)}) collective-permute-start(bf16[16,8192]{1,0:T(8,128)(2,1)} %get-tuple-element.91), channel_id=1, source_target_pairs={{0,2},{1,3},{2,0},{3,1},{4,6},{5,7},{6,4},{7,5},{8,10},{9,11},{10,... | collective-permute-start | bytes 786440 | tf_op jit(solution)/shard_map/ppermute | solution.py:424
  58.1 9.7 %collective-permute-start.14 = (bf16[16,8192]{1,0:T(8,128)(2,1)}, bf16[16,8192]{1,0:T(8,128)(2,1)S(1)}, u32[]{:S(2)}, u32[]{:S(2)}) collective-permute-start(bf16[16,8192]{1,0:T(8,128)(2,1)} %get-tuple-element.113), channel_id=1, source_target_pairs={{0,1},{1,0},{2,3},{3,2},{4,5},{5,4},{6,7},{7,6},{8,9},{9,8},{10,11... | collective-permute-start | bytes 786440 | tf_op jit(solution)/shard_map/ppermute | solution.py:424
  58.1 9.7 %collective-permute-start.15 = (bf16[16,8192]{1,0:T(8,128)(2,1)}, bf16[16,8192]{1,0:T(8,128)(2,1)S(1)}, u32[]{:S(2)}, u32[]{:S(2)}) collective-permute-start(bf16[16,8192]{1,0:T(8,128)(2,1)} %get-tuple-element.114), channel_id=1, source_target_pairs={{0,2},{1,3},{2,0},{3,1},{4,6},{5,7},{6,4},{7,5},{8,10},{9,11},{10,... | collective-permute-start | bytes 786440 | tf_op jit(solution)/shard_map/ppermute | solution.py:424
  59.4 12.8 %collective-permute-start.16 = (bf16[16,8192]{1,0:T(8,128)(2,1)}, bf16[16,8192]{1,0:T(8,128)(2,1)S(1)}, u32[]{:S(2)}, u32[]{:S(2)}) collective-permute-start(bf16[16,8192]{1,0:T(8,128)(2,1)} %get-tuple-element.115), channel_id=1, source_target_pairs={{0,3},{1,2},{2,1},{3,0},{4,7},{5,6},{6,5},{7,4},{8,11},{9,10},{10,... | collective-permute-start | bytes 786440 | tf_op jit(solution)/shard_map/ppermute | solution.py:424
  59.9 1.3 %copy-start.3 = (bf16[64,9216]{1,0:T(8,128)(2,1)S(1)}, bf16[64,9216]{1,0:T(8,128)(2,1)}, u32[]{:S(2)}) copy-start(bf16[64,9216]{1,0:T(8,128)(2,1)} %choose.1.refs_13_) | copy-start | bytes 3538948
  61.2 0.9 %copy-start.12 = (bf16[16,8192]{1,0:T(8,128)(2,1)S(1)}, bf16[16,8192]{1,0:T(8,128)(2,1)}, u32[]{:S(2)}) copy-start(bf16[16,8192]{1,0:T(8,128)(2,1)} %get-tuple-element.71.refs_0_) | copy-start | bytes 786436
  62.1 0.9 %copy-start.15 = (bf16[16,8192]{1,0:T(8,128)(2,1)S(1)}, bf16[16,8192]{1,0:T(8,128)(2,1)}, u32[]{:S(2)}) copy-start(bf16[16,8192]{1,0:T(8,128)(2,1)} %get-tuple-element.85.refs_4_) | copy-start | bytes 786436
  63.1 0.9 %copy-start.16 = (bf16[16,8192]{1,0:T(8,128)(2,1)S(1)}, bf16[16,8192]{1,0:T(8,128)(2,1)}, u32[]{:S(2)}) copy-start(bf16[16,8192]{1,0:T(8,128)(2,1)} %get-tuple-element.97.refs_8_) | copy-start | bytes 786436
  64.1 8.2 %copy-start.14 = (bf16[16,8192]{1,0:T(8,128)(2,1)S(1)}, bf16[16,8192]{1,0:T(8,128)(2,1)}, u32[]{:S(2)}) copy-start(bf16[16,8192]{1,0:T(8,128)(2,1)} %get-tuple-element.112.refs_0_) | copy-start | bytes 786436
  67.8 19.5 %copy-start.13 = (bf16[128,1024]{1,0:T(8,128)(2,1)S(1)}, bf16[128,1024]{1,0:T(8,128)(2,1)}, u32[]{:S(2)}) copy-start(bf16[128,1024]{1,0:T(8,128)(2,1)} %base_ref.1) | copy-start | bytes 786436
  67.8 19.5 %copy-start.18 = (f32[128,128]{1,0:T(8,128)S(1)}, f32[128,128]{1,0:T(8,128)}, u32[]{:S(2)}) copy-start(f32[128,128]{1,0:T(8,128)} %copy-done.17) | copy-start | bytes 196612
  72.2 15.0 %copy-start.7 = (bf16[128,4096]{1,0:T(8,128)(2,1)S(1)}, bf16[128,4096]{1,0:T(8,128)(2,1)}, u32[]{:S(2)}) copy-start(bf16[128,4096]{1,0:T(8,128)(2,1)} %copy-done.6) | copy-start | bytes 3145732
  74.1 13.1 %all-to-all-start = ((bf16[8,16,1024]{2,1,0:T(8,128)(2,1)}), bf16[8,16,1024]{2,1,0:T(8,128)(2,1)S(1)}, u32[]{:S(2)}, u32[]{:S(2)}) async-start(bf16[8,16,1024]{2,1,0:T(8,128)(2,1)} %bitcast.12), calls=%async_computation | async-start | bytes 524288 | tf_op jit(solution)/shard_map/all_to_all | solution.py:429
  77.8 2.3 %collective-permute-start.11 = (bf16[48,1024]{1,0:T(8,128)(2,1)}, bf16[48,1024]{1,0:T(8,128)(2,1)S(1)}, u32[]{:S(2)}, u32[]{:S(2)}) collective-permute-start(bf16[48,1024]{1,0:T(8,128)(2,1)} %get-tuple-element.108), channel_id=1, source_target_pairs={{0,1},{1,0},{2,3},{3,2},{4,5},{5,4},{6,7},{7,6},{8,9},{9,8},{10,11... | collective-permute-start | bytes 294920 | tf_op jit(solution)/shard_map/ppermute | solution.py:424
  78.2 7.8 %collective-permute-start.12 = (bf16[48,1024]{1,0:T(8,128)(2,1)}, bf16[48,1024]{1,0:T(8,128)(2,1)S(1)}, u32[]{:S(2)}, u32[]{:S(2)}) collective-permute-start(bf16[48,1024]{1,0:T(8,128)(2,1)} %get-tuple-element.109), channel_id=1, source_target_pairs={{0,2},{1,3},{2,0},{3,1},{4,6},{5,7},{6,4},{7,5},{8,10},{9,11},{10,... | collective-permute-start | bytes 294920 | tf_op jit(solution)/shard_map/ppermute | solution.py:424
  79.9 7.3 %collective-permute-start.13 = (bf16[48,1024]{1,0:T(8,128)(2,1)S(1)}, bf16[48,1024]{1,0:T(8,128)(2,1)S(1)}, u32[]{:S(2)}, u32[]{:S(2)}) collective-permute-start(bf16[48,1024]{1,0:T(8,128)(2,1)S(1)} %get-tuple-element.110), channel_id=1, source_target_pairs={{0,3},{1,2},{2,1},{3,0},{4,7},{5,6},{6,5},{7,4},{8,11},{9,10},{10,... | collective-permute-start | bytes 294920 | tf_op jit(solution)/shard_map/ppermute | solution.py:424

commit v4 on v3

--- a/solution.py
+++ b/solution.py
@@ -116,11 +116,13 @@
     )(lengths.reshape(rows, 1), queries, cache)
 
 
-def finish_kernel(count, target_ref, base_ref, q_ref, log_ref, mixed_hbm, *refs):
+def finish_kernel(count, target_ref, log_ref, base_hbm, q_hbm, mixed_hbm, *refs):
     pieces, refs = refs[:count], refs[count:]
     attention_hbm, written_hbm, attention_ref, written_ref, stack_ref, mixed_ref = refs[:6]
-    sems, piece_sems, mixed_sems = refs[6:]
+    base_ref, q_ref, sems, piece_sems, mixed_sems = refs[6:]
     rows = base_ref.shape[0]
+    base_copy = pltpu.make_async_copy(base_hbm, base_ref, piece_sems.at[count])
+    base_copy.start()
     total = stack_ref.shape[0]
     arrivals, start = [], 0
     for i, piece in enumerate(pieces):
@@ -133,14 +135,18 @@
     mixes = []
     for head in range(KEY_VALUE_HEADS):
         wide = slice(head * GROUP * HEAD_SIZE, (head + 1) * GROUP * HEAD_SIZE)
-        mixes.append(
+        pair = (
+            pltpu.make_async_copy(q_hbm.at[:, wide], q_ref.at[:, wide], mixed_sems.at[0, head]),
             pltpu.make_async_copy(
-                mixed_hbm.at[:, wide], mixed_ref.at[:, wide], mixed_sems.at[head]
-            )
+                mixed_hbm.at[:, wide], mixed_ref.at[:, wide], mixed_sems.at[1, head]
+            ),
         )
-        mixes[-1].start()
+        for copy in pair:
+            copy.start()
+        mixes.append(pair)
     for arrival in arrivals:
         arrival.wait()
+    base_copy.wait()
     delta = jnp.dot(place, stack_ref[...], preferred_element_type=jnp.float32)
     written_ref[...] = (base_ref[...].astype(jnp.float32) + delta).astype(jnp.bfloat16)
     copies = [pltpu.make_async_copy(written_ref, written_hbm, sems.at[KEY_VALUE_HEADS])]
@@ -152,7 +158,8 @@
         new_key = written_ref[:, own].astype(jnp.float32)
         own = slice(SPLIT + head * HEAD_SIZE, SPLIT + (head + 1) * HEAD_SIZE)
         new_value = written_ref[:, own].astype(jnp.float32)
-        mixes[head].wait()
+        for copy in mixes[head]:
+            copy.wait()
         for i in range(head * GROUP, (head + 1) * GROUP):
             part = slice(i * HEAD_SIZE, (i + 1) * HEAD_SIZE)
             query = q_ref[:, part].astype(jnp.float32)
@@ -176,7 +183,7 @@
     rows = base.shape[0]
     return pl.pallas_call(
         functools.partial(finish_kernel, len(pieces)),
-        in_specs=[VMEM] * 4 + [HBM] * (1 + len(pieces)),
+        in_specs=[VMEM] * 2 + [HBM] * (3 + len(pieces)),
         out_specs=[HBM] * 2,
         out_shape=[
             jax.ShapeDtypeStruct(queries.shape, jnp.bfloat16),
@@ -187,12 +194,14 @@
             pltpu.VMEM(base.shape, jnp.bfloat16),
             pltpu.VMEM((sum(piece.shape[0] for piece in pieces), base.shape[1]), jnp.bfloat16),
             pltpu.VMEM(mixed.shape, mixed.dtype),
+            pltpu.VMEM(base.shape, base.dtype),
+            pltpu.VMEM(queries.shape, queries.dtype),
             pltpu.SemaphoreType.DMA((KEY_VALUE_HEADS + 1,)),
-            pltpu.SemaphoreType.DMA((len(pieces),)),
-            pltpu.SemaphoreType.DMA((KEY_VALUE_HEADS,)),
+            pltpu.SemaphoreType.DMA((len(pieces) + 1,)),
+            pltpu.SemaphoreType.DMA((2, KEY_VALUE_HEADS)),
         ],
-        **options("finish", 1000),
-    )(target.reshape(rows, 1), base, queries, logs, mixed, *pieces)
+        **options("finish", 1000, 60),
+    )(target.reshape(rows, 1), logs, base, queries, mixed, *pieces)
 
 
 def pack_kernel(target_ref, hidden_hbm, *refs):
@@ -332,7 +341,7 @@
         in_specs=[SMEM] + [VMEM] * (3 * PLANE + 3),
         out_specs=[VMEM] * PLANE,
         out_shape=[jax.ShapeDtypeStruct((3 * capacity, out_width), jnp.bfloat16)] * PLANE,
-        **options("early", LONG),
+        **options("early", 1000),
     )(where, *rows, outward, middle, own)
 
 
@@ -461,17 +470,18 @@
     first, own = lax.optimization_barrier((exchange([kept, *first]), own))
     own = exchange(own)
     done = meanwhile()
-    outward, middle, done = lax.optimization_barrier((outward, middle, done))
     middle = choose(where, middle, first)
-    own, near, outward, middle = lax.optimization_barrier((own, near, outward, middle))
+    own, near, middle = lax.optimization_barrier((own, near, middle))
     middle2, swapped = send(outward, to_middle), send(middle, to_outward)
-    near, far = lax.optimization_barrier((exchange(near), far))
+    near, far, done = lax.optimization_barrier((exchange(near), far, done))
     far = exchange(far)
     rows = [*first, *own, *near]
     soon = early(where, rows, outward, middle, weights, capacity)
     soon, where = lax.optimization_barrier((soon, where))
     soon = exchange(soon)
-    last = gather(late(where, far, middle2, swapped, capacity), 2 * PLANE)
+    last = late(where, far, middle2, swapped, capacity)
+    soon, last = lax.optimization_barrier((soon, last))
+    last = gather(last, 2 * PLANE)
     return back, [*soon, last], done
 
 

time: 91.1 us -> 90.9 us (level)
  starting transfers between devices: 21.7 us -> 25.2 us
  local copies, waits for them, and re-layouts: 9.3 us -> 6.73 us
  waiting for transfers between devices: 31.5 us -> 29 us
    ppermute x19, waiting for transfers between devices: 31.5 us -> 24 us  [by_planes(): send = lambda a, pairs: lax.ppermute(a, 'adapter', pairs)]
    all_to_all x1, waiting for transfers between devices: 0.01 us -> 5.08 us  [gather(): lax.all_to_all(parts, 'adapter', 0, 0, axis_index_groups=groups, tiled=True)]
    unnamed x46 -> x68, local copies, waits for them, and re-layouts: 8.97 us -> 6.39 us
    pallas_call x1, Pallas kernels: 3.35 us -> 5.29 us  [finish(): pl.pallas_call(functools.partial(finish_kernel, len(pieces)), in_specs=[V...]
    ppermute x19, starting transfers between devices: 18.3 us -> 20.1 us  [by_planes(): send = lambda a, pairs: lax.ppermute(a, 'adapter', pairs)]
    all_to_all x1, starting transfers between devices: 3.41 us -> 5.14 us  [gather(): lax.all_to_all(parts, 'adapter', 0, 0, axis_index_groups=groups, tiled=True)]
  transfers between devices with their start and end apart: 20 -> 20, of which waited for: 7 -> 9; matrix products, arithmetic and copies ran while one was open for 2% -> 3% of each run, Pallas kernels for 20% -> 20%
where the time goes in v4:
time: 90.9 us; the launch traced here: 90.4 us
  waiting for transfers between devices  29 us (32%)
  Pallas kernels  26.1 us (29%)
  starting transfers between devices  25.2 us (28%)
  local copies, waits for them, and re-layouts  6.73 us (7%)
  other arithmetic  2.23 us (2%)
  between operations  1.05 us (1%)
    ppermute x19, waiting for transfers between devices, by_planes(): send = lambda a, pairs: lax.ppermute(a, 'adapter', pairs)  24 us
    ppermute x19, starting transfers between devices, by_planes(): send = lambda a, pairs: lax.ppermute(a, 'adapter', pairs)  20.1 us
    unnamed x68, local copies, waits for them, and re-layouts  6.39 us
    pallas_call x1, Pallas kernels, cached_attention(): pl.pallas_call(functools.partial(cached_kernel, 16), in_specs=[VMEM] * 3,...  5.63 us
    pallas_call x1, Pallas kernels, finish(): pl.pallas_call(functools.partial(finish_kernel, len(pieces)), in_specs=[V...  5.29 us
    all_to_all x1, starting transfers between devices, gather(): lax.all_to_all(parts, 'adapter', 0, 0, axis_index_groups=groups, tiled=True)  5.14 us
    all_to_all x1, waiting for transfers between devices, gather(): lax.all_to_all(parts, 'adapter', 0, 0, axis_index_groups=groups, tiled=True)  5.08 us
    pallas_call x1, Pallas kernels, pack(): pl.pallas_call(pack_kernel, in_specs=[VMEM, HBM], out_specs=[HBM] * len(h...  4.57 us
  transfers between devices with their start and end apart: 20, of which 9 were waited for; matrix products, arithmetic and copies ran while one was open for 3% of the time, Pallas kernels for 20%

profile of v4, /device:TPU:0, one launch (start us, length us, event | category | flops | bytes accessed | tf_op | source)
XLA Modules:
  0.0 90.4 jit_solution(7044232662620629860)
XLA Ops:
  0.7 0.0 copy-start
  0.7 2.4 %join.1.refs_14_ = bf16[64,9216]{1,0:T(8,128)(2,1)} custom-call(bf16[64,8192]{1,0:T(8,128)(2,1)} %bitcast.45, bf16[64,1024]{1,0:T(8,128)(2,1)} %bitcast.46), custom_call_target="tpu_custom_call" | custom-call | flops 1000 | bytes 1000 | tf_op jit(solution)/shard_map/join/pallas_call | solution.py:308
  3.1 0.7 collective-permute-start.6
  3.9 5.8 %collective-permute-start.10 = (bf16[64,9216]{1,0:T(8,128)(2,1)}, bf16[64,9216]{1,0:T(8,128)(2,1)}, u32[]{:S(2)}, u32[]{:S(2)}) collective-permute-start(bf16[64,9216]{1,0:T(8,128)(2,1)} %join.1.refs_14_), channel_id=1, source_target_pairs={{0,4},{1,5},{2,6},{3,7},{4,0},{5,1},{6,2},{7,3},{8,12},{9,13},{10,... | collective-permute-start | bytes 3538952 | tf_op jit(solution)/shard_map/ppermute | solution.py:433
  9.7 0.1 select_reduce_fusion
  9.8 0.2 convert_reduce_fusion
  10.0 0.6 compare_select_fusion.7
  10.5 0.4 first.1
  10.9 0.1 collective-permute-start
  11.0 1.6 %collective-permute-start.1 = (bf16[16,8192]{1,0:T(8,128)(2,1)S(1)}, bf16[16,8192]{1,0:T(8,128)(2,1)S(1)}, u32[]{:S(2)}, u32[]{:S(2)}) collective-permute-start(bf16[16,8192]{1,0:T(8,128)(2,1)S(1)} %get-tuple-element.63), channel_id=1, source_target_pairs={{0,2},{1,3},{2,0},{3,1},{4,6},{5,7},{6,4},{7,5},{8,10},{9,11},{10,... | collective-permute-start | bytes 786440 | tf_op jit(solution)/shard_map/ppermute | solution.py:433
  12.6 0.3 collective-permute-start.2
  12.9 4.6 %pack.1 = (bf16[16,8192]{1,0:T(8,128)(2,1)}, bf16[16,8192]{1,0:T(8,128)(2,1)}, bf16[16,8192]{1,0:T(8,128)(2,1)}, bf16[16,8192]{1,0:T(8,128)(2,1)}, bf16[16,8192]...) custom-call(s32[1,128]{1,0:T(1,128)} %get-tuple-element.121.target_r, ...), custom_call_target="tpu_custom_call" | custom-call | flops 1000 | bytes 20000000000 | tf_op jit(solution)/shard_map/pack/pallas_call | solution.py:238
  17.5 0.0 collective-permute-done.refs_1_
  17.5 2.7 %collective-permute-done.1.refs_2_ = bf16[16,8192]{1,0:T(8,128)(2,1)S(1)} collective-permute-done((bf16[16,8192]{1,0:T(8,128)(2,1)S(1)}, bf16[16,8192]{1,0:T(8,128)(2,1)S(1)}, u32[]{:S(2)}, u32[]{:S(2)}) %collective-permute-start.1) | collective-permute-done | bytes 262176 | tf_op jit(solution)/shard_map/ppermute | solution.py:433
  20.2 4.7 %collective-permute-done.2.refs_3_ = bf16[16,8192]{1,0:T(8,128)(2,1)S(1)} collective-permute-done((bf16[16,8192]{1,0:T(8,128)(2,1)S(1)}, bf16[16,8192]{1,0:T(8,128)(2,1)S(1)}, u32[]{:S(2)}, u32[]{:S(2)}) %collective-permute-start.2) | collective-permute-done | bytes 262176 | tf_op jit(solution)/shard_map/ppermute | solution.py:433
  24.9 0.7 collective-permute-start.3
  25.6 1.5 %collective-permute-start.4 = (bf16[16,8192]{1,0:T(8,128)(2,1)}, bf16[16,8192]{1,0:T(8,128)(2,1)S(1)}, u32[]{:S(2)}, u32[]{:S(2)}) collective-permute-start(bf16[16,8192]{1,0:T(8,128)(2,1)} %get-tuple-element.71), channel_id=1, source_target_pairs={{0,2},{1,3},{2,0},{3,1},{4,6},{5,7},{6,4},{7,5},{8,10},{9,11},{10,... | collective-permute-start | bytes 786440 | tf_op jit(solution)/shard_map/ppermute | solution.py:433
  27.1 0.0 collective-permute-start.5
  27.1 0.7 pad_add_fusion.where_ref
  27.7 0.0 collective-permute-done.6.weights_hbm
  27.8 1.0 %copy-done.2 = bf16[64,9216]{1,0:T(8,128)(2,1)} copy-done((bf16[64,9216]{1,0:T(8,128)(2,1)}, bf16[64,9216]{1,0:T(8,128)(2,1)S(1)}, u32[]{:S(2)}) %copy-start.2) | copy-done | bytes 1179672
  28.8 2.8 %choose.1.refs_13_ = bf16[64,9216]{1,0:T(8,128)(2,1)} custom-call(s32[4]{0:T(128)} %pad_add_fusion.where_ref, bf16[64,9216]{1,0:T(8,128)(2,1)} %copy-done.2, bf16[16,8192]{1,0:T(8,128)(2,1)} %get-tuple-element.77.refs_0_, bf16[16,8192]{1,0:T(8,128)(2,1)} %copy-done.7, bf16[16,8192]{1,0:T(8,128)(2,1)} %copy-done.9, ...), custom_call_target="tpu_custom_call", output_to_operand_aliasing={{}: (1, {})} | custom-call | flops 1000 | bytes 1000 | tf_op jit(solution)/shard_map/choose/pallas_call | solution.py:405
  31.7 0.0 collective-permute-done.3.refs_5_
  31.7 0.7 copy-done.17
  32.4 2.6 %collective-permute-done.4.refs_6_ = bf16[16,8192]{1,0:T(8,128)(2,1)S(1)} collective-permute-done((bf16[16,8192]{1,0:T(8,128)(2,1)}, bf16[16,8192]{1,0:T(8,128)(2,1)S(1)}, u32[]{:S(2)}, u32[]{:S(2)}) %collective-permute-start.4) | collective-permute-done | bytes 262176 | tf_op jit(solution)/shard_map/ppermute | solution.py:433
  35.0 0.7 copy-done.19
  35.7 3.1 %collective-permute-done.5.refs_7_ = bf16[16,8192]{1,0:T(8,128)(2,1)} collective-permute-done((bf16[16,8192]{1,0:T(8,128)(2,1)}, bf16[16,8192]{1,0:T(8,128)(2,1)}, u32[]{:S(2)}, u32[]{:S(2)}) %collective-permute-start.5) | collective-permute-done | bytes 262176 | tf_op jit(solution)/shard_map/ppermute | solution.py:433
  38.8 0.7 collective-permute-start.18
  39.4 0.0 collective-permute-done.10.refs_12_
  39.5 0.7 collective-permute-start.17
  40.2 0.2 collective-permute-start.7
  40.4 1.5 %collective-permute-start.8 = (bf16[16,8192]{1,0:T(8,128)(2,1)}, bf16[16,8192]{1,0:T(8,128)(2,1)}, u32[]{:S(2)}, u32[]{:S(2)}) collective-permute-start(bf16[16,8192]{1,0:T(8,128)(2,1)} %get-tuple-element.83), channel_id=1, source_target_pairs={{0,2},{1,3},{2,0},{3,1},{4,6},{5,7},{6,4},{7,5},{8,10},{9,11},{10,... | collective-permute-start | bytes 786440 | tf_op jit(solution)/shard_map/ppermute | solution.py:433
  41.9 0.3 collective-permute-start.9
  42.1 0.1 copy.27.length_ref
  42.3 0.0 copy-start.4
  42.3 2.2 %copy-done.4 = bf16[128,16,1024]{2,1,0:T(8,128)(2,1)S(1)} copy-done((bf16[128,16,1024]{2,1,0:T(8,128)(2,1)S(1)}, bf16[128,16,1024]{2,1,0:T(8,128)(2,1)}, u32[]{:S(2)}) %copy-start.4) | copy-done | bytes 4194328
  44.5 0.0 copy-start.13
  44.5 0.0 copy-start.15
  44.6 5.6 %cached.1 = (bf16[128,4096]{1,0:T(8,128)(2,1)S(1)}, f32[128,128]{1,0:T(8,128)S(1)}) custom-call(s32[128,1]{1,0:T(8,128)S(1)} %copy.27.length_ref, bf16[128,4096]{1,0:T(8,128)(2,1)S(1)} %copy-done.5, bf16[128,16,1024]{2,1,0:T(8,128)(2,1)S(1)} %copy-done.4), custom_call_target="tpu_custom_call" | custom-call | flops 1000 | bytes 20000000000 | tf_op jit(solution)/shard_map/cached/pallas_call | solution.py:107
  50.2 1.0 %copy-done.6 = bf16[128,4096]{1,0:T(8,128)(2,1)} copy-done((bf16[128,4096]{1,0:T(8,128)(2,1)}, bf16[128,4096]{1,0:T(8,128)(2,1)S(1)}, u32[]{:S(2)}) %copy-start.6) | copy-done | bytes 1048600
  51.2 0.0 collective-permute-done.7.refs_9_
  51.2 0.0 collective-permute-done.8.refs_10_
  51.2 3.3 %collective-permute-done.9.refs_11_ = bf16[16,8192]{1,0:T(8,128)(2,1)} collective-permute-done((bf16[16,8192]{1,0:T(8,128)(2,1)}, bf16[16,8192]{1,0:T(8,128)(2,1)}, u32[]{:S(2)}, u32[]{:S(2)}) %collective-permute-start.9) | collective-permute-done | bytes 262176 | tf_op jit(solution)/shard_map/ppermute | solution.py:433
  54.5 0.5 collective-permute-start.14
  55.0 1.5 %collective-permute-start.15 = (bf16[16,8192]{1,0:T(8,128)(2,1)S(1)}, bf16[16,8192]{1,0:T(8,128)(2,1)S(1)}, u32[]{:S(2)}, u32[]{:S(2)}) collective-permute-start(bf16[16,8192]{1,0:T(8,128)(2,1)S(1)} %copy-done.30), channel_id=1, source_target_pairs={{0,2},{1,3},{2,0},{3,1},{4,6},{5,7},{6,4},{7,5},{8,10},{9,11},{10,... | collective-permute-start | bytes 786440 | tf_op jit(solution)/shard_map/ppermute | solution.py:433
  56.5 0.0 collective-permute-start.16
  56.6 3.0 %early.1 = (bf16[48,1024]{1,0:T(8,128)(2,1)S(1)}, bf16[48,1024]{1,0:T(8,128)(2,1)S(1)}, bf16[48,1024]{1,0:T(8,128)(2,1)S(1)}, bf16[48,1024]{1,0:T(8,128)(2,1)S(1)}) custom-call(s32[4]{0:T(128)S(1)} %copy-done.23, bf16[16,8192]{1,0:T(8,128)(2,1)S(1)} %copy-done.13, bf16[16,8192]{1,0:T(8,128)(2,1)S(1)} %copy-done.8, bf16[16,8192]{1,0:T(8,128)(2,1)S(1)} %copy-done.10, ...), custom_call_target="tpu_custom_call" | custom-call | flops 1000 | bytes 1000 | tf_op jit(solution)/shard_map/early/pallas_call | solution.py:339
  59.6 0.0 collective-permute-done.14.refs_1_
  59.6 0.7 collective-permute-start.11
  60.3 3.8 %collective-permute-done.15.refs_2_ = bf16[16,8192]{1,0:T(8,128)(2,1)S(1)} collective-permute-done((bf16[16,8192]{1,0:T(8,128)(2,1)S(1)}, bf16[16,8192]{1,0:T(8,128)(2,1)S(1)}, u32[]{:S(2)}, u32[]{:S(2)}) %collective-permute-start.15) | collective-permute-done | bytes 262176 | tf_op jit(solution)/shard_map/ppermute | solution.py:433
  64.1 1.5 %collective-permute-start.12 = (bf16[48,1024]{1,0:T(8,128)(2,1)S(1)}, bf16[48,1024]{1,0:T(8,128)(2,1)S(1)}, u32[]{:S(2)}, u32[]{:S(2)}) collective-permute-start(bf16[48,1024]{1,0:T(8,128)(2,1)S(1)} %get-tuple-element.108), channel_id=1, source_target_pairs={{0,2},{1,3},{2,0},{3,1},{4,6},{5,7},{6,4},{7,5},{8,10},{9,11},{10,... | collective-permute-start | bytes 294920 | tf_op jit(solution)/shard_map/ppermute | solution.py:433
  65.6 3.1 %collective-permute-done.16.refs_3_ = bf16[16,8192]{1,0:T(8,128)(2,1)S(1)} collective-permute-done((bf16[16,8192]{1,0:T(8,128)(2,1)S(1)}, bf16[16,8192]{1,0:T(8,128)(2,1)S(1)}, u32[]{:S(2)}, u32[]{:S(2)}) %collective-permute-start.16) | collective-permute-done | bytes 262176 | tf_op jit(solution)/shard_map/ppermute | solution.py:433
  68.7 1.9 %collective-permute-start.13 = (bf16[48,1024]{1,0:T(8,128)(2,1)S(1)}, bf16[48,1024]{1,0:T(8,128)(2,1)S(1)}, u32[]{:S(2)}, u32[]{:S(2)}) collective-permute-start(bf16[48,1024]{1,0:T(8,128)(2,1)S(1)} %get-tuple-element.109), channel_id=1, source_target_pairs={{0,3},{1,2},{2,1},{3,0},{4,7},{5,6},{6,5},{7,4},{8,11},{9,10},{10,... | collective-permute-start | bytes 294920 | tf_op jit(solution)/shard_map/ppermute | solution.py:433
  70.7 0.0 collective-permute-done.18.refs_5_
  70.7 0.0 collective-permute-done.17.refs_4_
  70.7 1.9 %late.1 = bf16[128,1024]{1,0:T(8,128)(2,1)} custom-call(s32[4]{0:T(128)S(1)} %copy-done.23, bf16[16,8192]{1,0:T(8,128)(2,1)S(1)} %copy-done.14, bf16[16,8192]{1,0:T(8,128)(2,1)S(1)} %collective-permute-done.14.refs_1_, bf16[16,8192]{1,0:T(8,128)(2,1)S(1)} %collective-permute-done.15.refs_2_, bf16[16,8192]{1,0:T(8,128)(2,1)S(1)} %collective-permute-done.16.refs_3_, ...), custom_call_target="tpu_custom_call" | custom-call | tf_op jit(solution)/shard_map/late/pallas_call | solution.py:373
  72.6 0.6 collective-permute-done.13.refs_3_
  73.2 5.1 %all-to-all-start = ((bf16[8,16,1024]{2,1,0:T(8,128)(2,1)}), bf16[8,16,1024]{2,1,0:T(8,128)(2,1)S(1)}, u32[]{:S(2)}, u32[]{:S(2)}) async-start(bf16[8,16,1024]{2,1,0:T(8,128)(2,1)} %bitcast.12), calls=%async_computation | async-start | bytes 524288 | tf_op jit(solution)/shard_map/all_to_all | solution.py:438
  78.3 0.1 copy.24
  78.5 0.1 copy.20
  78.6 0.7 select_select_fusion.target_ref
  79.3 5.1 %all-to-all-done = bf16[8,16,1024]{2,1,0:T(8,128)(2,1)S(1)} async-done(((bf16[8,16,1024]{2,1,0:T(8,128)(2,1)}), bf16[8,16,1024]{2,1,0:T(8,128)(2,1)S(1)}, u32[]{:S(2)}, u32[]{:S(2)}) %all-to-all-start) | async-done | bytes 262176 | tf_op jit(solution)/shard_map/all_to_all | solution.py:438
  84.4 0.7 copy-done.24
  85.1 5.3 %finish.1 = (bf16[128,4096]{1,0:T(8,128)(2,1)}, bf16[128,1024]{1,0:T(8,128)(2,1)}) custom-call(s32[128,1]{1,0:T(8,128)} %select_select_fusion.target_ref, f32[128,128]{1,0:T(8,128)} %copy-done.22, bf16[128,1024]{1,0:T(8,128)(2,1)} %base_hbm.1, bf16[128,4096]{1,0:T(8,128)(2,1)} %q_hbm.1, bf16[128,4096]{1,0:T(8,128)(2,1)} %copy-done.6, ...), custom_call_target="tpu_custom_call" | custom-call | flops 1000 | bytes 1000 | tf_op jit(solution)/shard_map/finish/pallas_call | solution.py:184
  (60 shorter events, 0.1 us)
Async XLA Ops:
  0.6 9.1 %copy-start.32 = (s32[16]{0:T(128)S(1)}, s32[16]{0:T(128)}, u32[]{:S(2)}) copy-start(s32[16]{0:T(128)} %param.15) | copy-start | bytes 196
  0.6 9.1 %copy-start.33 = (s32[128,1]{0,1:T(1,128)S(1)}, s32[128,1]{0,1:T(1,128)}, u32[]{:S(2)}) copy-start(s32[128,1]{0,1:T(1,128)} %param.14) | copy-start | bytes 1540
  0.7 9.9 %copy-start = (bf16[128,8192]{1,0:T(8,128)(2,1)S(1)}, bf16[128,8192]{1,0:T(8,128)(2,1)}, u32[]{:S(2)}) copy-start(bf16[128,8192]{1,0:T(8,128)(2,1)} %hidden_ref.1) | copy-start | bytes 6291460
  3.1 24.6 %collective-permute-start.6 = (bf16[64,9216]{1,0:T(8,128)(2,1)}, bf16[64,9216]{1,0:T(8,128)(2,1)S(1)}, u32[]{:S(2)}, u32[]{:S(2)}) collective-permute-start(bf16[64,9216]{1,0:T(8,128)(2,1)} %join.1.refs_14_), channel_id=1, source_target_pairs={{4,8},{5,9},{6,10},{7,11},{8,4},{9,5},{10,6},{11,7},{20,24},{21,25... | collective-permute-start | bytes 3538952 | tf_op jit(solution)/shard_map/ppermute | solution.py:433
  3.9 35.6 %collective-permute-start.10 = (bf16[64,9216]{1,0:T(8,128)(2,1)}, bf16[64,9216]{1,0:T(8,128)(2,1)}, u32[]{:S(2)}, u32[]{:S(2)}) collective-permute-start(bf16[64,9216]{1,0:T(8,128)(2,1)} %join.1.refs_14_), channel_id=1, source_target_pairs={{0,4},{1,5},{2,6},{3,7},{4,0},{5,1},{6,2},{7,3},{8,12},{9,13},{10,... | collective-permute-start | bytes 3538952 | tf_op jit(solution)/shard_map/ppermute | solution.py:433
  10.9 6.5 %collective-permute-start = (bf16[16,8192]{1,0:T(8,128)(2,1)S(1)}, bf16[16,8192]{1,0:T(8,128)(2,1)S(1)}, u32[]{:S(2)}, u32[]{:S(2)}) collective-permute-start(bf16[16,8192]{1,0:T(8,128)(2,1)S(1)} %get-tuple-element.62), channel_id=1, source_target_pairs={{0,1},{1,0},{2,3},{3,2},{4,5},{5,4},{6,7},{7,6},{8,9},{9,8},{10,11... | collective-permute-start | bytes 786440 | tf_op jit(solution)/shard_map/ppermute | solution.py:433
  11.0 9.2 %collective-permute-start.1 = (bf16[16,8192]{1,0:T(8,128)(2,1)S(1)}, bf16[16,8192]{1,0:T(8,128)(2,1)S(1)}, u32[]{:S(2)}, u32[]{:S(2)}) collective-permute-start(bf16[16,8192]{1,0:T(8,128)(2,1)S(1)} %get-tuple-element.63), channel_id=1, source_target_pairs={{0,2},{1,3},{2,0},{3,1},{4,6},{5,7},{6,4},{7,5},{8,10},{9,11},{10,... | collective-permute-start | bytes 786440 | tf_op jit(solution)/shard_map/ppermute | solution.py:433
  12.6 12.3 %collective-permute-start.2 = (bf16[16,8192]{1,0:T(8,128)(2,1)S(1)}, bf16[16,8192]{1,0:T(8,128)(2,1)S(1)}, u32[]{:S(2)}, u32[]{:S(2)}) collective-permute-start(bf16[16,8192]{1,0:T(8,128)(2,1)S(1)} %get-tuple-element.64), channel_id=1, source_target_pairs={{0,3},{1,2},{2,1},{3,0},{4,7},{5,6},{6,5},{7,4},{8,11},{9,10},{10,... | collective-permute-start | bytes 786440 | tf_op jit(solution)/shard_map/ppermute | solution.py:433
  17.5 10.3 %copy-start.7 = (bf16[16,8192]{1,0:T(8,128)(2,1)}, bf16[16,8192]{1,0:T(8,128)(2,1)S(1)}, u32[]{:S(2)}) copy-start(bf16[16,8192]{1,0:T(8,128)(2,1)S(1)} %collective-permute-done.refs_1_) | copy-start | bytes 786436
  20.2 7.6 %copy-start.9 = (bf16[16,8192]{1,0:T(8,128)(2,1)}, bf16[16,8192]{1,0:T(8,128)(2,1)S(1)}, u32[]{:S(2)}) copy-start(bf16[16,8192]{1,0:T(8,128)(2,1)S(1)} %collective-permute-done.1.refs_2_) | copy-start | bytes 786436
  24.9 2.9 %copy-start.11 = (bf16[16,8192]{1,0:T(8,128)(2,1)}, bf16[16,8192]{1,0:T(8,128)(2,1)S(1)}, u32[]{:S(2)}) copy-start(bf16[16,8192]{1,0:T(8,128)(2,1)S(1)} %collective-permute-done.2.refs_3_) | copy-start | bytes 786436
  24.9 6.7 %collective-permute-start.3 = (bf16[16,8192]{1,0:T(8,128)(2,1)}, bf16[16,8192]{1,0:T(8,128)(2,1)S(1)}, u32[]{:S(2)}, u32[]{:S(2)}) collective-permute-start(bf16[16,8192]{1,0:T(8,128)(2,1)} %get-tuple-element.70), channel_id=1, source_target_pairs={{0,1},{1,0},{2,3},{3,2},{4,5},{5,4},{6,7},{7,6},{8,9},{9,8},{10,11... | collective-permute-start | bytes 786440 | tf_op jit(solution)/shard_map/ppermute | solution.py:433
  25.6 9.4 %collective-permute-start.4 = (bf16[16,8192]{1,0:T(8,128)(2,1)}, bf16[16,8192]{1,0:T(8,128)(2,1)S(1)}, u32[]{:S(2)}, u32[]{:S(2)}) collective-permute-start(bf16[16,8192]{1,0:T(8,128)(2,1)} %get-tuple-element.71), channel_id=1, source_target_pairs={{0,2},{1,3},{2,0},{3,1},{4,6},{5,7},{6,4},{7,5},{8,10},{9,11},{10,... | collective-permute-start | bytes 786440 | tf_op jit(solution)/shard_map/ppermute | solution.py:433
  27.1 11.7 %collective-permute-start.5 = (bf16[16,8192]{1,0:T(8,128)(2,1)}, bf16[16,8192]{1,0:T(8,128)(2,1)}, u32[]{:S(2)}, u32[]{:S(2)}) collective-permute-start(bf16[16,8192]{1,0:T(8,128)(2,1)} %get-tuple-element.72), channel_id=1, source_target_pairs={{0,3},{1,2},{2,1},{3,0},{4,7},{5,6},{6,5},{7,4},{8,11},{9,10},{10,... | collective-permute-start | bytes 786440 | tf_op jit(solution)/shard_map/ppermute | solution.py:433
  27.7 14.4 %copy-start.28 = (s32[128]{0:T(128)S(1)}, s32[128]{0:T(128)}, u32[]{:S(2)}) copy-start(s32[128]{0:T(128)} %param.13) | copy-start | bytes 1540
  27.7 14.5 %copy-start.5 = (bf16[128,4096]{1,0:T(8,128)(2,1)S(1)}, bf16[128,4096]{1,0:T(8,128)(2,1)}, u32[]{:S(2)}) copy-start(bf16[128,4096]{1,0:T(8,128)(2,1)} %q_hbm.1) | copy-start | bytes 3145732
  27.8 1.0 %copy-start.2 = (bf16[64,9216]{1,0:T(8,128)(2,1)}, bf16[64,9216]{1,0:T(8,128)(2,1)S(1)}, u32[]{:S(2)}) copy-start(bf16[64,9216]{1,0:T(8,128)(2,1)S(1)} %collective-permute-done.6.weights_hbm) | copy-start | bytes 3538948
  31.7 0.7 copy-start.17
  35.0 0.7 copy-start.19
  38.8 31.9 %collective-permute-start.18 = (bf16[64,9216]{1,0:T(8,128)(2,1)}, bf16[64,9216]{1,0:T(8,128)(2,1)S(1)}, u32[]{:S(2)}, u32[]{:S(2)}) collective-permute-start(bf16[64,9216]{1,0:T(8,128)(2,1)} %choose.1.refs_13_), channel_id=1, source_target_pairs={{0,4},{1,5},{2,6},{3,7},{4,0},{5,1},{6,2},{7,3},{8,12},{9,13},{10,... | collective-permute-start | bytes 3538952 | tf_op jit(solution)/shard_map/ppermute | solution.py:433
  39.5 31.2 %collective-permute-start.17 = (bf16[64,9216]{1,0:T(8,128)(2,1)}, bf16[64,9216]{1,0:T(8,128)(2,1)S(1)}, u32[]{:S(2)}, u32[]{:S(2)}) collective-permute-start(bf16[64,9216]{1,0:T(8,128)(2,1)} %collective-permute-done.10.refs_12_), channel_id=1, source_target_pairs={{4,8},{5,9},{6,10},{7,11},{8,4},{9,5},{10,6},{11,7},{20,24},{21,25... | collective-permute-start | bytes 3538952 | tf_op jit(solution)/shard_map/ppermute | solution.py:433
  40.2 11.0 %collective-permute-start.7 = (bf16[16,8192]{1,0:T(8,128)(2,1)}, bf16[16,8192]{1,0:T(8,128)(2,1)}, u32[]{:S(2)}, u32[]{:S(2)}) collective-permute-start(bf16[16,8192]{1,0:T(8,128)(2,1)} %get-tuple-element.82), channel_id=1, source_target_pairs={{0,1},{1,0},{2,3},{3,2},{4,5},{5,4},{6,7},{7,6},{8,9},{9,8},{10,11... | collective-permute-start | bytes 786440 | tf_op jit(solution)/shard_map/ppermute | solution.py:433
  40.4 10.8 %collective-permute-start.8 = (bf16[16,8192]{1,0:T(8,128)(2,1)}, bf16[16,8192]{1,0:T(8,128)(2,1)}, u32[]{:S(2)}, u32[]{:S(2)}) collective-permute-start(bf16[16,8192]{1,0:T(8,128)(2,1)} %get-tuple-element.83), channel_id=1, source_target_pairs={{0,2},{1,3},{2,0},{3,1},{4,6},{5,7},{6,4},{7,5},{8,10},{9,11},{10,... | collective-permute-start | bytes 786440 | tf_op jit(solution)/shard_map/ppermute | solution.py:433
  41.9 12.6 %collective-permute-start.9 = (bf16[16,8192]{1,0:T(8,128)(2,1)}, bf16[16,8192]{1,0:T(8,128)(2,1)}, u32[]{:S(2)}, u32[]{:S(2)}) collective-permute-start(bf16[16,8192]{1,0:T(8,128)(2,1)} %get-tuple-element.84), channel_id=1, source_target_pairs={{0,3},{1,2},{2,1},{3,0},{4,7},{5,6},{6,5},{7,4},{8,11},{9,10},{10,... | collective-permute-start | bytes 786440 | tf_op jit(solution)/shard_map/ppermute | solution.py:433
  42.3 2.2 %copy-start.4 = (bf16[128,16,1024]{2,1,0:T(8,128)(2,1)S(1)}, bf16[128,16,1024]{2,1,0:T(8,128)(2,1)}, u32[]{:S(2)}) copy-start(bf16[128,16,1024]{2,1,0:T(8,128)(2,1)} %cache_ref.1) | copy-start | bytes 12582916
  44.5 10.0 %copy-start.31 = (bf16[16,8192]{1,0:T(8,128)(2,1)S(1)}, bf16[16,8192]{1,0:T(8,128)(2,1)}, u32[]{:S(2)}) copy-start(bf16[16,8192]{1,0:T(8,128)(2,1)} %get-tuple-element.112) | copy-start | bytes 786436
  44.5 10.5 %copy-start.30 = (bf16[16,8192]{1,0:T(8,128)(2,1)S(1)}, bf16[16,8192]{1,0:T(8,128)(2,1)}, u32[]{:S(2)}) copy-start(bf16[16,8192]{1,0:T(8,128)(2,1)} %get-tuple-element.113) | copy-start | bytes 786436
  44.5 12.0 %copy-start.29 = (bf16[16,8192]{1,0:T(8,128)(2,1)S(1)}, bf16[16,8192]{1,0:T(8,128)(2,1)}, u32[]{:S(2)}) copy-start(bf16[16,8192]{1,0:T(8,128)(2,1)} %get-tuple-element.114) | copy-start | bytes 786436
  44.5 12.0 %copy-start.1 = (bf16[64,9216]{1,0:T(8,128)(2,1)S(1)}, bf16[64,9216]{1,0:T(8,128)(2,1)}, u32[]{:S(2)}) copy-start(bf16[64,9216]{1,0:T(8,128)(2,1)} %join.1.refs_14_) | copy-start | bytes 3538948
  44.5 12.0 %copy-start.3 = (bf16[64,9216]{1,0:T(8,128)(2,1)S(1)}, bf16[64,9216]{1,0:T(8,128)(2,1)}, u32[]{:S(2)}) copy-start(bf16[64,9216]{1,0:T(8,128)(2,1)} %choose.1.refs_13_) | copy-start | bytes 3538948
  44.5 12.0 %copy-start.8 = (bf16[16,8192]{1,0:T(8,128)(2,1)S(1)}, bf16[16,8192]{1,0:T(8,128)(2,1)}, u32[]{:S(2)}) copy-start(bf16[16,8192]{1,0:T(8,128)(2,1)} %copy-done.7) | copy-start | bytes 786436
  44.5 12.0 %copy-start.10 = (bf16[16,8192]{1,0:T(8,128)(2,1)S(1)}, bf16[16,8192]{1,0:T(8,128)(2,1)}, u32[]{:S(2)}) copy-start(bf16[16,8192]{1,0:T(8,128)(2,1)} %copy-done.9) | copy-start | bytes 786436
  44.5 12.0 %copy-start.12 = (bf16[16,8192]{1,0:T(8,128)(2,1)S(1)}, bf16[16,8192]{1,0:T(8,128)(2,1)}, u32[]{:S(2)}) copy-start(bf16[16,8192]{1,0:T(8,128)(2,1)} %copy-done.11) | copy-start | bytes 786436
  44.5 12.0 %copy-start.13 = (bf16[16,8192]{1,0:T(8,128)(2,1)S(1)}, bf16[16,8192]{1,0:T(8,128)(2,1)}, u32[]{:S(2)}) copy-start(bf16[16,8192]{1,0:T(8,128)(2,1)} %get-tuple-element.77.refs_0_) | copy-start | bytes 786436
  44.5 12.0 %copy-start.15 = (bf16[16,8192]{1,0:T(8,128)(2,1)S(1)}, bf16[16,8192]{1,0:T(8,128)(2,1)}, u32[]{:S(2)}) copy-start(bf16[16,8192]{1,0:T(8,128)(2,1)} %get-tuple-element.93.refs_4_) | copy-start | bytes 786436
  44.5 12.0 %copy-start.16 = (bf16[16,8192]{1,0:T(8,128)(2,1)S(1)}, bf16[16,8192]{1,0:T(8,128)(2,1)}, u32[]{:S(2)}) copy-start(bf16[16,8192]{1,0:T(8,128)(2,1)} %get-tuple-element.97.refs_8_) | copy-start | bytes 786436
  44.5 12.0 %copy-start.18 = (bf16[16,8192]{1,0:T(8,128)(2,1)S(1)}, bf16[16,8192]{1,0:T(8,128)(2,1)}, u32[]{:S(2)}) copy-start(bf16[16,8192]{1,0:T(8,128)(2,1)} %copy-done.17) | copy-start | bytes 786436
  44.5 12.0 %copy-start.20 = (bf16[16,8192]{1,0:T(8,128)(2,1)S(1)}, bf16[16,8192]{1,0:T(8,128)(2,1)}, u32[]{:S(2)}) copy-start(bf16[16,8192]{1,0:T(8,128)(2,1)} %copy-done.19) | copy-start | bytes 786436
  44.6 12.0 %copy-start.23 = (s32[4]{0:T(128)S(1)}, s32[4]{0:T(128)}, u32[]{:S(2)}) copy-start(s32[4]{0:T(128)} %pad_add_fusion.where_ref) | copy-start | bytes 52
  50.2 1.0 %copy-start.6 = (bf16[128,4096]{1,0:T(8,128)(2,1)}, bf16[128,4096]{1,0:T(8,128)(2,1)S(1)}, u32[]{:S(2)}) copy-start(bf16[128,4096]{1,0:T(8,128)(2,1)S(1)} %get-tuple-element.92.mixed_hbm) | copy-start | bytes 3145732
  51.2 8.4 %copy-start.22 = (f32[128,128]{1,0:T(8,128)}, f32[128,128]{1,0:T(8,128)S(1)}, u32[]{:S(2)}) copy-start(f32[128,128]{1,0:T(8,128)S(1)} %get-tuple-element.91.log_ref) | copy-start | bytes 196612
  54.5 16.2 %copy-start.14 = (bf16[16,8192]{1,0:T(8,128)(2,1)S(1)}, bf16[16,8192]{1,0:T(8,128)(2,1)}, u32[]{:S(2)}) copy-start(bf16[16,8192]{1,0:T(8,128)(2,1)} %get-tuple-element.111.refs_0_) | copy-start | bytes 786436
  54.5 5.1 %collective-permute-start.14 = (bf16[16,8192]{1,0:T(8,128)(2,1)S(1)}, bf16[16,8192]{1,0:T(8,128)(2,1)S(1)}, u32[]{:S(2)}, u32[]{:S(2)}) collective-permute-start(bf16[16,8192]{1,0:T(8,128)(2,1)S(1)} %copy-done.31), channel_id=1, source_target_pairs={{0,1},{1,0},{2,3},{3,2},{4,5},{5,4},{6,7},{7,6},{8,9},{9,8},{10,11... | collective-permute-start | bytes 786440 | tf_op jit(solution)/shard_map/ppermute | solution.py:433
  55.0 9.2 %collective-permute-start.15 = (bf16[16,8192]{1,0:T(8,128)(2,1)S(1)}, bf16[16,8192]{1,0:T(8,128)(2,1)S(1)}, u32[]{:S(2)}, u32[]{:S(2)}) collective-permute-start(bf16[16,8192]{1,0:T(8,128)(2,1)S(1)} %copy-done.30), channel_id=1, source_target_pairs={{0,2},{1,3},{2,0},{3,1},{4,6},{5,7},{6,4},{7,5},{8,10},{9,11},{10,... | collective-permute-start | bytes 786440 | tf_op jit(solution)/shard_map/ppermute | solution.py:433
  56.5 12.3 %collective-permute-start.16 = (bf16[16,8192]{1,0:T(8,128)(2,1)S(1)}, bf16[16,8192]{1,0:T(8,128)(2,1)S(1)}, u32[]{:S(2)}, u32[]{:S(2)}) collective-permute-start(bf16[16,8192]{1,0:T(8,128)(2,1)S(1)} %copy-done.29), channel_id=1, source_target_pairs={{0,3},{1,2},{2,1},{3,0},{4,7},{5,6},{6,5},{7,4},{8,11},{9,10},{10,... | collective-permute-start | bytes 786440 | tf_op jit(solution)/shard_map/ppermute | solution.py:433
  59.6 13.0 %copy-start.21 = (bf16[48,1024]{1,0:T(8,128)(2,1)}, bf16[48,1024]{1,0:T(8,128)(2,1)S(1)}, u32[]{:S(2)}) copy-start(bf16[48,1024]{1,0:T(8,128)(2,1)S(1)} %get-tuple-element.115.refs_0_) | copy-start | bytes 294916
  59.6 12.9 %collective-permute-start.11 = (bf16[48,1024]{1,0:T(8,128)(2,1)S(1)}, bf16[48,1024]{1,0:T(8,128)(2,1)S(1)}, u32[]{:S(2)}, u32[]{:S(2)}) collective-permute-start(bf16[48,1024]{1,0:T(8,128)(2,1)S(1)} %get-tuple-element.107), channel_id=1, source_target_pairs={{0,1},{1,0},{2,3},{3,2},{4,5},{5,4},{6,7},{7,6},{8,9},{9,8},{10,11... | collective-permute-start | bytes 294920 | tf_op jit(solution)/shard_map/ppermute | solution.py:433
  64.1 8.5 %collective-permute-start.12 = (bf16[48,1024]{1,0:T(8,128)(2,1)S(1)}, bf16[48,1024]{1,0:T(8,128)(2,1)S(1)}, u32[]{:S(2)}, u32[]{:S(2)}) collective-permute-start(bf16[48,1024]{1,0:T(8,128)(2,1)S(1)} %get-tuple-element.108), channel_id=1, source_target_pairs={{0,2},{1,3},{2,0},{3,1},{4,6},{5,7},{6,4},{7,5},{8,10},{9,11},{10,... | collective-permute-start | bytes 294920 | tf_op jit(solution)/shard_map/ppermute | solution.py:433
  68.7 4.5 %collective-permute-start.13 = (bf16[48,1024]{1,0:T(8,128)(2,1)S(1)}, bf16[48,1024]{1,0:T(8,128)(2,1)S(1)}, u32[]{:S(2)}, u32[]{:S(2)}) collective-permute-start(bf16[48,1024]{1,0:T(8,128)(2,1)S(1)} %get-tuple-element.109), channel_id=1, source_target_pairs={{0,3},{1,2},{2,1},{3,0},{4,7},{5,6},{6,5},{7,4},{8,11},{9,10},{10,... | collective-permute-start | bytes 294920 | tf_op jit(solution)/shard_map/ppermute | solution.py:433
  72.6 11.8 %copy-start.25 = (bf16[48,1024]{1,0:T(8,128)(2,1)}, bf16[48,1024]{1,0:T(8,128)(2,1)S(1)}, u32[]{:S(2)}) copy-start(bf16[48,1024]{1,0:T(8,128)(2,1)S(1)} %collective-permute-done.11.refs_1_) | copy-start | bytes 294916
  72.6 11.8 %copy-start.26 = (bf16[48,1024]{1,0:T(8,128)(2,1)}, bf16[48,1024]{1,0:T(8,128)(2,1)S(1)}, u32[]{:S(2)}) copy-start(bf16[48,1024]{1,0:T(8,128)(2,1)S(1)} %collective-permute-done.12.refs_2_) | copy-start | bytes 294916
  73.2 11.2 %copy-start.27 = (bf16[48,1024]{1,0:T(8,128)(2,1)}, bf16[48,1024]{1,0:T(8,128)(2,1)S(1)}, u32[]{:S(2)}) copy-start(bf16[48,1024]{1,0:T(8,128)(2,1)S(1)} %collective-permute-done.13.refs_3_) | copy-start | bytes 294916
  73.2 11.2 %all-to-all-start = ((bf16[8,16,1024]{2,1,0:T(8,128)(2,1)}), bf16[8,16,1024]{2,1,0:T(8,128)(2,1)S(1)}, u32[]{:S(2)}, u32[]{:S(2)}) async-start(bf16[8,16,1024]{2,1,0:T(8,128)(2,1)} %bitcast.12), calls=%async_computation | async-start | bytes 524288 | tf_op jit(solution)/shard_map/all_to_all | solution.py:438
  84.4 0.7 copy-start.24

commit v5 on v4

--- a/solution.py
+++ b/solution.py
@@ -480,7 +480,7 @@
     soon, where = lax.optimization_barrier((soon, where))
     soon = exchange(soon)
     last = late(where, far, middle2, swapped, capacity)
-    soon, last = lax.optimization_barrier((soon, last))
+    soon[1], soon[2], last = lax.optimization_barrier((soon[1], soon[2], last))
     last = gather(last, 2 * PLANE)
     return back, [*soon, last], done
 

time: 90.9 us -> 90.8 us (level)
    all_to_all x1, waiting for transfers between devices: 5.08 us -> 0.01 us  [gather(): lax.all_to_all(parts, 'adapter', 0, 0, axis_index_groups=groups, tiled=True)]
    ppermute x19, waiting for transfers between devices: 24 us -> 28.5 us  [by_planes(): send = lambda a, pairs: lax.ppermute(a, 'adapter', pairs)]
where the time goes in v5:
time: 90.8 us; the launch traced here: 90.3 us
  waiting for transfers between devices  28.5 us (31%)
  Pallas kernels  26.1 us (29%)
  starting transfers between devices  25.6 us (28%)
  local copies, waits for them, and re-layouts  6.75 us (7%)
  other arithmetic  2.23 us (2%)
  between operations  1.05 us (1%)
    ppermute x19, waiting for transfers between devices, by_planes(): send = lambda a, pairs: lax.ppermute(a, 'adapter', pairs)  28.5 us
    ppermute x19, starting transfers between devices, by_planes(): send = lambda a, pairs: lax.ppermute(a, 'adapter', pairs)  20 us
    unnamed x68, local copies, waits for them, and re-layouts  6.41 us
    pallas_call x1, Pallas kernels, cached_attention(): pl.pallas_call(functools.partial(cached_kernel, 16), in_specs=[VMEM] * 3,...  5.63 us
    all_to_all x1, starting transfers between devices, gather(): lax.all_to_all(parts, 'adapter', 0, 0, axis_index_groups=groups, tiled=True)  5.62 us
    pallas_call x1, Pallas kernels, finish(): pl.pallas_call(functools.partial(finish_kernel, len(pieces)), in_specs=[V...  5.29 us
    pallas_call x1, Pallas kernels, pack(): pl.pallas_call(pack_kernel, in_specs=[VMEM, HBM], out_specs=[HBM] * len(h...  4.57 us
    pallas_call x1, Pallas kernels, early(): pl.pallas_call(functools.partial(early_kernel, capacity), in_specs=[SMEM]...  3.02 us
  transfers between devices with their start and end apart: 20, of which 9 were waited for; matrix products, arithmetic and copies ran while one was open for 3% of the time, Pallas kernels for 20%

profile of v5, /device:TPU:0, one launch (start us, length us, event | category | flops | bytes accessed | tf_op | source)
XLA Modules:
  0.0 90.3 jit_solution(15009475974278542644)
XLA Ops:
  0.7 0.0 copy-start
  0.7 2.4 %join.1.refs_14_ = bf16[64,9216]{1,0:T(8,128)(2,1)} custom-call(bf16[64,8192]{1,0:T(8,128)(2,1)} %bitcast.45, bf16[64,1024]{1,0:T(8,128)(2,1)} %bitcast.46), custom_call_target="tpu_custom_call" | custom-call | flops 1000 | bytes 1000 | tf_op jit(solution)/shard_map/join/pallas_call | solution.py:308
  3.1 0.7 collective-permute-start.6
  3.9 5.8 %collective-permute-start.10 = (bf16[64,9216]{1,0:T(8,128)(2,1)}, bf16[64,9216]{1,0:T(8,128)(2,1)}, u32[]{:S(2)}, u32[]{:S(2)}) collective-permute-start(bf16[64,9216]{1,0:T(8,128)(2,1)} %join.1.refs_14_), channel_id=1, source_target_pairs={{0,4},{1,5},{2,6},{3,7},{4,0},{5,1},{6,2},{7,3},{8,12},{9,13},{10,... | collective-permute-start | bytes 3538952 | tf_op jit(solution)/shard_map/ppermute | solution.py:433
  9.7 0.1 select_reduce_fusion
  9.8 0.2 convert_reduce_fusion
  10.0 0.6 compare_select_fusion.7
  10.5 0.4 first.1
  10.9 0.1 collective-permute-start
  11.0 1.6 %collective-permute-start.1 = (bf16[16,8192]{1,0:T(8,128)(2,1)S(1)}, bf16[16,8192]{1,0:T(8,128)(2,1)S(1)}, u32[]{:S(2)}, u32[]{:S(2)}) collective-permute-start(bf16[16,8192]{1,0:T(8,128)(2,1)S(1)} %get-tuple-element.61), channel_id=1, source_target_pairs={{0,2},{1,3},{2,0},{3,1},{4,6},{5,7},{6,4},{7,5},{8,10},{9,11},{10,... | collective-permute-start | bytes 786440 | tf_op jit(solution)/shard_map/ppermute | solution.py:433
  12.6 0.3 collective-permute-start.2
  12.9 4.6 %pack.1 = (bf16[16,8192]{1,0:T(8,128)(2,1)}, bf16[16,8192]{1,0:T(8,128)(2,1)}, bf16[16,8192]{1,0:T(8,128)(2,1)}, bf16[16,8192]{1,0:T(8,128)(2,1)}, bf16[16,8192]...) custom-call(s32[1,128]{1,0:T(1,128)} %get-tuple-element.117.target_r, ...), custom_call_target="tpu_custom_call" | custom-call | flops 1000 | bytes 20000000000 | tf_op jit(solution)/shard_map/pack/pallas_call | solution.py:238
  17.5 0.0 collective-permute-done.refs_1_
  17.5 2.7 %collective-permute-done.1.refs_2_ = bf16[16,8192]{1,0:T(8,128)(2,1)S(1)} collective-permute-done((bf16[16,8192]{1,0:T(8,128)(2,1)S(1)}, bf16[16,8192]{1,0:T(8,128)(2,1)S(1)}, u32[]{:S(2)}, u32[]{:S(2)}) %collective-permute-start.1) | collective-permute-done | bytes 262176 | tf_op jit(solution)/shard_map/ppermute | solution.py:433
  20.2 4.7 %collective-permute-done.2.refs_3_ = bf16[16,8192]{1,0:T(8,128)(2,1)S(1)} collective-permute-done((bf16[16,8192]{1,0:T(8,128)(2,1)S(1)}, bf16[16,8192]{1,0:T(8,128)(2,1)S(1)}, u32[]{:S(2)}, u32[]{:S(2)}) %collective-permute-start.2) | collective-permute-done | bytes 262176 | tf_op jit(solution)/shard_map/ppermute | solution.py:433
  24.9 0.7 collective-permute-start.3
  25.6 1.5 %collective-permute-start.4 = (bf16[16,8192]{1,0:T(8,128)(2,1)}, bf16[16,8192]{1,0:T(8,128)(2,1)S(1)}, u32[]{:S(2)}, u32[]{:S(2)}) collective-permute-start(bf16[16,8192]{1,0:T(8,128)(2,1)} %get-tuple-element.69), channel_id=1, source_target_pairs={{0,2},{1,3},{2,0},{3,1},{4,6},{5,7},{6,4},{7,5},{8,10},{9,11},{10,... | collective-permute-start | bytes 786440 | tf_op jit(solution)/shard_map/ppermute | solution.py:433
  27.1 0.0 collective-permute-start.5
  27.1 0.7 pad_add_fusion.where_ref
  27.7 0.0 collective-permute-done.6.weights_hbm
  27.8 1.0 %copy-done.2 = bf16[64,9216]{1,0:T(8,128)(2,1)} copy-done((bf16[64,9216]{1,0:T(8,128)(2,1)}, bf16[64,9216]{1,0:T(8,128)(2,1)S(1)}, u32[]{:S(2)}) %copy-start.2) | copy-done | bytes 1179672
  28.8 2.8 %choose.1.refs_13_ = bf16[64,9216]{1,0:T(8,128)(2,1)} custom-call(s32[4]{0:T(128)} %pad_add_fusion.where_ref, bf16[64,9216]{1,0:T(8,128)(2,1)} %copy-done.2, bf16[16,8192]{1,0:T(8,128)(2,1)} %get-tuple-element.75.refs_0_, bf16[16,8192]{1,0:T(8,128)(2,1)} %copy-done.7, bf16[16,8192]{1,0:T(8,128)(2,1)} %copy-done.9, ...), custom_call_target="tpu_custom_call", output_to_operand_aliasing={{}: (1, {})} | custom-call | flops 1000 | bytes 1000 | tf_op jit(solution)/shard_map/choose/pallas_call | solution.py:405
  31.7 0.0 collective-permute-done.3.refs_5_
  31.7 0.7 copy-done.17
  32.4 2.6 %collective-permute-done.4.refs_6_ = bf16[16,8192]{1,0:T(8,128)(2,1)S(1)} collective-permute-done((bf16[16,8192]{1,0:T(8,128)(2,1)}, bf16[16,8192]{1,0:T(8,128)(2,1)S(1)}, u32[]{:S(2)}, u32[]{:S(2)}) %collective-permute-start.4) | collective-permute-done | bytes 262176 | tf_op jit(solution)/shard_map/ppermute | solution.py:433
  35.0 0.7 copy-done.19
  35.7 3.1 %collective-permute-done.5.refs_7_ = bf16[16,8192]{1,0:T(8,128)(2,1)} collective-permute-done((bf16[16,8192]{1,0:T(8,128)(2,1)}, bf16[16,8192]{1,0:T(8,128)(2,1)}, u32[]{:S(2)}, u32[]{:S(2)}) %collective-permute-start.5) | collective-permute-done | bytes 262176 | tf_op jit(solution)/shard_map/ppermute | solution.py:433
  38.8 0.7 collective-permute-start.17
  39.4 0.0 collective-permute-done.10.refs_12_
  39.5 0.7 collective-permute-start.16
  40.2 0.2 collective-permute-start.7
  40.4 1.5 %collective-permute-start.8 = (bf16[16,8192]{1,0:T(8,128)(2,1)}, bf16[16,8192]{1,0:T(8,128)(2,1)}, u32[]{:S(2)}, u32[]{:S(2)}) collective-permute-start(bf16[16,8192]{1,0:T(8,128)(2,1)} %get-tuple-element.81), channel_id=1, source_target_pairs={{0,2},{1,3},{2,0},{3,1},{4,6},{5,7},{6,4},{7,5},{8,10},{9,11},{10,... | collective-permute-start | bytes 786440 | tf_op jit(solution)/shard_map/ppermute | solution.py:433
  41.9 0.3 collective-permute-start.9
  42.1 0.1 copy.27.length_ref
  42.3 0.0 copy-start.4
  42.3 2.2 %copy-done.4 = bf16[128,16,1024]{2,1,0:T(8,128)(2,1)S(1)} copy-done((bf16[128,16,1024]{2,1,0:T(8,128)(2,1)S(1)}, bf16[128,16,1024]{2,1,0:T(8,128)(2,1)}, u32[]{:S(2)}) %copy-start.4) | copy-done | bytes 4194328
  44.5 0.0 copy-start.13
  44.5 0.0 copy-start.15
  44.6 5.6 %cached.1 = (bf16[128,4096]{1,0:T(8,128)(2,1)S(1)}, f32[128,128]{1,0:T(8,128)S(1)}) custom-call(s32[128,1]{1,0:T(8,128)S(1)} %copy.27.length_ref, bf16[128,4096]{1,0:T(8,128)(2,1)S(1)} %copy-done.5, bf16[128,16,1024]{2,1,0:T(8,128)(2,1)S(1)} %copy-done.4), custom_call_target="tpu_custom_call" | custom-call | flops 1000 | bytes 20000000000 | tf_op jit(solution)/shard_map/cached/pallas_call | solution.py:107
  50.2 1.0 %copy-done.6 = bf16[128,4096]{1,0:T(8,128)(2,1)} copy-done((bf16[128,4096]{1,0:T(8,128)(2,1)}, bf16[128,4096]{1,0:T(8,128)(2,1)S(1)}, u32[]{:S(2)}) %copy-start.6) | copy-done | bytes 1048600
  51.2 0.0 collective-permute-done.7.refs_9_
  51.2 0.0 collective-permute-done.8.refs_10_
  51.2 3.3 %collective-permute-done.9.refs_11_ = bf16[16,8192]{1,0:T(8,128)(2,1)} collective-permute-done((bf16[16,8192]{1,0:T(8,128)(2,1)}, bf16[16,8192]{1,0:T(8,128)(2,1)}, u32[]{:S(2)}, u32[]{:S(2)}) %collective-permute-start.9) | collective-permute-done | bytes 262176 | tf_op jit(solution)/shard_map/ppermute | solution.py:433
  54.5 0.5 collective-permute-start.13
  55.0 1.5 %collective-permute-start.14 = (bf16[16,8192]{1,0:T(8,128)(2,1)S(1)}, bf16[16,8192]{1,0:T(8,128)(2,1)S(1)}, u32[]{:S(2)}, u32[]{:S(2)}) collective-permute-start(bf16[16,8192]{1,0:T(8,128)(2,1)S(1)} %copy-done.30), channel_id=1, source_target_pairs={{0,2},{1,3},{2,0},{3,1},{4,6},{5,7},{6,4},{7,5},{8,10},{9,11},{10,... | collective-permute-start | bytes 786440 | tf_op jit(solution)/shard_map/ppermute | solution.py:433
  56.5 0.0 collective-permute-start.15
  56.6 3.0 %early.1 = (bf16[48,1024]{1,0:T(8,128)(2,1)S(1)}, bf16[48,1024]{1,0:T(8,128)(2,1)S(1)}, bf16[48,1024]{1,0:T(8,128)(2,1)S(1)}, bf16[48,1024]{1,0:T(8,128)(2,1)S(1)}) custom-call(s32[4]{0:T(128)S(1)} %copy-done.23, bf16[16,8192]{1,0:T(8,128)(2,1)S(1)} %copy-done.13, bf16[16,8192]{1,0:T(8,128)(2,1)S(1)} %copy-done.8, bf16[16,8192]{1,0:T(8,128)(2,1)S(1)} %copy-done.10, ...), custom_call_target="tpu_custom_call" | custom-call | flops 1000 | bytes 1000 | tf_op jit(solution)/shard_map/early/pallas_call | solution.py:339
  59.6 0.0 collective-permute-done.13.refs_1_
  59.6 0.7 collective-permute-start.11
  60.3 3.8 %collective-permute-done.14.refs_2_ = bf16[16,8192]{1,0:T(8,128)(2,1)S(1)} collective-permute-done((bf16[16,8192]{1,0:T(8,128)(2,1)S(1)}, bf16[16,8192]{1,0:T(8,128)(2,1)S(1)}, u32[]{:S(2)}, u32[]{:S(2)}) %collective-permute-start.14) | collective-permute-done | bytes 262176 | tf_op jit(solution)/shard_map/ppermute | solution.py:433
  64.1 1.5 %collective-permute-start.12 = (bf16[48,1024]{1,0:T(8,128)(2,1)S(1)}, bf16[48,1024]{1,0:T(8,128)(2,1)S(1)}, u32[]{:S(2)}, u32[]{:S(2)}) collective-permute-start(bf16[48,1024]{1,0:T(8,128)(2,1)S(1)} %get-tuple-element.106), channel_id=1, source_target_pairs={{0,2},{1,3},{2,0},{3,1},{4,6},{5,7},{6,4},{7,5},{8,10},{9,11},{10,... | collective-permute-start | bytes 294920 | tf_op jit(solution)/shard_map/ppermute | solution.py:433
  65.6 3.1 %collective-permute-done.15.refs_3_ = bf16[16,8192]{1,0:T(8,128)(2,1)S(1)} collective-permute-done((bf16[16,8192]{1,0:T(8,128)(2,1)S(1)}, bf16[16,8192]{1,0:T(8,128)(2,1)S(1)}, u32[]{:S(2)}, u32[]{:S(2)}) %collective-permute-start.15) | collective-permute-done | bytes 262176 | tf_op jit(solution)/shard_map/ppermute | solution.py:433
  68.8 1.9 %late.1 = bf16[128,1024]{1,0:T(8,128)(2,1)} custom-call(s32[4]{0:T(128)S(1)} %copy-done.23, bf16[16,8192]{1,0:T(8,128)(2,1)S(1)} %copy-done.14, bf16[16,8192]{1,0:T(8,128)(2,1)S(1)} %collective-permute-done.13.refs_1_, bf16[16,8192]{1,0:T(8,128)(2,1)S(1)} %collective-permute-done.14.refs_2_, bf16[16,8192]{1,0:T(8,128)(2,1)S(1)} %collective-permute-done.15.refs_3_, ...), custom_call_target="tpu_custom_call" | custom-call | tf_op jit(solution)/shard_map/late/pallas_call | solution.py:373
  70.6 0.0 collective-permute-done.11.refs_1_
  70.7 0.3 collective-permute-done.12.refs_2_
  71.0 5.6 %all-to-all-start = ((bf16[8,16,1024]{2,1,0:T(8,128)(2,1)}), bf16[8,16,1024]{2,1,0:T(8,128)(2,1)S(1)}, u32[]{:S(2)}, u32[]{:S(2)}) async-start(bf16[8,16,1024]{2,1,0:T(8,128)(2,1)} %bitcast.12), calls=%async_computation | async-start | bytes 524288 | tf_op jit(solution)/shard_map/all_to_all | solution.py:438
  76.6 0.1 copy.24
  76.7 0.1 copy.20
  76.8 1.8 %collective-permute-start.18 = (bf16[48,1024]{1,0:T(8,128)(2,1)S(1)}, bf16[48,1024]{1,0:T(8,128)(2,1)S(1)}, u32[]{:S(2)}, u32[]{:S(2)}) collective-permute-start(bf16[48,1024]{1,0:T(8,128)(2,1)S(1)} %get-tuple-element.114), channel_id=1, source_target_pairs={{0,3},{1,2},{2,1},{3,0},{4,7},{5,6},{6,5},{7,4},{8,11},{9,10},{10,... | collective-permute-start | bytes 294920 | tf_op jit(solution)/shard_map/ppermute | solution.py:433
  78.6 0.7 select_select_fusion.target_ref
  79.4 4.9 %collective-permute-done.18.refs_3_ = bf16[48,1024]{1,0:T(8,128)(2,1)S(1)} collective-permute-done((bf16[48,1024]{1,0:T(8,128)(2,1)S(1)}, bf16[48,1024]{1,0:T(8,128)(2,1)S(1)}, u32[]{:S(2)}, u32[]{:S(2)}) %collective-permute-start.18) | collective-permute-done | bytes 98336 | tf_op jit(solution)/shard_map/ppermute | solution.py:433
  84.3 0.6 copy-done.27
  84.9 0.1 copy-done.24
  85.0 5.3 %finish.1 = (bf16[128,4096]{1,0:T(8,128)(2,1)}, bf16[128,1024]{1,0:T(8,128)(2,1)}) custom-call(s32[128,1]{1,0:T(8,128)} %select_select_fusion.target_ref, f32[128,128]{1,0:T(8,128)} %copy-done.22, bf16[128,1024]{1,0:T(8,128)(2,1)} %base_hbm.1, bf16[128,4096]{1,0:T(8,128)(2,1)} %q_hbm.1, bf16[128,4096]{1,0:T(8,128)(2,1)} %copy-done.6, ...), custom_call_target="tpu_custom_call" | custom-call | flops 1000 | bytes 1000 | tf_op jit(solution)/shard_map/finish/pallas_call | solution.py:184
  (60 shorter events, 0.1 us)
Async XLA Ops:
  0.6 9.1 %copy-start.32 = (s32[16]{0:T(128)S(1)}, s32[16]{0:T(128)}, u32[]{:S(2)}) copy-start(s32[16]{0:T(128)} %param.15) | copy-start | bytes 196
  0.6 9.1 %copy-start.33 = (s32[128,1]{0,1:T(1,128)S(1)}, s32[128,1]{0,1:T(1,128)}, u32[]{:S(2)}) copy-start(s32[128,1]{0,1:T(1,128)} %param.14) | copy-start | bytes 1540
  0.7 9.9 %copy-start = (bf16[128,8192]{1,0:T(8,128)(2,1)S(1)}, bf16[128,8192]{1,0:T(8,128)(2,1)}, u32[]{:S(2)}) copy-start(bf16[128,8192]{1,0:T(8,128)(2,1)} %hidden_ref.1) | copy-start | bytes 6291460
  3.1 24.6 %collective-permute-start.6 = (bf16[64,9216]{1,0:T(8,128)(2,1)}, bf16[64,9216]{1,0:T(8,128)(2,1)S(1)}, u32[]{:S(2)}, u32[]{:S(2)}) collective-permute-start(bf16[64,9216]{1,0:T(8,128)(2,1)} %join.1.refs_14_), channel_id=1, source_target_pairs={{4,8},{5,9},{6,10},{7,11},{8,4},{9,5},{10,6},{11,7},{20,24},{21,25... | collective-permute-start | bytes 3538952 | tf_op jit(solution)/shard_map/ppermute | solution.py:433
  3.9 35.6 %collective-permute-start.10 = (bf16[64,9216]{1,0:T(8,128)(2,1)}, bf16[64,9216]{1,0:T(8,128)(2,1)}, u32[]{:S(2)}, u32[]{:S(2)}) collective-permute-start(bf16[64,9216]{1,0:T(8,128)(2,1)} %join.1.refs_14_), channel_id=1, source_target_pairs={{0,4},{1,5},{2,6},{3,7},{4,0},{5,1},{6,2},{7,3},{8,12},{9,13},{10,... | collective-permute-start | bytes 3538952 | tf_op jit(solution)/shard_map/ppermute | solution.py:433
  10.9 6.5 %collective-permute-start = (bf16[16,8192]{1,0:T(8,128)(2,1)S(1)}, bf16[16,8192]{1,0:T(8,128)(2,1)S(1)}, u32[]{:S(2)}, u32[]{:S(2)}) collective-permute-start(bf16[16,8192]{1,0:T(8,128)(2,1)S(1)} %get-tuple-element.60), channel_id=1, source_target_pairs={{0,1},{1,0},{2,3},{3,2},{4,5},{5,4},{6,7},{7,6},{8,9},{9,8},{10,11... | collective-permute-start | bytes 786440 | tf_op jit(solution)/shard_map/ppermute | solution.py:433
  11.0 9.2 %collective-permute-start.1 = (bf16[16,8192]{1,0:T(8,128)(2,1)S(1)}, bf16[16,8192]{1,0:T(8,128)(2,1)S(1)}, u32[]{:S(2)}, u32[]{:S(2)}) collective-permute-start(bf16[16,8192]{1,0:T(8,128)(2,1)S(1)} %get-tuple-element.61), channel_id=1, source_target_pairs={{0,2},{1,3},{2,0},{3,1},{4,6},{5,7},{6,4},{7,5},{8,10},{9,11},{10,... | collective-permute-start | bytes 786440 | tf_op jit(solution)/shard_map/ppermute | solution.py:433
  12.6 12.3 %collective-permute-start.2 = (bf16[16,8192]{1,0:T(8,128)(2,1)S(1)}, bf16[16,8192]{1,0:T(8,128)(2,1)S(1)}, u32[]{:S(2)}, u32[]{:S(2)}) collective-permute-start(bf16[16,8192]{1,0:T(8,128)(2,1)S(1)} %get-tuple-element.62), channel_id=1, source_target_pairs={{0,3},{1,2},{2,1},{3,0},{4,7},{5,6},{6,5},{7,4},{8,11},{9,10},{10,... | collective-permute-start | bytes 786440 | tf_op jit(solution)/shard_map/ppermute | solution.py:433
  17.5 10.3 %copy-start.7 = (bf16[16,8192]{1,0:T(8,128)(2,1)}, bf16[16,8192]{1,0:T(8,128)(2,1)S(1)}, u32[]{:S(2)}) copy-start(bf16[16,8192]{1,0:T(8,128)(2,1)S(1)} %collective-permute-done.refs_1_) | copy-start | bytes 786436
  20.2 7.6 %copy-start.9 = (bf16[16,8192]{1,0:T(8,128)(2,1)}, bf16[16,8192]{1,0:T(8,128)(2,1)S(1)}, u32[]{:S(2)}) copy-start(bf16[16,8192]{1,0:T(8,128)(2,1)S(1)} %collective-permute-done.1.refs_2_) | copy-start | bytes 786436
  24.9 2.9 %copy-start.11 = (bf16[16,8192]{1,0:T(8,128)(2,1)}, bf16[16,8192]{1,0:T(8,128)(2,1)S(1)}, u32[]{:S(2)}) copy-start(bf16[16,8192]{1,0:T(8,128)(2,1)S(1)} %collective-permute-done.2.refs_3_) | copy-start | bytes 786436
  24.9 6.7 %collective-permute-start.3 = (bf16[16,8192]{1,0:T(8,128)(2,1)}, bf16[16,8192]{1,0:T(8,128)(2,1)S(1)}, u32[]{:S(2)}, u32[]{:S(2)}) collective-permute-start(bf16[16,8192]{1,0:T(8,128)(2,1)} %get-tuple-element.68), channel_id=1, source_target_pairs={{0,1},{1,0},{2,3},{3,2},{4,5},{5,4},{6,7},{7,6},{8,9},{9,8},{10,11... | collective-permute-start | bytes 786440 | tf_op jit(solution)/shard_map/ppermute | solution.py:433
  25.6 9.4 %collective-permute-start.4 = (bf16[16,8192]{1,0:T(8,128)(2,1)}, bf16[16,8192]{1,0:T(8,128)(2,1)S(1)}, u32[]{:S(2)}, u32[]{:S(2)}) collective-permute-start(bf16[16,8192]{1,0:T(8,128)(2,1)} %get-tuple-element.69), channel_id=1, source_target_pairs={{0,2},{1,3},{2,0},{3,1},{4,6},{5,7},{6,4},{7,5},{8,10},{9,11},{10,... | collective-permute-start | bytes 786440 | tf_op jit(solution)/shard_map/ppermute | solution.py:433
  27.1 11.7 %collective-permute-start.5 = (bf16[16,8192]{1,0:T(8,128)(2,1)}, bf16[16,8192]{1,0:T(8,128)(2,1)}, u32[]{:S(2)}, u32[]{:S(2)}) collective-permute-start(bf16[16,8192]{1,0:T(8,128)(2,1)} %get-tuple-element.70), channel_id=1, source_target_pairs={{0,3},{1,2},{2,1},{3,0},{4,7},{5,6},{6,5},{7,4},{8,11},{9,10},{10,... | collective-permute-start | bytes 786440 | tf_op jit(solution)/shard_map/ppermute | solution.py:433
  27.7 14.4 %copy-start.28 = (s32[128]{0:T(128)S(1)}, s32[128]{0:T(128)}, u32[]{:S(2)}) copy-start(s32[128]{0:T(128)} %param.13) | copy-start | bytes 1540
  27.7 14.5 %copy-start.5 = (bf16[128,4096]{1,0:T(8,128)(2,1)S(1)}, bf16[128,4096]{1,0:T(8,128)(2,1)}, u32[]{:S(2)}) copy-start(bf16[128,4096]{1,0:T(8,128)(2,1)} %q_hbm.1) | copy-start | bytes 3145732
  27.8 1.0 %copy-start.2 = (bf16[64,9216]{1,0:T(8,128)(2,1)}, bf16[64,9216]{1,0:T(8,128)(2,1)S(1)}, u32[]{:S(2)}) copy-start(bf16[64,9216]{1,0:T(8,128)(2,1)S(1)} %collective-permute-done.6.weights_hbm) | copy-start | bytes 3538948
  31.7 0.7 copy-start.17
  35.0 0.7 copy-start.19
  38.8 30.0 %collective-permute-start.17 = (bf16[64,9216]{1,0:T(8,128)(2,1)}, bf16[64,9216]{1,0:T(8,128)(2,1)S(1)}, u32[]{:S(2)}, u32[]{:S(2)}) collective-permute-start(bf16[64,9216]{1,0:T(8,128)(2,1)} %choose.1.refs_13_), channel_id=1, source_target_pairs={{0,4},{1,5},{2,6},{3,7},{4,0},{5,1},{6,2},{7,3},{8,12},{9,13},{10,... | collective-permute-start | bytes 3538952 | tf_op jit(solution)/shard_map/ppermute | solution.py:433
  39.5 29.3 %collective-permute-start.16 = (bf16[64,9216]{1,0:T(8,128)(2,1)}, bf16[64,9216]{1,0:T(8,128)(2,1)S(1)}, u32[]{:S(2)}, u32[]{:S(2)}) collective-permute-start(bf16[64,9216]{1,0:T(8,128)(2,1)} %collective-permute-done.10.refs_12_), channel_id=1, source_target_pairs={{4,8},{5,9},{6,10},{7,11},{8,4},{9,5},{10,6},{11,7},{20,24},{21,25... | collective-permute-start | bytes 3538952 | tf_op jit(solution)/shard_map/ppermute | solution.py:433
  40.2 11.0 %collective-permute-start.7 = (bf16[16,8192]{1,0:T(8,128)(2,1)}, bf16[16,8192]{1,0:T(8,128)(2,1)}, u32[]{:S(2)}, u32[]{:S(2)}) collective-permute-start(bf16[16,8192]{1,0:T(8,128)(2,1)} %get-tuple-element.80), channel_id=1, source_target_pairs={{0,1},{1,0},{2,3},{3,2},{4,5},{5,4},{6,7},{7,6},{8,9},{9,8},{10,11... | collective-permute-start | bytes 786440 | tf_op jit(solution)/shard_map/ppermute | solution.py:433
  40.4 10.8 %collective-permute-start.8 = (bf16[16,8192]{1,0:T(8,128)(2,1)}, bf16[16,8192]{1,0:T(8,128)(2,1)}, u32[]{:S(2)}, u32[]{:S(2)}) collective-permute-start(bf16[16,8192]{1,0:T(8,128)(2,1)} %get-tuple-element.81), channel_id=1, source_target_pairs={{0,2},{1,3},{2,0},{3,1},{4,6},{5,7},{6,4},{7,5},{8,10},{9,11},{10,... | collective-permute-start | bytes 786440 | tf_op jit(solution)/shard_map/ppermute | solution.py:433
  41.9 12.6 %collective-permute-start.9 = (bf16[16,8192]{1,0:T(8,128)(2,1)}, bf16[16,8192]{1,0:T(8,128)(2,1)}, u32[]{:S(2)}, u32[]{:S(2)}) collective-permute-start(bf16[16,8192]{1,0:T(8,128)(2,1)} %get-tuple-element.82), channel_id=1, source_target_pairs={{0,3},{1,2},{2,1},{3,0},{4,7},{5,6},{6,5},{7,4},{8,11},{9,10},{10,... | collective-permute-start | bytes 786440 | tf_op jit(solution)/shard_map/ppermute | solution.py:433
  42.3 2.2 %copy-start.4 = (bf16[128,16,1024]{2,1,0:T(8,128)(2,1)S(1)}, bf16[128,16,1024]{2,1,0:T(8,128)(2,1)}, u32[]{:S(2)}) copy-start(bf16[128,16,1024]{2,1,0:T(8,128)(2,1)} %cache_ref.1) | copy-start | bytes 12582916
  44.5 10.0 %copy-start.31 = (bf16[16,8192]{1,0:T(8,128)(2,1)S(1)}, bf16[16,8192]{1,0:T(8,128)(2,1)}, u32[]{:S(2)}) copy-start(bf16[16,8192]{1,0:T(8,128)(2,1)} %get-tuple-element.109) | copy-start | bytes 786436
  44.5 10.5 %copy-start.30 = (bf16[16,8192]{1,0:T(8,128)(2,1)S(1)}, bf16[16,8192]{1,0:T(8,128)(2,1)}, u32[]{:S(2)}) copy-start(bf16[16,8192]{1,0:T(8,128)(2,1)} %get-tuple-element.110) | copy-start | bytes 786436
  44.5 12.0 %copy-start.29 = (bf16[16,8192]{1,0:T(8,128)(2,1)S(1)}, bf16[16,8192]{1,0:T(8,128)(2,1)}, u32[]{:S(2)}) copy-start(bf16[16,8192]{1,0:T(8,128)(2,1)} %get-tuple-element.111) | copy-start | bytes 786436
  44.5 12.0 %copy-start.1 = (bf16[64,9216]{1,0:T(8,128)(2,1)S(1)}, bf16[64,9216]{1,0:T(8,128)(2,1)}, u32[]{:S(2)}) copy-start(bf16[64,9216]{1,0:T(8,128)(2,1)} %join.1.refs_14_) | copy-start | bytes 3538948
  44.5 12.0 %copy-start.3 = (bf16[64,9216]{1,0:T(8,128)(2,1)S(1)}, bf16[64,9216]{1,0:T(8,128)(2,1)}, u32[]{:S(2)}) copy-start(bf16[64,9216]{1,0:T(8,128)(2,1)} %choose.1.refs_13_) | copy-start | bytes 3538948
  44.5 12.0 %copy-start.8 = (bf16[16,8192]{1,0:T(8,128)(2,1)S(1)}, bf16[16,8192]{1,0:T(8,128)(2,1)}, u32[]{:S(2)}) copy-start(bf16[16,8192]{1,0:T(8,128)(2,1)} %copy-done.7) | copy-start | bytes 786436
  44.5 12.0 %copy-start.10 = (bf16[16,8192]{1,0:T(8,128)(2,1)S(1)}, bf16[16,8192]{1,0:T(8,128)(2,1)}, u32[]{:S(2)}) copy-start(bf16[16,8192]{1,0:T(8,128)(2,1)} %copy-done.9) | copy-start | bytes 786436
  44.5 12.0 %copy-start.12 = (bf16[16,8192]{1,0:T(8,128)(2,1)S(1)}, bf16[16,8192]{1,0:T(8,128)(2,1)}, u32[]{:S(2)}) copy-start(bf16[16,8192]{1,0:T(8,128)(2,1)} %copy-done.11) | copy-start | bytes 786436
  44.5 12.0 %copy-start.13 = (bf16[16,8192]{1,0:T(8,128)(2,1)S(1)}, bf16[16,8192]{1,0:T(8,128)(2,1)}, u32[]{:S(2)}) copy-start(bf16[16,8192]{1,0:T(8,128)(2,1)} %get-tuple-element.75.refs_0_) | copy-start | bytes 786436
  44.5 12.0 %copy-start.15 = (bf16[16,8192]{1,0:T(8,128)(2,1)S(1)}, bf16[16,8192]{1,0:T(8,128)(2,1)}, u32[]{:S(2)}) copy-start(bf16[16,8192]{1,0:T(8,128)(2,1)} %get-tuple-element.91.refs_4_) | copy-start | bytes 786436
  44.5 12.0 %copy-start.16 = (bf16[16,8192]{1,0:T(8,128)(2,1)S(1)}, bf16[16,8192]{1,0:T(8,128)(2,1)}, u32[]{:S(2)}) copy-start(bf16[16,8192]{1,0:T(8,128)(2,1)} %get-tuple-element.95.refs_8_) | copy-start | bytes 786436
  44.5 12.0 %copy-start.18 = (bf16[16,8192]{1,0:T(8,128)(2,1)S(1)}, bf16[16,8192]{1,0:T(8,128)(2,1)}, u32[]{:S(2)}) copy-start(bf16[16,8192]{1,0:T(8,128)(2,1)} %copy-done.17) | copy-start | bytes 786436
  44.5 12.0 %copy-start.20 = (bf16[16,8192]{1,0:T(8,128)(2,1)S(1)}, bf16[16,8192]{1,0:T(8,128)(2,1)}, u32[]{:S(2)}) copy-start(bf16[16,8192]{1,0:T(8,128)(2,1)} %copy-done.19) | copy-start | bytes 786436
  44.6 12.0 %copy-start.23 = (s32[4]{0:T(128)S(1)}, s32[4]{0:T(128)}, u32[]{:S(2)}) copy-start(s32[4]{0:T(128)} %pad_add_fusion.where_ref) | copy-start | bytes 52
  50.2 1.0 %copy-start.6 = (bf16[128,4096]{1,0:T(8,128)(2,1)}, bf16[128,4096]{1,0:T(8,128)(2,1)S(1)}, u32[]{:S(2)}) copy-start(bf16[128,4096]{1,0:T(8,128)(2,1)S(1)} %get-tuple-element.90.mixed_hbm) | copy-start | bytes 3145732
  51.2 8.4 %copy-start.22 = (f32[128,128]{1,0:T(8,128)}, f32[128,128]{1,0:T(8,128)S(1)}, u32[]{:S(2)}) copy-start(f32[128,128]{1,0:T(8,128)S(1)} %get-tuple-element.89.log_ref) | copy-start | bytes 196612
  54.5 14.3 %copy-start.14 = (bf16[16,8192]{1,0:T(8,128)(2,1)S(1)}, bf16[16,8192]{1,0:T(8,128)(2,1)}, u32[]{:S(2)}) copy-start(bf16[16,8192]{1,0:T(8,128)(2,1)} %get-tuple-element.108.refs_0_) | copy-start | bytes 786436
  54.5 5.1 %collective-permute-start.13 = (bf16[16,8192]{1,0:T(8,128)(2,1)S(1)}, bf16[16,8192]{1,0:T(8,128)(2,1)S(1)}, u32[]{:S(2)}, u32[]{:S(2)}) collective-permute-start(bf16[16,8192]{1,0:T(8,128)(2,1)S(1)} %copy-done.31), channel_id=1, source_target_pairs={{0,1},{1,0},{2,3},{3,2},{4,5},{5,4},{6,7},{7,6},{8,9},{9,8},{10,11... | collective-permute-start | bytes 786440 | tf_op jit(solution)/shard_map/ppermute | solution.py:433
  55.0 9.2 %collective-permute-start.14 = (bf16[16,8192]{1,0:T(8,128)(2,1)S(1)}, bf16[16,8192]{1,0:T(8,128)(2,1)S(1)}, u32[]{:S(2)}, u32[]{:S(2)}) collective-permute-start(bf16[16,8192]{1,0:T(8,128)(2,1)S(1)} %copy-done.30), channel_id=1, source_target_pairs={{0,2},{1,3},{2,0},{3,1},{4,6},{5,7},{6,4},{7,5},{8,10},{9,11},{10,... | collective-permute-start | bytes 786440 | tf_op jit(solution)/shard_map/ppermute | solution.py:433
  56.5 12.3 %collective-permute-start.15 = (bf16[16,8192]{1,0:T(8,128)(2,1)S(1)}, bf16[16,8192]{1,0:T(8,128)(2,1)S(1)}, u32[]{:S(2)}, u32[]{:S(2)}) collective-permute-start(bf16[16,8192]{1,0:T(8,128)(2,1)S(1)} %copy-done.29), channel_id=1, source_target_pairs={{0,3},{1,2},{2,1},{3,0},{4,7},{5,6},{6,5},{7,4},{8,11},{9,10},{10,... | collective-permute-start | bytes 786440 | tf_op jit(solution)/shard_map/ppermute | solution.py:433
  59.6 11.1 %copy-start.21 = (bf16[48,1024]{1,0:T(8,128)(2,1)}, bf16[48,1024]{1,0:T(8,128)(2,1)S(1)}, u32[]{:S(2)}) copy-start(bf16[48,1024]{1,0:T(8,128)(2,1)S(1)} %get-tuple-element.104.refs_0_) | copy-start | bytes 294916
  59.6 11.0 %collective-permute-start.11 = (bf16[48,1024]{1,0:T(8,128)(2,1)S(1)}, bf16[48,1024]{1,0:T(8,128)(2,1)S(1)}, u32[]{:S(2)}, u32[]{:S(2)}) collective-permute-start(bf16[48,1024]{1,0:T(8,128)(2,1)S(1)} %get-tuple-element.105), channel_id=1, source_target_pairs={{0,1},{1,0},{2,3},{3,2},{4,5},{5,4},{6,7},{7,6},{8,9},{9,8},{10,11... | collective-permute-start | bytes 294920 | tf_op jit(solution)/shard_map/ppermute | solution.py:433
  64.1 6.9 %collective-permute-start.12 = (bf16[48,1024]{1,0:T(8,128)(2,1)S(1)}, bf16[48,1024]{1,0:T(8,128)(2,1)S(1)}, u32[]{:S(2)}, u32[]{:S(2)}) collective-permute-start(bf16[48,1024]{1,0:T(8,128)(2,1)S(1)} %get-tuple-element.106), channel_id=1, source_target_pairs={{0,2},{1,3},{2,0},{3,1},{4,6},{5,7},{6,4},{7,5},{8,10},{9,11},{10,... | collective-permute-start | bytes 294920 | tf_op jit(solution)/shard_map/ppermute | solution.py:433
  70.7 13.6 %copy-start.25 = (bf16[48,1024]{1,0:T(8,128)(2,1)}, bf16[48,1024]{1,0:T(8,128)(2,1)S(1)}, u32[]{:S(2)}) copy-start(bf16[48,1024]{1,0:T(8,128)(2,1)S(1)} %collective-permute-done.11.refs_1_) | copy-start | bytes 294916
  71.0 13.3 %copy-start.26 = (bf16[48,1024]{1,0:T(8,128)(2,1)}, bf16[48,1024]{1,0:T(8,128)(2,1)S(1)}, u32[]{:S(2)}) copy-start(bf16[48,1024]{1,0:T(8,128)(2,1)S(1)} %collective-permute-done.12.refs_2_) | copy-start | bytes 294916
  71.0 13.3 %all-to-all-start = ((bf16[8,16,1024]{2,1,0:T(8,128)(2,1)}), bf16[8,16,1024]{2,1,0:T(8,128)(2,1)S(1)}, u32[]{:S(2)}, u32[]{:S(2)}) async-start(bf16[8,16,1024]{2,1,0:T(8,128)(2,1)} %bitcast.12), calls=%async_computation | async-start | bytes 524288 | tf_op jit(solution)/shard_map/all_to_all | solution.py:438
  76.8 7.4 %collective-permute-start.18 = (bf16[48,1024]{1,0:T(8,128)(2,1)S(1)}, bf16[48,1024]{1,0:T(8,128)(2,1)S(1)}, u32[]{:S(2)}, u32[]{:S(2)}) collective-permute-start(bf16[48,1024]{1,0:T(8,128)(2,1)S(1)} %get-tuple-element.114), channel_id=1, source_target_pairs={{0,3},{1,2},{2,1},{3,0},{4,7},{5,6},{6,5},{7,4},{8,11},{9,10},{10,... | collective-permute-start | bytes 294920 | tf_op jit(solution)/shard_map/ppermute | solution.py:433
  84.3 0.6 copy-start.27
  84.3 0.7 copy-start.24
